TPU v7x, 128 devices: a whole 4x4x4 slice. The times are simulated.
128 devices in a mesh: row: 16 (over x, z_hi, core), col: 8 (over y, z_lo).
Axes of the slice: x: 4, y: 4, z: 4 (z_hi: 2, z_lo: 2; z = z_hi * 2 + z_lo), core: 2. Of those that a mesh axis runs over, the one named last changes fastest.
Arguments:
- loads: float32 [3, 24576], P(None, 'row'), may hold values from -6 to 6
- nd_source: int32 [24576], P('row'), may hold values from 0 to 24575, as said below
- panel: bfloat16 [24576, 512], P('row', 'col'), as said below
- trailing: bfloat16 [24576, 24576], P('row', 'col'), may hold values from -6 to 6
- pattern: int32 [192, 192], P('row', 'col'), may hold values from 0 to 1
- owner: int32 [16], replicated, may hold values from 0 to 15, each once
Outputs:
- loads_out: float32 [3, 24576], P(None, 'row')
- trailing_out: bfloat16 [24576, 24576], P('row', 'col')
Inputs may be any that keep to these rules, and one draw needn't show every extreme that they name: `nd_source`: a permutation; the rows t * 1536 to (t + 1) * 1536 - 1 take, from each block s of 1536 columns, exactly the columns s * 1536 + t * 96 to s * 1536 + (t + 1) * 96 - 1. `panel`: the 512 x 512 block at rows owner[0] * 1536 has a positive definite symmetric part. `owner`: a permutation of the row indices.
All inputs are finite; a program needn't handle non-finite values.
Results may differ from a plain program's by a relative error of at most 0.005.
Values may be sent and summed in bfloat16 or wider, within the bound.
No kernel may reach another device: no remote copies, remote signals or barrier semaphores. Data moves between devices by JAX's collectives and lax.ppermute only.
A program may use at most 128 MiB of HBM per device.

v0:
```python
import jax
import jax.numpy as jnp
from jax import lax
from jax.sharding import PartitionSpec as P


def broadcast(array, axis, root):
    mine = lax.axis_index(axis) == root
    return lax.psum(jnp.where(mine, array, jnp.zeros_like(array)), axis)


def per_device(loads, nd_source, panel, trailing, pattern, owner):
    row_dev = panel.shape[0]
    row_count = lax.axis_size("row")
    col_count = lax.axis_size("col")
    pivot_size = panel.shape[1] * col_count
    share_size = row_dev // row_count
    row_place = lax.axis_index("row")
    col_place = lax.axis_index("col")
    arrived = lax.all_to_all(loads, "row", split_axis=1, concat_axis=1, tiled=True)
    source_slot = nd_source // row_dev * share_size + (nd_source % row_dev - row_place * share_size)
    regrouped = jnp.take(arrived, source_slot, axis=1)
    panel_rows = lax.all_gather(panel, "col", axis=1, tiled=True)
    owner_row = owner[0]
    pivot_block, pivot_loads = (
        broadcast(
            panel_rows[:pivot_size].astype(jnp.float32).astype(jnp.bfloat16), "row", owner_row
        ).astype(jnp.float32),
        broadcast(regrouped[:, :pivot_size].astype(jnp.bfloat16), "row", owner_row).astype(
            jnp.float32
        ),
    )
    symmetric = 0.5 * (pivot_block + pivot_block.T)
    lower_factor = jnp.linalg.cholesky(symmetric)
    inverse = lax.linalg.triangular_solve(
        lower_factor, jnp.eye(pivot_size, dtype=jnp.float32), left_side=True, lower=True
    )
    inverse_half = inverse.astype(jnp.bfloat16)
    factor_rows = jnp.dot(panel_rows, inverse_half.T, preferred_element_type=jnp.float32).astype(
        jnp.bfloat16
    )
    pivot_solve = jnp.dot(inverse, pivot_loads.T, precision=lax.Precision.HIGHEST)
    update = jnp.dot(
        factor_rows.astype(jnp.float32), pivot_solve, precision=lax.Precision.HIGHEST
    ).T
    pivot_start = owner_row * row_dev
    positions = row_place * row_dev + jnp.arange(row_dev, dtype=jnp.int32)
    in_pivot = (positions >= pivot_start) & (positions < pivot_start + pivot_size)
    pivot_offset = jnp.clip(positions - pivot_start, 0, pivot_size - 1)
    loads_out = jnp.where(
        in_pivot[None, :], jnp.take(pivot_solve.T, pivot_offset, axis=1), regrouped - update
    )
    slice_width = panel.shape[1]
    column_part = lax.dynamic_slice_in_dim(factor_rows, col_place * slice_width, slice_width, 1)
    gathered = lax.all_gather(column_part, "row", axis=0, tiled=True)
    factor_cols = lax.all_to_all(gathered, "col", split_axis=0, concat_axis=1, tiled=True)
    block_rows = pattern.shape[0]
    block_cols = pattern.shape[1]
    block_size = trailing.shape[0] // block_rows
    col_dev = trailing.shape[1]
    product = jnp.einsum("ik,jk->ij", factor_rows, factor_cols, preferred_element_type=jnp.float32)
    masked = (
        product.reshape(block_rows, block_size, block_cols, block_size)
        * pattern.astype(jnp.float32)[:, None, :, None]
    ).reshape(row_dev, col_dev)
    trailing_out = (trailing.astype(jnp.float32) - masked).astype(jnp.bfloat16)
    return (loads_out, trailing_out)


def solution(mesh):
    return jax.shard_map(
        per_device,
        mesh=mesh,
        in_specs=(P(None, "row"), P("row"), P("row", "col"), P("row", "col"), P("row", "col"), P()),
        out_specs=(P(None, "row"), P("row", "col")),
        check_vma=False,
    )
```

profile of v0, /device:TPU:16, one launch (start us, length us, event | category | flops | bytes accessed | tf_op | source)
XLA Modules:
  0.0 527.6 jit_solution(13422207087617151163)
XLA Ops:
  8.6 45.7 %all-gather.3.cloned.1.call-done = bf16[1536,512]{0,1:T(8,128)(2,1)} async-done(((bf16[1536,64]{0,1:T(8,128)(2,1)}), bf16[1536,512]{0,1:T(8,128)(2,1)}) %all-gather.3.cloned.1.call-update) | async-done | bytes 1572880 | tf_op jit(solution)/shard_map/all_gather | solution.py:23
  54.3 1.9 slice_select_fusion
  57.2 139.9 %all-reduce.3.cloned.1.call-done = bf16[512,512]{0,1:T(8,128)(2,1)} async-done(((bf16[512,512]{0,1:T(8,128)(2,1)}), bf16[512,512]{0,1:T(8,128)(2,1)}) %all-reduce.3.cloned.1.call-update) | async-done | bytes 524304 | tf_op jit(solution)/shard_map/psum | solution.py:9
  201.9 11.7 %cholesky.104 = f32[128,128]{1,0:T(8,128)S(1)} custom-call(f32[128,128]{1,0:T(8,128)S(1)} %cholesky.266), custom_call_target="Cholesky" | custom-call | tf_op jit(solution)/shard_map/jit(cholesky)/cholesky | solution.py:34
  213.7 9.8 %custom-call.30 = f32[1,128,128]{1,2,0:T(8,128)S(1)} custom-call(f32[1,128,128]{2,1,0:T(8,128)S(1)} %get-tuple-element.31), custom_call_target="InvertDiagBlocksLowerTriangular" | custom-call | tf_op jit(solution)/shard_map/jit(cholesky)/cholesky | solution.py:34
  226.2 11.7 %cholesky.217 = f32[128,128]{1,0:T(8,128)S(1)} custom-call(f32[128,128]{1,0:T(8,128)S(1)} %cholesky.270), custom_call_target="Cholesky" | custom-call | tf_op jit(solution)/shard_map/jit(cholesky)/cholesky | solution.py:34
  237.9 9.9 %custom-call.31 = f32[1,128,128]{1,2,0:T(8,128)S(1)} custom-call(f32[1,128,128]{2,1,0:T(8,128)S(1)} %get-tuple-element.28), custom_call_target="InvertDiagBlocksLowerTriangular" | custom-call | tf_op jit(solution)/shard_map/jit(cholesky)/cholesky | solution.py:34
  249.4 11.7 %cholesky.238 = f32[128,128]{1,0:T(8,128)S(1)} custom-call(f32[128,128]{1,0:T(8,128)S(1)} %cholesky.275), custom_call_target="Cholesky" | custom-call | tf_op jit(solution)/shard_map/jit(cholesky)/cholesky | solution.py:34
  261.9 9.8 %custom-call.32 = f32[1,128,128]{1,2,0:T(8,128)S(1)} custom-call(f32[1,128,128]{2,1,0:T(8,128)S(1)} %get-tuple-element.25), custom_call_target="InvertDiagBlocksLowerTriangular" | custom-call | tf_op jit(solution)/shard_map/jit(cholesky)/cholesky | solution.py:34
  273.2 11.9 %cholesky.255 = f32[128,128]{1,0:T(8,128)S(1)} custom-call(f32[128,128]{1,0:T(8,128)S(1)} %convolution_subtract_fusion.6), custom_call_target="Cholesky" | custom-call | tf_op jit(solution)/shard_map/jit(cholesky)/cholesky | solution.py:34
  289.2 8.5 %while.1 = (s32[]{:T(128)}, f32[512,512]{1,0:T(8,128)S(1)}, s32[4,2]{0,1:T(2,128)S(1)}, f32[4,128,128]{2,1,0:T(8,128)S(1)}, s32[]{:T(128)}) while((s32[]{:T(128)}, f32[512,512]{1,0:T(8,128)S(1)}, s32[4,2]{0,1:T(2,128)S(1)}, f32[4,128,128]{2,1,0:T(8,128)S(1)}, s32[]{:T(128)}) %tuple.32), condition=%wide.while_cond, body=%wide.while_body.sunk | while | flops 2 | bytes 131189 | solution.py:35
  289.9 1.4 bitcast_dynamic-update-slice_fusion.2
  292.0 1.4 bitcast_dynamic-update-slice_fusion.2
  294.1 1.4 bitcast_dynamic-update-slice_fusion.2
  296.2 1.4 bitcast_dynamic-update-slice_fusion.2
  297.7 39.3 %custom-call.33 = f32[4,128,128]{1,2,0:T(8,128)S(1)} custom-call(f32[4,128,128]{2,1,0:T(8,128)S(1)} %get-tuple-element.9), custom_call_target="InvertDiagBlocksLowerTriangular" | custom-call | tf_op jit(solution)/shard_map/triangular_solve | solution.py:35
  344.6 6.6 %all-to-all-start = ((f32[3,16,96]{2,0,1:T(4,128)}), f32[3,16,96]{2,0,1:T(4,128)S(1)}, u32[]{:S(2)}, u32[]{:S(2)}) async-start(f32[3,16,96]{2,0,1:T(4,128)} %copy.38), calls=%async_computation | async-start | bytes 65536 | tf_op jit(solution)/shard_map/all_to_all | solution.py:20
  351.2 46.1 %all-gather.5.cloned.1.call-done = bf16[24576,64]{0,1:T(8,128)(2,1)} async-done(((bf16[1536,64]{0,1:T(8,128)(2,1)}), bf16[24576,64]{0,1:T(8,128)(2,1)}) %all-gather.5.cloned.1.call-update) | async-done | bytes 3145744 | tf_op jit(solution)/shard_map/all_gather | solution.py:55
  397.3 3.8 copy.53
  401.2 5.0 all-to-all-start.1
  407.7 4.8 gather_fusion
  412.4 1.4 copy.40
  413.9 53.5 %psum.15 = bf16[3,512]{1,0:T(4,128)(2,1)S(1)} all-reduce(bf16[3,512]{1,0:T(4,128)(2,1)S(1)} %fusion.47), channel_id=1, replica_groups=mesh['row'=16,'col'=8] {'row'}, use_global_device_ids=true, to_apply=%region_9.10 | all-reduce | flops 1536 | bytes 6144 | tf_op jit(solution)/shard_map/psum | solution.py:9
  467.4 1.7 fusion.11
  469.2 3.7 gather_fusion.1
  474.3 2.6 copy.43
  476.9 2.7 fusion.2
  479.7 2.5 copy.49
  482.2 3.8 copy.45
  486.1 10.5 %broadcast_multiply_fusion = f32[12,128,24,128]{3,1,2,0:T(8,128)} fusion(f32[12,24]{1,0:T(8,128)S(1)} %convert_element_type.39, bf16[12,128,512,1]{2,1,3,0:T(8,128)(2,1)} %bitcast.99, bf16[24,128,512]{2,1,0:T(8,128)(2,1)S(1)} %copy.45), kind=kOutput, calls=%fused_computation.6 | convolution fusion | flops 4836556800 | bytes 23594112 | tf_op jit(solution)/shard_map/ik,jk->ij/dot_general | solution.py:61
  496.6 17.1 %copy.46 = f32[12,128,24,128]{3,2,1,0:T(8,128)S(1)} copy(f32[12,128,24,128]{3,1,2,0:T(8,128)} %broadcast_multiply_fusion) | data formatting | bytes 37748736 | tf_op jit(solution)/shard_map/mul | solution.py:63
  513.7 6.9 %fusion = bf16[1536,3072]{1,0:T(8,128)(2,1)} fusion(f32[192,8,24,128]{3,2,1,0:T(8,128)S(1)} %bitcast.92, bf16[1536,3072]{1,0:T(8,128)(2,1)S(1)} %bitcast.96), kind=kLoop, calls=%fused_computation.5 | loop fusion | flops 14155776 | bytes 37748736 | tf_op jit(solution)/shard_map/convert_element_type | solution.py:66
  (91 shorter events, 27.6 us)
Async XLA Ops:
  7.2 47.2 %all-gather.3.cloned.1.call-start = ((), (), s32[]{:S(2)}) async-start(), calls=%async_computation.2 | async-start | bytes 1769472 | tf_op jit(solution)/shard_map/all_gather | solution.py:23
  7.9 189.2 %all-reduce.3.cloned.1.call-start = ((), (), s32[]{:S(2)}) async-start(), calls=%async_computation.3 | async-start | bytes 1048576 | tf_op jit(solution)/shard_map/psum | solution.py:9
  56.2 341.1 %all-gather.5.cloned.1.call-start = ((), (), s32[]{:S(2)}) async-start(), calls=%async_computation.4 | async-start | bytes 3342336 | tf_op jit(solution)/shard_map/all_gather | solution.py:55
  337.0 4.0 copy-start.4
  339.0 3.0 copy-start.1
  339.9 2.1 copy-start.2
  340.6 3.3 copy-start.5
  341.0 60.2 %copy-start.3 = (f32[128,512]{1,0:T(8,128)}, f32[128,512]{1,0:T(8,128)S(1)}, u32[]{:S(2)}) copy-start(f32[128,512]{1,0:T(8,128)S(1)} %fusion.27) | copy-start | bytes 786436
  342.0 1.1 copy-start
  344.6 56.5 %all-to-all-start = ((f32[3,16,96]{2,0,1:T(4,128)}), f32[3,16,96]{2,0,1:T(4,128)S(1)}, u32[]{:S(2)}, u32[]{:S(2)}) async-start(f32[3,16,96]{2,0,1:T(4,128)} %copy.38), calls=%async_computation | async-start | bytes 65536 | tf_op jit(solution)/shard_map/all_to_all | solution.py:20
  401.2 5.1 copy-start.8
  401.2 5.1 copy-start.7
  401.2 5.2 copy-start.6
  401.2 78.5 %all-to-all-start.1 = ((bf16[8,3072,64]{1,2,0:T(8,128)(2,1)}), bf16[8,3072,64]{1,2,0:T(8,128)(2,1)S(1)}, u32[]{:S(2)}, u32[]{:S(2)}) async-start(bf16[8,3072,64]{1,2,0:T(8,128)(2,1)} %bitcast.84), calls=%async_computation.1 | async-start | bytes 6291456 | tf_op jit(solution)/shard_map/all_to_all | solution.py:56
  486.0 27.6 %slice-start = ((s8[9437184]{0:T(1024)(128)(4,1)}), s8[4194304]{0:T(1024)(128)(4,1)S(1)}, s32[]{:S(2)}) async-start(s8[9437184]{0:T(1024)(128)(4,1)} %bitcast.95), calls=%async_computation.5 | async-start | bytes 8388608
  486.1 27.6 %slice-start.1 = ((s8[9437184]{0:T(1024)(128)(4,1)}), s8[4194304]{0:T(1024)(128)(4,1)S(1)}, s32[]{:S(2)}) async-start(s8[9437184]{0:T(1024)(128)(4,1)} %bitcast.95), calls=%async_computation.6 | async-start | bytes 8388608
  496.6 17.1 %slice-start.2 = ((s8[9437184]{0:T(1024)(128)(4,1)}), s8[1048576]{0:T(1024)(128)(4,1)S(1)}, s32[]{:S(2)}) async-start(s8[9437184]{0:T(1024)(128)(4,1)} %bitcast.95), calls=%async_computation.7 | async-start | bytes 2097152
Sparse Core Ops, SparseCore 0:
  9.6 44.6 all-gather.2
  57.4 139.6 all-reduce.2
  344.0 53.2 all-gather.4
where the time goes:
time: 537 us; the launch traced here: 528 us
  waiting for transfers between devices  232 us (43%)
  other arithmetic  130 us (24%)
  local copies, waits for them, and re-layouts  56.1 us (10%)
  blocking collectives  53.5 us (10%)
  matrix products  25.3 us (5%)
  between operations  18 us (3%)
  starting transfers between devices  11.8 us (2%)
    psum x1, waiting for transfers between devices, broadcast(): return lax.psum(jnp.where(mine, array, jnp.zeros_like(array)), axis)  140 us
    another operation x14, other arithmetic, per_device(): lower_factor = jnp.linalg.cholesky(symmetric)  78.8 us
    psum x1, blocking collectives, broadcast(): return lax.psum(jnp.where(mine, array, jnp.zeros_like(array)), axis)  53.5 us
    all_gather x1, waiting for transfers between devices, per_device(): gathered = lax.all_gather(column_part, 'row', axis=0, tiled=True)  46.1 us
    all_gather x1, waiting for transfers between devices, per_device(): panel_rows = lax.all_gather(panel, 'col', axis=1, tiled=True)  45.7 us
    another operation x3, other arithmetic, per_device(): lax.linalg.triangular_solve(lower_factor, jnp.eye(pivot_size, dtype=jnp.f...  39.4 us
    mul x1, local copies, waits for them, and re-layouts, per_device(): product.reshape(block_rows, block_size, block_cols, block_size)  17.1 us
  transfers between devices with their start and end apart: 5, of which 3 were waited for; matrix products, arithmetic and copies ran while one was open for 5% of the time, Pallas kernels for 0%

commit v1 on v0

v1 whole, which is shorter than its diff:
```python
import jax
import jax.numpy as jnp
from jax import lax
from jax.experimental import pallas as pl
from jax.experimental.pallas import tpu as pltpu
from jax.sharding import PartitionSpec as P

HI = lax.Precision.HIGHEST
F32 = jnp.float32
BF16 = jnp.bfloat16
BLOCK = 128

X_SHIFT = {k: [(i, (i // 4 + k) % 4 * 4 + i % 4) for i in range(16)] for k in (1, 2, 3)}
Y_SHIFT = {k: [(i, (i // 2 + k) % 4 * 2 + i % 2) for i in range(8)] for k in (1, 2, 3)}
Z_HI = [(i, i ^ 2) for i in range(16)]
CORE = [(i, i ^ 1) for i in range(16)]
Z_LO = [(i, i ^ 1) for i in range(8)]


def transposed_place():
    pairs = []
    for row in range(16):
        for col in range(8):
            x, z_hi, core = row // 4, row // 2 % 2, row % 2
            y, z_lo = col // 2, col % 2
            pairs.append((row * 8 + col, ((y * 2 + z_lo) * 2 + core) * 8 + x * 2 + z_hi))
    return pairs


def pair_up(mine, bit, perm, axis):
    other = lax.ppermute(mine, axis, perm)
    low = jnp.where(bit == 0, mine, other)
    high = jnp.where(bit == 0, other, mine)
    return jnp.concatenate([low, high], 0)


def ring(mine, shifts, axis):
    return [mine] + [lax.ppermute(mine, axis, shifts[k]) for k in (1, 2, 3)]


def select_root(mine, row_place, root):
    x, root_x = row_place // 4, root // 4
    pieces = ring(mine, X_SHIFT, "row")
    back = (x - root_x) % 4
    mine = jnp.where(
        back == 0, pieces[0], jnp.where(back == 1, pieces[1], jnp.where(back == 2, pieces[2], pieces[3]))
    )
    other = lax.ppermute(mine, "row", Z_HI)
    mine = jnp.where(row_place // 2 % 2 == root // 2 % 2, mine, other)
    other = lax.ppermute(mine, "row", CORE)
    return jnp.where(row_place % 2 == root % 2, mine, other)


def block_inverse(rows):
    n = rows[0].shape[1]
    lane = lax.broadcasted_iota(jnp.int32, (8, n), 1)
    sub = lax.broadcasted_iota(jnp.int32, (8, n), 0)
    rows = list(rows)
    out = []
    for g in range(len(rows)):
        p = 8 * g
        below = range(g + 1, len(rows))
        strip = rows[g]
        cols = [jnp.broadcast_to(strip[:, p + k : p + k + 1], (8, n)) for k in range(8)]
        cols_below = {
            i: [jnp.broadcast_to(rows[i][:, p + k : p + k + 1], (8, n)) for k in range(8)] for i in below
        }
        in_block = (lane >= p) & (lane < p + 8)
        for i in below:
            rows[i] = jnp.where(in_block, 0.0, rows[i])
        pivots = None
        for k in range(8):
            d = jnp.broadcast_to(cols[k][k : k + 1, :], (8, n))
            r = 1.0 / d
            pivots = d if k == 0 else jnp.where(sub == k, d, pivots)
            m = jnp.where(sub > k, cols[k] * r, 0.0)
            piv = jnp.where(lane == p + k, 1.0, jnp.broadcast_to(strip[k : k + 1, :], (8, n)))
            strip = jnp.where((lane == p + k) & (sub > k), 0.0, strip) - m * piv
            piv = jnp.where((lane > p + k) & (lane < p + 8), 0.0, piv)
            u = [None] * 8
            for q in range(k + 1, 8):
                u[q] = jnp.broadcast_to(cols[q][k : k + 1, :], (8, n))
                cols[q] = cols[q] - m * u[q]
            for i in below:
                f = cols_below[i][k] * r
                for q in range(k + 1, 8):
                    cols_below[i][q] = cols_below[i][q] - f * u[q]
                rows[i] = rows[i] - f * piv
        s = lax.rsqrt(pivots)
        out.append(jnp.where(lane == sub + p, s, strip * s))
    return out


def inverse_kernel(place_ref, p0, p1, p2, p3, w_ref, half_ref, g_ref):
    n = w_ref.shape[0]
    B = BLOCK
    for k, piece in enumerate((p0, p1, p2, p3)):
        at = pl.multiple_of((place_ref[0] + 4 - k) % 4 * B, B)
        g_ref[pl.ds(at, B), :] = piece[...].astype(F32)
    whole = g_ref[...]
    g_ref[...] = 0.5 * (whole + whole.T)
    lane = lax.broadcasted_iota(jnp.int32, (B, n), 1)
    row = lax.broadcasted_iota(jnp.int32, (B, n), 0)
    lane_b = lax.broadcasted_iota(jnp.int32, (B, B), 1)
    row_b = lax.broadcasted_iota(jnp.int32, (B, B), 0)

    def step(k, carry):
        at = pl.multiple_of(k * B, B)
        diag = g_ref[pl.ds(at, B), pl.ds(at, B)]
        wk = jnp.concatenate(block_inverse([diag[8 * i : 8 * i + 8] for i in range(B // 8)]), 0)
        wk = jnp.where(lane_b <= row_b, wk, 0.0)
        here = (lane >= at) & (lane < at + B)
        strip = jnp.where(here, jnp.where(lane == row + at, 1.0, 0.0), g_ref[pl.ds(at, B), :])
        y = jnp.dot(wk, strip, precision=HI, preferred_element_type=F32)
        done = jnp.where(lane <= row + at, y, 0.0)
        w_ref[pl.ds(at, B), :] = done
        half_ref[pl.ds(at, B), :] = done.astype(BF16)
        for j in range(1, n // B):

            @pl.when(j > k)
            def _():
                old = jnp.where(here, 0.0, g_ref[j * B : (j + 1) * B, :])
                g_ref[j * B : (j + 1) * B, :] = old - lax.dot_general(
                    y[:, j * B : (j + 1) * B],
                    y,
                    (((0,), (0,)), ((), ())),
                    precision=HI,
                    preferred_element_type=F32,
                )

        return carry

    lax.fori_loop(0, n // B, step, 0)


def inverse_of(pieces, y):
    n = pieces[0].shape[1]
    vmem = pl.BlockSpec(memory_space=pltpu.VMEM)
    return pl.pallas_call(
        inverse_kernel,
        out_shape=(jax.ShapeDtypeStruct((n, n), F32), jax.ShapeDtypeStruct((n, n), BF16)),
        in_specs=[pl.BlockSpec(memory_space=pltpu.SMEM)] + [vmem] * 4,
        out_specs=(vmem, vmem),
        scratch_shapes=[pltpu.VMEM((n, n), F32)],
        compiler_params=pltpu.CompilerParams(vmem_limit_bytes=24 << 20),
        cost_estimate=pl.CostEstimate(flops=2 * n**3, bytes_accessed=4 * n * n, transcendentals=0),
    )(y.reshape(1), *pieces)


def update_kernel(place_ref, pattern_ref, *refs):
    rows_in, first_in, second_in = refs[0:4], refs[4:8], refs[8:12]
    w_ref, half_ref, loads_ref, pivot_ref, trailing_ref, out_ref, loads_out_ref = refs[12:19]
    raw_ref, factor_ref, other_ref = refs[19:22]
    n = half_ref.shape[0]
    row_dev = rows_in[0].shape[1]
    tile = out_ref.shape[1]
    step = pl.program_id(0)
    x, y, core, is_owner = place_ref[0], place_ref[1], place_ref[2], place_ref[3]

    def factor_of(pieces, spot, target, column):
        for k, piece in enumerate(pieces):
            at = pl.multiple_of((spot + 4 - k) % 4 * BLOCK, BLOCK)
            raw_ref[pl.ds(at, BLOCK), :] = piece[...]
        for c in range(0, row_dev, 512):
            part = jnp.dot(half_ref[...], raw_ref[:, c : c + 512], preferred_element_type=F32).astype(BF16)
            target[:, pl.ds(pl.multiple_of(column + c, 128), 512)] = part

    @pl.when(step == 0)
    def _():
        factor_of(first_in, x, other_ref, core * row_dev)
        factor_of(second_in, x, other_ref, (1 - core) * row_dev)
        for k, piece in enumerate(rows_in):
            at = pl.multiple_of((y + 4 - k) % 4 * BLOCK, BLOCK)
            raw_ref[pl.ds(at, BLOCK), :] = piece[...]
        for c in range(0, row_dev, 512):
            part = lax.dot_general(
                raw_ref[:, c : c + 512], half_ref[...], (((0,), (1,)), ((), ())), preferred_element_type=F32
            )
            factor_ref[c : c + 512, :] = part.astype(BF16)
        solve = lax.dot_general(
            pivot_ref[...], w_ref[...], (((1,), (1,)), ((), ())), precision=HI, preferred_element_type=F32
        )
        change = lax.dot_general(
            solve, factor_ref[...].astype(F32), (((1,), (1,)), ((), ())), precision=HI, preferred_element_type=F32
        )
        loads_out_ref[...] = loads_ref[...] - change

        @pl.when(is_owner == 1)
        def _():
            loads_out_ref[:, :n] = solve

    columns = other_ref[:, pl.ds(pl.multiple_of(step * tile, tile), tile)]
    for b in range(0, row_dev, 512):
        product = jnp.dot(factor_ref[b : b + 512, :], columns, preferred_element_type=F32)
        for i in range(0, 512, BLOCK):
            for j in range(0, tile, BLOCK):
                flag = pattern_ref[(b + i) // BLOCK, step * (tile // BLOCK) + j // BLOCK].astype(F32)
                old = trailing_ref[b + i : b + i + BLOCK, j : j + BLOCK].astype(F32)
                new = old - product[i : i + BLOCK, j : j + BLOCK] * flag
                out_ref[b + i : b + i + BLOCK, j : j + BLOCK] = new.astype(BF16)


def update(place, pattern, rows, first, second, w, half, regrouped, pivot_loads, trailing):
    row_dev, col_dev = trailing.shape
    n = half.shape[0]
    tile = 256
    smem = pl.BlockSpec(memory_space=pltpu.SMEM)
    vmem = pl.BlockSpec(memory_space=pltpu.VMEM)
    tiled = pl.BlockSpec((row_dev, tile), lambda s: (0, s))
    return pl.pallas_call(
        update_kernel,
        grid=(col_dev // tile,),
        out_shape=(
            jax.ShapeDtypeStruct((row_dev, col_dev), BF16),
            jax.ShapeDtypeStruct((8, row_dev), F32),
        ),
        in_specs=[smem, smem] + [vmem] * 16 + [tiled],
        out_specs=(tiled, vmem),
        scratch_shapes=[
            pltpu.VMEM((n, row_dev), BF16),
            pltpu.VMEM((row_dev, n), BF16),
            pltpu.VMEM((n, col_dev), BF16),
        ],
        compiler_params=pltpu.CompilerParams(vmem_limit_bytes=48 << 20),
        cost_estimate=pl.CostEstimate(flops=8 << 30, bytes_accessed=24 << 20, transcendentals=0),
    )(place, pattern, *rows, *first, *second, w, half, regrouped, pivot_loads, trailing)


def per_device(loads, nd_source, panel, trailing, pattern, owner):
    row_dev = panel.shape[0]
    row_count = lax.axis_size("row")
    pivot_size = panel.shape[1] * lax.axis_size("col")
    share_size = row_dev // row_count
    row_place = lax.axis_index("row")
    col_place = lax.axis_index("col")
    root = owner[0]
    x, z_hi, core = row_place // 4, row_place // 2 % 2, row_place % 2
    y, z_lo = col_place // 2, col_place % 2
    mine = panel.T

    pivot = select_root(mine[:, :pivot_size], row_place, root)
    pivot = ring(pair_up(pivot, z_lo, Z_LO, "col"), Y_SHIFT, "col")
    w, half = inverse_of(pivot, y)

    arrived = lax.all_to_all(loads, "row", split_axis=1, concat_axis=1, tiled=True)
    slot = nd_source // row_dev * share_size + (nd_source % row_dev - row_place * share_size)
    regrouped = jnp.take(arrived, slot, axis=1)
    regrouped = jnp.pad(regrouped, ((0, 5), (0, 0)))
    pivot_loads = select_root(regrouped[:, :pivot_size], row_place, root)

    rows = ring(pair_up(mine, z_lo, Z_LO, "col"), Y_SHIFT, "col")
    moved = lax.ppermute(mine, ("row", "col"), transposed_place())
    first = ring(pair_up(moved, z_hi, Z_HI, "row"), X_SHIFT, "row")
    second = [lax.ppermute(piece, "row", CORE) for piece in first]

    place = jnp.stack([x, y, core, (row_place == root).astype(jnp.int32)]).astype(jnp.int32)
    trailing_out, loads_out = update(
        place, pattern, rows, first, second, w, half, regrouped, pivot_loads, trailing
    )
    return loads_out[:3], trailing_out


def solution(mesh):
    return jax.shard_map(
        per_device,
        mesh=mesh,
        in_specs=(P(None, "row"), P("row"), P("row", "col"), P("row", "col"), P("row", "col"), P()),
        out_specs=(P(None, "row"), P("row", "col")),
        check_vma=False,
    )
```

time: 537 us -> 141 us (0.26)
  the two profiles are of different devices: /device:TPU:16 before, /device:TPU:9 now
where the time goes in v1:
time: 141 us; the launch traced here: 140 us
  waiting for transfers between devices  41.5 us (29%)
  Pallas kernels  41 us (29%)
  starting transfers between devices  40.3 us (29%)
  local copies, waits for them, and re-layouts  10 us (7%)
  between operations  4.24 us (3%)
  other arithmetic  2.8 us (2%)
    ppermute x15, waiting for transfers between devices, ring(): return [mine] + [lax.ppermute(mine, axis, shifts[k]) for k in (1, 2, 3)]  28.9 us
    pallas_call x1, Pallas kernels, update(): pl.pallas_call(update_kernel, grid=(col_dev // tile,), out_shape=(jax.Sha...  20.6 us
    pallas_call x1, Pallas kernels, inverse_of(): pl.pallas_call(inverse_kernel, out_shape=(jax.ShapeDtypeStruct((n, n), F3...  20.5 us
    ppermute x15, starting transfers between devices, ring(): return [mine] + [lax.ppermute(mine, axis, shifts[k]) for k in (1, 2, 3)]  10.3 us
    all_to_all x1, starting transfers between devices, per_device(): lax.all_to_all(loads, 'row', split_axis=1, concat_axis=1, tiled=True)  9.55 us
    ppermute x4, starting transfers between devices, per_device(): second = [lax.ppermute(piece, 'row', CORE) for piece in first]  7.81 us
    ppermute x3, waiting for transfers between devices, pair_up(): other = lax.ppermute(mine, axis, perm)  6.93 us
    ppermute x2, starting transfers between devices, select_root(): other = lax.ppermute(mine, 'row', CORE)  5.31 us
  transfers between devices with their start and end apart: 28, of which 10 were waited for; matrix products, arithmetic and copies ran while one was open for 5% of the time, Pallas kernels for 15%

profile of v1, /device:TPU:9, one launch (start us, length us, event | category | flops | bytes accessed | tf_op | source)
XLA Modules:
  0.0 139.9 jit_solution(15530169271636808205)
XLA Ops:
  0.6 0.8 slice.18
  1.5 2.5 %collective-permute-start.15 = (bf16[64,512]{1,0:T(8,128)(2,1)S(1)}, bf16[64,512]{1,0:T(8,128)(2,1)S(1)}, u32[]{:S(2)}, u32[]{:S(2)}) collective-permute-start(bf16[64,512]{1,0:T(8,128)(2,1)S(1)} %slice.18), channel_id=1, source_target_pairs={{0,96},{8,104},{16,112},{24,120},{32,0},{40,8},{48,16},{56,24},{64... | collective-permute-start | bytes 196616 | tf_op jit(solution)/shard_map/ppermute | solution.py:38
  5.1 3.3 %collective-permute-start.4 = (bf16[64,1536]{1,0:T(8,128)(2,1)}, bf16[64,1536]{1,0:T(8,128)(2,1)S(1)}, u32[]{:S(2)}, u32[]{:S(2)}) collective-permute-start(bf16[64,1536]{1,0:T(8,128)(2,1)} %bitcast.14), channel_id=1, source_target_pairs={{0,0},{1,16},{2,32},{3,48},{4,64},{5,80},{6,96},{7,112},{8,8},{9,2... | collective-permute-start | bytes 589832 | tf_op jit(solution)/shard_map/ppermute | solution.py:252
  8.4 3.1 %collective-permute-start = (bf16[64,1536]{1,0:T(8,128)(2,1)}, bf16[64,1536]{1,0:T(8,128)(2,1)S(1)}, u32[]{:S(2)}, u32[]{:S(2)}) collective-permute-start(bf16[64,1536]{1,0:T(8,128)(2,1)} %bitcast.15), channel_id=1, source_target_pairs={{0,1},{1,0},{2,3},{3,2},{4,5},{5,4},{6,7},{7,6},{8,9},{9,8},{10,11... | collective-permute-start | bytes 589832 | tf_op jit(solution)/shard_map/ppermute | solution.py:31
  11.5 0.8 all_to_all.8
  12.9 9.5 %all-to-all-start = ((f32[3,16,96]{2,0,1:T(4,128)}), f32[3,16,96]{2,0,1:T(4,128)S(1)}, u32[]{:S(2)}, u32[]{:S(2)}) async-start(f32[3,16,96]{2,0,1:T(4,128)} %copy.12), calls=%async_computation | async-start | bytes 65536 | tf_op jit(solution)/shard_map/all_to_all | solution.py:245
  25.9 3.9 %all-to-all-done = f32[3,16,96]{2,0,1:T(4,128)S(1)} async-done(((f32[3,16,96]{2,0,1:T(4,128)}), f32[3,16,96]{2,0,1:T(4,128)S(1)}, u32[]{:S(2)}, u32[]{:S(2)}) %all-to-all-start) | async-done | bytes 18464 | tf_op jit(solution)/shard_map/all_to_all | solution.py:245
  30.1 2.6 %gather_fusion = f32[1536,3]{1,0:T(8,128)S(1)} fusion(f32[3,1536]{0,1:T(8,128)S(1)} %bitcast.12, s32[2048]{0:T(1024)S(1)} %pad_clamp_fusion), kind=kCustom, calls=%fused_computation | custom fusion | bytes 43008 | tf_op jit(solution)/shard_map/jit(_take)/gather | solution.py:247
  33.0 0.9 collective-permute-start.24
  34.0 1.2 collective-permute-start.23
  35.2 0.9 select_select_fusion
  36.6 1.4 %collective-permute-done.23 = f32[8,512]{1,0:T(8,128)S(1)} collective-permute-done((f32[8,512]{1,0:T(8,128)S(1)}, f32[8,512]{1,0:T(8,128)S(1)}, u32[]{:S(2)}, u32[]{:S(2)}) %collective-permute-start.23) | collective-permute-done | bytes 16416 | tf_op jit(solution)/shard_map/ppermute | solution.py:38
  38.1 1.2 collective-permute-done.22
  39.3 1.4 %collective-permute-done.16 = bf16[64,512]{1,0:T(8,128)(2,1)S(1)} collective-permute-done((bf16[64,512]{1,0:T(8,128)(2,1)S(1)}, bf16[64,512]{1,0:T(8,128)(2,1)S(1)}, u32[]{:S(2)}, u32[]{:S(2)}) %collective-permute-start.16) | collective-permute-done | bytes 65568 | tf_op jit(solution)/shard_map/ppermute | solution.py:48
  40.7 2.4 %collective-permute-start.17 = (bf16[64,512]{1,0:T(8,128)(2,1)S(1)}, bf16[64,512]{1,0:T(8,128)(2,1)S(1)}, u32[]{:S(2)}, u32[]{:S(2)}) collective-permute-start(bf16[64,512]{1,0:T(8,128)(2,1)S(1)} %broadcast_select_fusion.4), channel_id=1, source_target_pairs={{0,8},{8,0},{16,24},{24,16},{32,40},{40,32},{48,56},{56,48},{64,72... | collective-permute-start | bytes 196616 | tf_op jit(solution)/shard_map/ppermute | solution.py:50
  43.4 3.0 %collective-permute-start.26 = (f32[8,512]{1,0:T(8,128)S(1)}, f32[8,512]{1,0:T(8,128)}, u32[]{:S(2)}, u32[]{:S(2)}) collective-permute-start(f32[8,512]{1,0:T(8,128)S(1)} %broadcast_select_fusion.8), channel_id=1, source_target_pairs={{0,8},{8,0},{16,24},{24,16},{32,40},{40,32},{48,56},{56,48},{64,72... | collective-permute-start | bytes 49160 | tf_op jit(solution)/shard_map/ppermute | solution.py:50
  46.5 1.0 broadcast_select_fusion.3
  48.0 2.2 %collective-permute-done.18 = bf16[64,512]{1,0:T(8,128)(2,1)S(1)} collective-permute-done((bf16[64,512]{1,0:T(8,128)(2,1)S(1)}, bf16[64,512]{1,0:T(8,128)(2,1)S(1)}, u32[]{:S(2)}, u32[]{:S(2)}) %collective-permute-start.18) | collective-permute-done | bytes 65568 | tf_op jit(solution)/shard_map/ppermute | solution.py:31
  50.6 4.8 %collective-permute-done.5 = bf16[64,1536]{1,0:T(8,128)(2,1)S(1)} collective-permute-done((bf16[64,1536]{1,0:T(8,128)(2,1)S(1)}, bf16[64,1536]{1,0:T(8,128)(2,1)S(1)}, u32[]{:S(2)}, u32[]{:S(2)}) %collective-permute-start.5) | collective-permute-done | bytes 196640 | tf_op jit(solution)/shard_map/ppermute | solution.py:31
  55.4 1.3 collective-permute-start.19
  56.8 1.1 collective-permute-start.2
  57.9 14.4 %collective-permute-done.21.p3 = bf16[128,512]{1,0:T(8,128)(2,1)S(1)} collective-permute-done((bf16[128,512]{1,0:T(8,128)(2,1)S(1)}, bf16[128,512]{1,0:T(8,128)(2,1)S(1)}, u32[]{:S(2)}, u32[]{:S(2)}) %collective-permute-start.21) | collective-permute-done | bytes 131104 | tf_op jit(solution)/shard_map/ppermute | solution.py:38
  72.7 0.9 collective-permute-start.7
  74.4 1.9 %collective-permute-start.9 = (bf16[128,1536]{1,0:T(8,128)(2,1)S(1)}, bf16[128,1536]{1,0:T(8,128)(2,1)}, u32[]{:S(2)}, u32[]{:S(2)}) collective-permute-start(bf16[128,1536]{1,0:T(8,128)(2,1)S(1)} %pad_maximum_fusion.1.refs_4_), channel_id=1, source_target_pairs={{0,8},{8,0},{16,24},{24,16},{32,40},{40,32},{48,56},{56,48},{64,72... | collective-permute-start | bytes 1179656 | tf_op jit(solution)/shard_map/ppermute | solution.py:254
  76.3 5.8 %collective-permute-done.8.refs_7_ = bf16[128,1536]{1,0:T(8,128)(2,1)S(1)} collective-permute-done((bf16[128,1536]{1,0:T(8,128)(2,1)S(1)}, bf16[128,1536]{1,0:T(8,128)(2,1)S(1)}, u32[]{:S(2)}, u32[]{:S(2)}) %collective-permute-start.8) | collective-permute-done | bytes 393248 | tf_op jit(solution)/shard_map/ppermute | solution.py:38
  82.1 3.0 %collective-permute-start.12 = (bf16[128,1536]{1,0:T(8,128)(2,1)S(1)}, bf16[128,1536]{1,0:T(8,128)(2,1)}, u32[]{:S(2)}, u32[]{:S(2)}) collective-permute-start(bf16[128,1536]{1,0:T(8,128)(2,1)S(1)} %collective-permute-done.8.refs_7_), channel_id=1, source_target_pairs={{0,8},{8,0},{16,24},{24,16},{32,40},{40,32},{48,56},{56,48},{64,72... | collective-permute-start | bytes 1179656 | tf_op jit(solution)/shard_map/ppermute | solution.py:254
  85.1 2.5 %collective-permute-start.11 = (bf16[128,1536]{1,0:T(8,128)(2,1)S(1)}, bf16[128,1536]{1,0:T(8,128)(2,1)}, u32[]{:S(2)}, u32[]{:S(2)}) collective-permute-start(bf16[128,1536]{1,0:T(8,128)(2,1)S(1)} %collective-permute-done.7.refs_6_), channel_id=1, source_target_pairs={{0,8},{8,0},{16,24},{24,16},{32,40},{40,32},{48,56},{56,48},{64,72... | collective-permute-start | bytes 1179656 | tf_op jit(solution)/shard_map/ppermute | solution.py:254
  87.6 6.1 %collective-permute-done.6.refs_5_ = bf16[128,1536]{1,0:T(8,128)(2,1)S(1)} collective-permute-done((bf16[128,1536]{1,0:T(8,128)(2,1)S(1)}, bf16[128,1536]{1,0:T(8,128)(2,1)S(1)}, u32[]{:S(2)}, u32[]{:S(2)}) %collective-permute-start.6) | collective-permute-done | bytes 393248 | tf_op jit(solution)/shard_map/ppermute | solution.py:38
  95.6 0.9 copy-done.1
  96.5 20.5 %shard_map.77 = (f32[512,512]{1,0:T(8,128)S(1)}, bf16[512,512]{1,0:T(8,128)(2,1)S(1)}) custom-call(s32[1]{0:T(128)} %bitcast.1.place_ref, bf16[128,512]{1,0:T(8,128)(2,1)S(1)} %pad_maximum_fusion.2.p0, bf16[128,512]{1,0:T(8,128)(2,1)S(1)} %copy-done.1, bf16[128,512]{1,0:T(8,128)(2,1)S(1)} %collective-permute-done.20.p2, ...), custom_call_target="tpu_custom_call" | custom-call | flops 268435456 | bytes 1048576 | tf_op jit(solution)/shard_map/pallas_call | solution.py:139
  117.0 1.0 copy-done.3
  118.7 20.6 %shard_map.78 = (bf16[1536,3072]{1,0:T(8,128)(2,1)}, f32[8,1536]{1,0:T(8,128)S(1)}) custom-call(s32[4]{0:T(128)S(1)} %pad_add_fusion.place_ref, s32[12,24]{1,0:T(8,128)S(1)} %copy-done.2, bf16[128,1536]{1,0:T(8,128)(2,1)S(1)} %pad_maximum_fusion.refs_0_, bf16[128,1536]{1,0:T(8,128)(2,1)S(1)} %collective-permute-done.1.refs_1_, ...), custom_call_target="tpu_custom_call" | custom-call | flops 8589934592 | bytes 25165824 | tf_op jit(solution)/shard_map/pallas_call | solution.py:210
  (61 shorter events, 9.1 us)
Async XLA Ops:
  1.5 31.5 %collective-permute-start.15 = (bf16[64,512]{1,0:T(8,128)(2,1)S(1)}, bf16[64,512]{1,0:T(8,128)(2,1)S(1)}, u32[]{:S(2)}, u32[]{:S(2)}) collective-permute-start(bf16[64,512]{1,0:T(8,128)(2,1)S(1)} %slice.18), channel_id=1, source_target_pairs={{0,96},{8,104},{16,112},{24,120},{32,0},{40,8},{48,16},{56,24},{64... | collective-permute-start | bytes 196616 | tf_op jit(solution)/shard_map/ppermute | solution.py:38
  4.0 30.0 %collective-permute-start.14 = (bf16[64,512]{1,0:T(8,128)(2,1)S(1)}, bf16[64,512]{1,0:T(8,128)(2,1)S(1)}, u32[]{:S(2)}, u32[]{:S(2)}) collective-permute-start(bf16[64,512]{1,0:T(8,128)(2,1)S(1)} %slice.18), channel_id=1, source_target_pairs={{0,64},{8,72},{16,80},{24,88},{32,96},{40,104},{48,112},{56,120},{... | collective-permute-start | bytes 196616 | tf_op jit(solution)/shard_map/ppermute | solution.py:38
  4.5 30.7 %collective-permute-start.13 = (bf16[64,512]{1,0:T(8,128)(2,1)S(1)}, bf16[64,512]{1,0:T(8,128)(2,1)S(1)}, u32[]{:S(2)}, u32[]{:S(2)}) collective-permute-start(bf16[64,512]{1,0:T(8,128)(2,1)S(1)} %slice.18), channel_id=1, source_target_pairs={{0,32},{8,40},{16,48},{24,56},{32,64},{40,72},{48,80},{56,88},{64,... | collective-permute-start | bytes 196616 | tf_op jit(solution)/shard_map/ppermute | solution.py:38
  5.1 42.6 %collective-permute-start.4 = (bf16[64,1536]{1,0:T(8,128)(2,1)}, bf16[64,1536]{1,0:T(8,128)(2,1)S(1)}, u32[]{:S(2)}, u32[]{:S(2)}) collective-permute-start(bf16[64,1536]{1,0:T(8,128)(2,1)} %bitcast.14), channel_id=1, source_target_pairs={{0,0},{1,16},{2,32},{3,48},{4,64},{5,80},{6,96},{7,112},{8,8},{9,2... | collective-permute-start | bytes 589832 | tf_op jit(solution)/shard_map/ppermute | solution.py:252
  8.4 38.0 %collective-permute-start = (bf16[64,1536]{1,0:T(8,128)(2,1)}, bf16[64,1536]{1,0:T(8,128)(2,1)S(1)}, u32[]{:S(2)}, u32[]{:S(2)}) collective-permute-start(bf16[64,1536]{1,0:T(8,128)(2,1)} %bitcast.15), channel_id=1, source_target_pairs={{0,1},{1,0},{2,3},{3,2},{4,5},{5,4},{6,7},{7,6},{8,9},{9,8},{10,11... | collective-permute-start | bytes 589832 | tf_op jit(solution)/shard_map/ppermute | solution.py:31
  12.9 16.9 %all-to-all-start = ((f32[3,16,96]{2,0,1:T(4,128)}), f32[3,16,96]{2,0,1:T(4,128)S(1)}, u32[]{:S(2)}, u32[]{:S(2)}) async-start(f32[3,16,96]{2,0,1:T(4,128)} %copy.12), calls=%async_computation | async-start | bytes 65536 | tf_op jit(solution)/shard_map/all_to_all | solution.py:245
  33.0 13.4 %copy-start.4 = (f32[3,1536]{1,0:T(4,128)}, f32[3,1536]{1,0:T(4,128)S(1)}, u32[]{:S(2)}) copy-start(f32[3,1536]{1,0:T(4,128)S(1)} %select_bitcast_fusion) | copy-start | bytes 55300
  33.0 3.0 %collective-permute-start.24 = (f32[8,512]{1,0:T(8,128)S(1)}, f32[8,512]{1,0:T(8,128)S(1)}, u32[]{:S(2)}, u32[]{:S(2)}) collective-permute-start(f32[8,512]{1,0:T(8,128)S(1)} %pad_slice_fusion), channel_id=1, source_target_pairs={{0,96},{8,104},{16,112},{24,120},{32,0},{40,8},{48,16},{56,24},{64... | collective-permute-start | bytes 49160 | tf_op jit(solution)/shard_map/ppermute | solution.py:38
  34.0 4.1 %collective-permute-start.23 = (f32[8,512]{1,0:T(8,128)S(1)}, f32[8,512]{1,0:T(8,128)S(1)}, u32[]{:S(2)}, u32[]{:S(2)}) collective-permute-start(f32[8,512]{1,0:T(8,128)S(1)} %pad_slice_fusion), channel_id=1, source_target_pairs={{0,64},{8,72},{16,80},{24,88},{32,96},{40,104},{48,112},{56,120},{... | collective-permute-start | bytes 49160 | tf_op jit(solution)/shard_map/ppermute | solution.py:38
  35.2 4.1 %collective-permute-start.22 = (f32[8,512]{1,0:T(8,128)S(1)}, f32[8,512]{1,0:T(8,128)S(1)}, u32[]{:S(2)}, u32[]{:S(2)}) collective-permute-start(f32[8,512]{1,0:T(8,128)S(1)} %pad_slice_fusion), channel_id=1, source_target_pairs={{0,32},{8,40},{16,48},{24,56},{32,64},{40,72},{48,80},{56,88},{64,... | collective-permute-start | bytes 49160 | tf_op jit(solution)/shard_map/ppermute | solution.py:38
  36.0 4.7 %collective-permute-start.16 = (bf16[64,512]{1,0:T(8,128)(2,1)S(1)}, bf16[64,512]{1,0:T(8,128)(2,1)S(1)}, u32[]{:S(2)}, u32[]{:S(2)}) collective-permute-start(bf16[64,512]{1,0:T(8,128)(2,1)S(1)} %select_select_fusion), channel_id=1, source_target_pairs={{0,16},{8,24},{16,0},{24,8},{32,48},{40,56},{48,32},{56,40},{64,80... | collective-permute-start | bytes 196616 | tf_op jit(solution)/shard_map/ppermute | solution.py:48
  39.3 4.1 %collective-permute-start.25 = (f32[8,512]{1,0:T(8,128)S(1)}, f32[8,512]{1,0:T(8,128)S(1)}, u32[]{:S(2)}, u32[]{:S(2)}) collective-permute-start(f32[8,512]{1,0:T(8,128)S(1)} %select_select_fusion.1), channel_id=1, source_target_pairs={{0,16},{8,24},{16,0},{24,8},{32,48},{40,56},{48,32},{56,40},{64,80... | collective-permute-start | bytes 49160 | tf_op jit(solution)/shard_map/ppermute | solution.py:48
  40.7 5.6 %collective-permute-start.17 = (bf16[64,512]{1,0:T(8,128)(2,1)S(1)}, bf16[64,512]{1,0:T(8,128)(2,1)S(1)}, u32[]{:S(2)}, u32[]{:S(2)}) collective-permute-start(bf16[64,512]{1,0:T(8,128)(2,1)S(1)} %broadcast_select_fusion.4), channel_id=1, source_target_pairs={{0,8},{8,0},{16,24},{24,16},{32,40},{40,32},{48,56},{56,48},{64,72... | collective-permute-start | bytes 196616 | tf_op jit(solution)/shard_map/ppermute | solution.py:50
  43.4 13.4 %collective-permute-start.26 = (f32[8,512]{1,0:T(8,128)S(1)}, f32[8,512]{1,0:T(8,128)}, u32[]{:S(2)}, u32[]{:S(2)}) collective-permute-start(f32[8,512]{1,0:T(8,128)S(1)} %broadcast_select_fusion.8), channel_id=1, source_target_pairs={{0,8},{8,0},{16,24},{24,16},{32,40},{40,32},{48,56},{56,48},{64,72... | collective-permute-start | bytes 49160 | tf_op jit(solution)/shard_map/ppermute | solution.py:50
  46.3 3.8 %collective-permute-start.18 = (bf16[64,512]{1,0:T(8,128)(2,1)S(1)}, bf16[64,512]{1,0:T(8,128)(2,1)S(1)}, u32[]{:S(2)}, u32[]{:S(2)}) collective-permute-start(bf16[64,512]{1,0:T(8,128)(2,1)S(1)} %broadcast_select_fusion.5), channel_id=1, source_target_pairs={{0,1},{1,0},{2,3},{3,2},{4,5},{5,4},{6,7},{7,6},{8,9},{9,8},{10,11... | collective-permute-start | bytes 196616 | tf_op jit(solution)/shard_map/ppermute | solution.py:31
  47.5 27.0 %collective-permute-start.3 = (bf16[128,1536]{1,0:T(8,128)(2,1)S(1)}, bf16[128,1536]{1,0:T(8,128)(2,1)S(1)}, u32[]{:S(2)}, u32[]{:S(2)}) collective-permute-start(bf16[128,1536]{1,0:T(8,128)(2,1)S(1)} %pad_maximum_fusion.refs_0_), channel_id=1, source_target_pairs={{0,6},{1,7},{2,0},{3,1},{4,2},{5,3},{6,4},{7,5},{8,14},{9,15},{10,... | collective-permute-start | bytes 1179656 | tf_op jit(solution)/shard_map/ppermute | solution.py:38
  47.6 7.7 %collective-permute-start.5 = (bf16[64,1536]{1,0:T(8,128)(2,1)S(1)}, bf16[64,1536]{1,0:T(8,128)(2,1)S(1)}, u32[]{:S(2)}, u32[]{:S(2)}) collective-permute-start(bf16[64,1536]{1,0:T(8,128)(2,1)S(1)} %collective-permute-done.4), channel_id=1, source_target_pairs={{0,16},{8,24},{16,0},{24,8},{32,48},{40,56},{48,32},{56,40},{64,80... | collective-permute-start | bytes 589832 | tf_op jit(solution)/shard_map/ppermute | solution.py:31
  50.2 22.1 %collective-permute-start.21 = (bf16[128,512]{1,0:T(8,128)(2,1)S(1)}, bf16[128,512]{1,0:T(8,128)(2,1)S(1)}, u32[]{:S(2)}, u32[]{:S(2)}) collective-permute-start(bf16[128,512]{1,0:T(8,128)(2,1)S(1)} %pad_maximum_fusion.2.p0), channel_id=1, source_target_pairs={{0,6},{1,7},{2,0},{3,1},{4,2},{5,3},{6,4},{7,5},{8,14},{9,15},{10,... | collective-permute-start | bytes 393224 | tf_op jit(solution)/shard_map/ppermute | solution.py:38
  50.4 22.3 %collective-permute-start.20 = (bf16[128,512]{1,0:T(8,128)(2,1)S(1)}, bf16[128,512]{1,0:T(8,128)(2,1)S(1)}, u32[]{:S(2)}, u32[]{:S(2)}) collective-permute-start(bf16[128,512]{1,0:T(8,128)(2,1)S(1)} %pad_maximum_fusion.2.p0), channel_id=1, source_target_pairs={{0,4},{1,5},{2,6},{3,7},{4,0},{5,1},{6,2},{7,3},{8,12},{9,13},{10,... | collective-permute-start | bytes 393224 | tf_op jit(solution)/shard_map/ppermute | solution.py:38
  55.4 18.2 %collective-permute-start.19 = (bf16[128,512]{1,0:T(8,128)(2,1)S(1)}, bf16[128,512]{1,0:T(8,128)(2,1)S(1)}, u32[]{:S(2)}, u32[]{:S(2)}) collective-permute-start(bf16[128,512]{1,0:T(8,128)(2,1)S(1)} %pad_maximum_fusion.2.p0), channel_id=1, source_target_pairs={{0,2},{1,3},{2,4},{3,5},{4,6},{5,7},{6,0},{7,1},{8,10},{9,11},{10,... | collective-permute-start | bytes 393224 | tf_op jit(solution)/shard_map/ppermute | solution.py:38
  56.8 17.7 %collective-permute-start.2 = (bf16[128,1536]{1,0:T(8,128)(2,1)S(1)}, bf16[128,1536]{1,0:T(8,128)(2,1)S(1)}, u32[]{:S(2)}, u32[]{:S(2)}) collective-permute-start(bf16[128,1536]{1,0:T(8,128)(2,1)S(1)} %pad_maximum_fusion.refs_0_), channel_id=1, source_target_pairs={{0,4},{1,5},{2,6},{3,7},{4,0},{5,1},{6,2},{7,3},{8,12},{9,13},{10,... | collective-permute-start | bytes 1179656 | tf_op jit(solution)/shard_map/ppermute | solution.py:38
  72.3 9.8 %collective-permute-start.8 = (bf16[128,1536]{1,0:T(8,128)(2,1)S(1)}, bf16[128,1536]{1,0:T(8,128)(2,1)S(1)}, u32[]{:S(2)}, u32[]{:S(2)}) collective-permute-start(bf16[128,1536]{1,0:T(8,128)(2,1)S(1)} %pad_maximum_fusion.1.refs_4_), channel_id=1, source_target_pairs={{0,96},{8,104},{16,112},{24,120},{32,0},{40,8},{48,16},{56,24},{64... | collective-permute-start | bytes 1179656 | tf_op jit(solution)/shard_map/ppermute | solution.py:38
  72.7 12.4 %collective-permute-start.7 = (bf16[128,1536]{1,0:T(8,128)(2,1)S(1)}, bf16[128,1536]{1,0:T(8,128)(2,1)S(1)}, u32[]{:S(2)}, u32[]{:S(2)}) collective-permute-start(bf16[128,1536]{1,0:T(8,128)(2,1)S(1)} %pad_maximum_fusion.1.refs_4_), channel_id=1, source_target_pairs={{0,64},{8,72},{16,80},{24,88},{32,96},{40,104},{48,112},{56,120},{... | collective-permute-start | bytes 1179656 | tf_op jit(solution)/shard_map/ppermute | solution.py:38
  74.2 19.4 %collective-permute-start.6 = (bf16[128,1536]{1,0:T(8,128)(2,1)S(1)}, bf16[128,1536]{1,0:T(8,128)(2,1)S(1)}, u32[]{:S(2)}, u32[]{:S(2)}) collective-permute-start(bf16[128,1536]{1,0:T(8,128)(2,1)S(1)} %pad_maximum_fusion.1.refs_4_), channel_id=1, source_target_pairs={{0,32},{8,40},{16,48},{24,56},{32,64},{40,72},{48,80},{56,88},{64,... | collective-permute-start | bytes 1179656 | tf_op jit(solution)/shard_map/ppermute | solution.py:38
  74.4 43.6 %collective-permute-start.1 = (bf16[128,1536]{1,0:T(8,128)(2,1)S(1)}, bf16[128,1536]{1,0:T(8,128)(2,1)S(1)}, u32[]{:S(2)}, u32[]{:S(2)}) collective-permute-start(bf16[128,1536]{1,0:T(8,128)(2,1)S(1)} %pad_maximum_fusion.refs_0_), channel_id=1, source_target_pairs={{0,2},{1,3},{2,4},{3,5},{4,6},{5,7},{6,0},{7,1},{8,10},{9,11},{10,... | collective-permute-start | bytes 1179656 | tf_op jit(solution)/shard_map/ppermute | solution.py:38
  74.4 43.6 %collective-permute-start.9 = (bf16[128,1536]{1,0:T(8,128)(2,1)S(1)}, bf16[128,1536]{1,0:T(8,128)(2,1)}, u32[]{:S(2)}, u32[]{:S(2)}) collective-permute-start(bf16[128,1536]{1,0:T(8,128)(2,1)S(1)} %pad_maximum_fusion.1.refs_4_), channel_id=1, source_target_pairs={{0,8},{8,0},{16,24},{24,16},{32,40},{40,32},{48,56},{56,48},{64,72... | collective-permute-start | bytes 1179656 | tf_op jit(solution)/shard_map/ppermute | solution.py:254
  82.1 35.9 %collective-permute-start.12 = (bf16[128,1536]{1,0:T(8,128)(2,1)S(1)}, bf16[128,1536]{1,0:T(8,128)(2,1)}, u32[]{:S(2)}, u32[]{:S(2)}) collective-permute-start(bf16[128,1536]{1,0:T(8,128)(2,1)S(1)} %collective-permute-done.8.refs_7_), channel_id=1, source_target_pairs={{0,8},{8,0},{16,24},{24,16},{32,40},{40,32},{48,56},{56,48},{64,72... | collective-permute-start | bytes 1179656 | tf_op jit(solution)/shard_map/ppermute | solution.py:254
  85.1 32.9 %collective-permute-start.11 = (bf16[128,1536]{1,0:T(8,128)(2,1)S(1)}, bf16[128,1536]{1,0:T(8,128)(2,1)}, u32[]{:S(2)}, u32[]{:S(2)}) collective-permute-start(bf16[128,1536]{1,0:T(8,128)(2,1)S(1)} %collective-permute-done.7.refs_6_), channel_id=1, source_target_pairs={{0,8},{8,0},{16,24},{24,16},{32,40},{40,32},{48,56},{56,48},{64,72... | collective-permute-start | bytes 1179656 | tf_op jit(solution)/shard_map/ppermute | solution.py:254
  93.6 24.4 %collective-permute-start.10 = (bf16[128,1536]{1,0:T(8,128)(2,1)S(1)}, bf16[128,1536]{1,0:T(8,128)(2,1)}, u32[]{:S(2)}, u32[]{:S(2)}) collective-permute-start(bf16[128,1536]{1,0:T(8,128)(2,1)S(1)} %collective-permute-done.6.refs_5_), channel_id=1, source_target_pairs={{0,8},{8,0},{16,24},{24,16},{32,40},{40,32},{48,56},{56,48},{64,72... | collective-permute-start | bytes 1179656 | tf_op jit(solution)/shard_map/ppermute | solution.py:254
  95.6 0.9 copy-start.1
  117.0 1.0 copy-start.3
  118.0 0.7 copy-start.2
  (1 other events, 0.7 us)

commit v2 on v1

--- a/solution.py
+++ b/solution.py
@@ -38,17 +38,54 @@
     return [mine] + [lax.ppermute(mine, axis, shifts[k]) for k in (1, 2, 3)]
 
 
-def select_root(mine, row_place, root):
-    x, root_x = row_place // 4, root // 4
-    pieces = ring(mine, X_SHIFT, "row")
-    back = (x - root_x) % 4
-    mine = jnp.where(
-        back == 0, pieces[0], jnp.where(back == 1, pieces[1], jnp.where(back == 2, pieces[2], pieces[3]))
-    )
-    other = lax.ppermute(mine, "row", Z_HI)
-    mine = jnp.where(row_place // 2 % 2 == root // 2 % 2, mine, other)
-    other = lax.ppermute(mine, "row", CORE)
-    return jnp.where(row_place % 2 == root % 2, mine, other)
+def after(value, *others):
+    return lax.optimization_barrier((value, others))[0]
+
+
+def pack_kernel(panel_ref, loads_ref, source_ref, out_ref):
+    size = out_ref.shape[1] // 3
+    source = source_ref[:, :size]
+    digits = jnp.concatenate([source // BLOCK, source % BLOCK, jnp.zeros((6, size), jnp.int32)], 0)
+    head = jnp.concatenate([panel_ref[:, :size].astype(F32), digits.astype(F32)], 0)
+    loads = loads_ref[...]
+    high = loads.astype(BF16).astype(F32)
+    low = loads - high
+    tail = jnp.concatenate([high, low, jnp.zeros((2, loads.shape[1]), F32)], 0)
+    for c in range(3):
+        out_ref[:24, c * size : (c + 1) * size] = head[24 * c : 24 * c + 24].astype(BF16)
+    out_ref[24:, :] = tail.astype(BF16)
+
+
+def pack(mine, loads, source):
+    return pl.pallas_call(
+        pack_kernel, out_shape=jax.ShapeDtypeStruct((32, mine.shape[1]), BF16)
+    )(mine, loads, source[None])
+
+
+def spread(packet, row_place, root):
+    back = (row_place // 4 - root // 4) % 4
+    pieces = ring(packet, X_SHIFT, "row")
+    head = pieces[3][:24]
+    for k in (2, 1, 0):
+        head = jnp.where(back == k, pieces[k][:24], head)
+    packet = jnp.concatenate([head] + [piece[24:] for piece in pieces], 0)
+    for bit, perm in ((2, Z_HI), (1, CORE)):
+        other = lax.ppermute(packet, "row", perm)
+        head = jnp.where((row_place & bit) == (root & bit), packet[:24], other[:24])
+        packet = jnp.concatenate([head, packet[24:], other[24:]], 0)
+    return packet
+
+
+def regroup(window_of, source, row_place, target, share):
+    arrived = lax.dynamic_slice_in_dim(window_of, target * share, share, 2)
+    arrived = arrived.transpose(1, 0, 2).reshape(arrived.shape[1], -1)
+    home = source // (share * 16)
+    flip = home ^ row_place
+    turn = (row_place // 4 - home // 4) % 4
+    place = ((flip & 1) * 2 + (flip // 2 & 1)) * 4 + turn
+    slot = place * share + source % (share * 16) - target * share
+    parts = jnp.take(arrived, slot, axis=1)
+    return jnp.concatenate([parts[:3].astype(F32) + parts[3:6].astype(F32), jnp.zeros((5, slot.shape[0]), F32)], 0)
 
 
 def block_inverse(rows):
@@ -91,14 +128,9 @@
     return out
 
 
-def inverse_kernel(place_ref, p0, p1, p2, p3, w_ref, half_ref, g_ref):
-    n = w_ref.shape[0]
+def eliminate(g_ref, w_ref, half_ref, blocks, first_row):
+    n = g_ref.shape[0]
     B = BLOCK
-    for k, piece in enumerate((p0, p1, p2, p3)):
-        at = pl.multiple_of((place_ref[0] + 4 - k) % 4 * B, B)
-        g_ref[pl.ds(at, B), :] = piece[...].astype(F32)
-    whole = g_ref[...]
-    g_ref[...] = 0.5 * (whole + whole.T)
     lane = lax.broadcasted_iota(jnp.int32, (B, n), 1)
     row = lax.broadcasted_iota(jnp.int32, (B, n), 0)
     lane_b = lax.broadcasted_iota(jnp.int32, (B, B), 1)
@@ -113,9 +145,10 @@
         strip = jnp.where(here, jnp.where(lane == row + at, 1.0, 0.0), g_ref[pl.ds(at, B), :])
         y = jnp.dot(wk, strip, precision=HI, preferred_element_type=F32)
         done = jnp.where(lane <= row + at, y, 0.0)
-        w_ref[pl.ds(at, B), :] = done
-        half_ref[pl.ds(at, B), :] = done.astype(BF16)
-        for j in range(1, n // B):
+        to = pl.multiple_of(at - first_row, B)
+        w_ref[pl.ds(to, B), :] = done
+        half_ref[pl.ds(to, B), :] = done.astype(BF16)
+        for j in range(blocks[0] + 1, n // B):
 
             @pl.when(j > k)
             def _():
@@ -130,27 +163,64 @@
 
         return carry
 
-    lax.fori_loop(0, n // B, step, 0)
-
-
-def inverse_of(pieces, y):
+    lax.fori_loop(*blocks, step, 0)
+
+
+def upper_kernel(place_ref, p0, p1, p2, p3, w_ref, half_ref, g_ref):
+    for k, piece in enumerate((p0, p1, p2, p3)):
+        at = pl.multiple_of((place_ref[0] + 4 - k) % 4 * BLOCK, BLOCK)
+        g_ref[pl.ds(at, BLOCK), :] = piece[...].astype(F32)
+    whole = g_ref[...]
+    g_ref[...] = 0.5 * (whole + whole.T)
+    eliminate(g_ref, w_ref, half_ref, (0, 2), 0)
+
+
+def lower_kernel(in_ref, w_ref, half_ref, g_ref):
+    g_ref[in_ref.shape[0] :, :] = in_ref[...]
+    eliminate(g_ref, w_ref, half_ref, (2, 4), 2 * BLOCK)
+
+
+def upper_inverse(pieces, y):
     n = pieces[0].shape[1]
     vmem = pl.BlockSpec(memory_space=pltpu.VMEM)
+
+    def kernel(place_ref, p0, p1, p2, p3, w_ref, half_ref, rest_ref, g_ref):
+        upper_kernel(place_ref, p0, p1, p2, p3, w_ref, half_ref, g_ref)
+        rest_ref[...] = g_ref[n // 2 :, :]
+
     return pl.pallas_call(
-        inverse_kernel,
-        out_shape=(jax.ShapeDtypeStruct((n, n), F32), jax.ShapeDtypeStruct((n, n), BF16)),
+        kernel,
+        out_shape=(
+            jax.ShapeDtypeStruct((n // 2, n), F32),
+            jax.ShapeDtypeStruct((n // 2, n), BF16),
+            jax.ShapeDtypeStruct((n // 2, n), F32),
+        ),
         in_specs=[pl.BlockSpec(memory_space=pltpu.SMEM)] + [vmem] * 4,
-        out_specs=(vmem, vmem),
+        out_specs=(vmem,) * 3,
         scratch_shapes=[pltpu.VMEM((n, n), F32)],
-        compiler_params=pltpu.CompilerParams(vmem_limit_bytes=24 << 20),
-        cost_estimate=pl.CostEstimate(flops=2 * n**3, bytes_accessed=4 * n * n, transcendentals=0),
+        compiler_params=pltpu.CompilerParams(vmem_limit_bytes=16 << 20),
+        cost_estimate=pl.CostEstimate(flops=10 << 30, bytes_accessed=4 * n * n, transcendentals=0),
     )(y.reshape(1), *pieces)
+
+
+def lower_inverse(rest):
+    half, n = rest.shape
+    vmem = pl.BlockSpec(memory_space=pltpu.VMEM)
+    return pl.pallas_call(
+        lower_kernel,
+        out_shape=(jax.ShapeDtypeStruct((half, n), F32), jax.ShapeDtypeStruct((half, n), BF16)),
+        in_specs=[vmem],
+        out_specs=(vmem,) * 2,
+        scratch_shapes=[pltpu.VMEM((n, n), F32)],
+        compiler_params=pltpu.CompilerParams(vmem_limit_bytes=16 << 20),
+        cost_estimate=pl.CostEstimate(flops=10 << 30, bytes_accessed=4 * n * n, transcendentals=0),
+    )(rest)
 
 
 def update_kernel(place_ref, pattern_ref, *refs):
     rows_in, first_in, second_in = refs[0:4], refs[4:8], refs[8:12]
-    w_ref, half_ref, loads_ref, pivot_ref, trailing_ref, out_ref, loads_out_ref = refs[12:19]
-    raw_ref, factor_ref, other_ref = refs[19:22]
+    w_top, w_low, half_top, half_low, loads_ref, pivot_ref, trailing_ref, out_ref, loads_out_ref = refs[12:21]
+    raw_ref, factor_ref, other_ref, half_ref = refs[21:25]
     n = half_ref.shape[0]
     row_dev = rows_in[0].shape[1]
     tile = out_ref.shape[1]
@@ -167,6 +237,8 @@
 
     @pl.when(step == 0)
     def _():
+        half_ref[: n // 2, :] = half_top[...]
+        half_ref[n // 2 :, :] = half_low[...]
         factor_of(first_in, x, other_ref, core * row_dev)
         factor_of(second_in, x, other_ref, (1 - core) * row_dev)
         for k, piece in enumerate(rows_in):
@@ -177,8 +249,14 @@
                 raw_ref[:, c : c + 512], half_ref[...], (((0,), (1,)), ((), ())), preferred_element_type=F32
             )
             factor_ref[c : c + 512, :] = part.astype(BF16)
-        solve = lax.dot_general(
-            pivot_ref[...], w_ref[...], (((1,), (1,)), ((), ())), precision=HI, preferred_element_type=F32
+        solve = jnp.concatenate(
+            [
+                lax.dot_general(
+                    pivot_ref[...], w[...], (((1,), (1,)), ((), ())), precision=HI, preferred_element_type=F32
+                )
+                for w in (w_top, w_low)
+            ],
+            1,
         )
         change = lax.dot_general(
             solve, factor_ref[...].astype(F32), (((1,), (1,)), ((), ())), precision=HI, preferred_element_type=F32
@@ -200,9 +278,9 @@
                 out_ref[b + i : b + i + BLOCK, j : j + BLOCK] = new.astype(BF16)
 
 
-def update(place, pattern, rows, first, second, w, half, regrouped, pivot_loads, trailing):
+def update(place, pattern, rows, first, second, w_parts, half_parts, regrouped, pivot_loads, trailing):
     row_dev, col_dev = trailing.shape
-    n = half.shape[0]
+    n = half_parts[0].shape[1]
     tile = 256
     smem = pl.BlockSpec(memory_space=pltpu.SMEM)
     vmem = pl.BlockSpec(memory_space=pltpu.VMEM)
@@ -214,16 +292,17 @@
             jax.ShapeDtypeStruct((row_dev, col_dev), BF16),
             jax.ShapeDtypeStruct((8, row_dev), F32),
         ),
-        in_specs=[smem, smem] + [vmem] * 16 + [tiled],
+        in_specs=[smem, smem] + [vmem] * 18 + [tiled],
         out_specs=(tiled, vmem),
         scratch_shapes=[
             pltpu.VMEM((n, row_dev), BF16),
             pltpu.VMEM((row_dev, n), BF16),
             pltpu.VMEM((n, col_dev), BF16),
+            pltpu.VMEM((n, n), BF16),
         ],
         compiler_params=pltpu.CompilerParams(vmem_limit_bytes=48 << 20),
         cost_estimate=pl.CostEstimate(flops=8 << 30, bytes_accessed=24 << 20, transcendentals=0),
-    )(place, pattern, *rows, *first, *second, w, half, regrouped, pivot_loads, trailing)
+    )(place, pattern, *rows, *first, *second, *w_parts, *half_parts, regrouped, pivot_loads, trailing)
 
 
 def per_device(loads, nd_source, panel, trailing, pattern, owner):
@@ -238,24 +317,29 @@
     y, z_lo = col_place // 2, col_place % 2
     mine = panel.T
 
-    pivot = select_root(mine[:, :pivot_size], row_place, root)
-    pivot = ring(pair_up(pivot, z_lo, Z_LO, "col"), Y_SHIFT, "col")
-    w, half = inverse_of(pivot, y)
-
-    arrived = lax.all_to_all(loads, "row", split_axis=1, concat_axis=1, tiled=True)
-    slot = nd_source // row_dev * share_size + (nd_source % row_dev - row_place * share_size)
-    regrouped = jnp.take(arrived, slot, axis=1)
-    regrouped = jnp.pad(regrouped, ((0, 5), (0, 0)))
-    pivot_loads = select_root(regrouped[:, :pivot_size], row_place, root)
-
-    rows = ring(pair_up(mine, z_lo, Z_LO, "col"), Y_SHIFT, "col")
-    moved = lax.ppermute(mine, ("row", "col"), transposed_place())
-    first = ring(pair_up(moved, z_hi, Z_HI, "row"), X_SHIFT, "row")
-    second = [lax.ppermute(piece, "row", CORE) for piece in first]
+    packet = spread(pack(mine, loads, nd_source), row_place, root)
+    head = jnp.concatenate([packet[:24, c * pivot_size : (c + 1) * pivot_size] for c in range(3)], 0)
+    pivot = pair_up(head[:64], z_lo, Z_LO, "col")
+    moved = lax.ppermute(after(mine, packet), ("row", "col"), transposed_place())
+    rows = pair_up(after(mine, packet), z_lo, Z_LO, "col")
+    pivot = ring(pivot, Y_SHIFT, "col")
+    first = pair_up(after(moved, pivot[0]), z_hi, Z_HI, "row")
+    first, rows = after((first, rows), *pivot)
+    first = ring(first, X_SHIFT, "row")
+    rows = ring(rows, Y_SHIFT, "col")
+
+    everyone = packet[24:].reshape(row_count, 8, row_dev)
+    regrouped = regroup(everyone, nd_source, row_place, row_place, share_size)
+    pivot_source = head[64].astype(jnp.int32) * BLOCK + head[65].astype(jnp.int32)
+    pivot_loads = regroup(everyone, pivot_source, row_place, root, share_size)
+
+    w_top, half_top, rest = upper_inverse(pivot, y)
+    second = [lax.ppermute(after(piece, rest), "row", CORE) for piece in first]
+    w_low, half_low = lower_inverse(rest)
 
     place = jnp.stack([x, y, core, (row_place == root).astype(jnp.int32)]).astype(jnp.int32)
     trailing_out, loads_out = update(
-        place, pattern, rows, first, second, w, half, regrouped, pivot_loads, trailing
+        place, pattern, rows, first, second, (w_top, w_low), (half_top, half_low), regrouped, pivot_loads, trailing
     )
     return loads_out[:3], trailing_out
 

time: 141 us -> 110 us (0.78)
  the two profiles are of different devices: /device:TPU:9 before, /device:TPU:1 now
where the time goes in v2:
time: 110 us; the launch traced here: 109 us
  Pallas kernels  42 us (38%)
  starting transfers between devices  34.5 us (31%)
  waiting for transfers between devices  13.8 us (13%)
  local copies, waits for them, and re-layouts  9.57 us (9%)
  between operations  6.2 us (6%)
  other arithmetic  3.07 us (3%)
    pallas_call x1, Pallas kernels, update(): pl.pallas_call(update_kernel, grid=(col_dev // tile,), out_shape=(jax.Sha...  19.9 us
    ppermute x12, starting transfers between devices, ring(): return [mine] + [lax.ppermute(mine, axis, shifts[k]) for k in (1, 2, 3)]  14.9 us
    pallas_call x1, Pallas kernels, upper_inverse(): pl.pallas_call(kernel, out_shape=(jax.ShapeDtypeStruct((n // 2, n), F32),...  11.3 us
    ppermute x12, waiting for transfers between devices, ring(): return [mine] + [lax.ppermute(mine, axis, shifts[k]) for k in (1, 2, 3)]  9.34 us
    pallas_call x1, Pallas kernels, lower_inverse(): pl.pallas_call(lower_kernel, out_shape=(jax.ShapeDtypeStruct((half, n), F...  9.2 us
    ppermute x2, starting transfers between devices, spread(): other = lax.ppermute(packet, 'row', perm)  6.49 us
    ppermute x4, starting transfers between devices, per_device(): second = [lax.ppermute(after(piece, rest), 'row', CORE) for piece in first]  6.2 us
    ppermute x3, starting transfers between devices, pair_up(): other = lax.ppermute(mine, axis, perm)  5.32 us
  transfers between devices with their start and end apart: 22, of which 7 were waited for; matrix products, arithmetic and copies ran while one was open for 9% of the time, Pallas kernels for 19%

profile of v2, /device:TPU:1, one launch (start us, length us, event | category | flops | bytes accessed | tf_op | source)
XLA Modules:
  0.0 109.1 jit_solution(12542623003637638096)
XLA Ops:
  0.6 1.3 %broadcast_in_dim.27.source_ref = s32[1,1536]{1,0:T(1,128)} reshape(s32[1536]{0:T(1024)} %param.7) | data formatting | bytes 12288 | tf_op jit(solution)/shard_map/broadcast_in_dim | solution.py:62
  1.9 1.6 %shard_map.77 = bf16[32,1536]{1,0:T(8,128)(2,1)} custom-call(bf16[64,1536]{1,0:T(8,128)(2,1)} %bitcast.43, f32[3,1536]{1,0:T(4,128)} %loads_ref.1, s32[1,1536]{1,0:T(1,128)} %broadcast_in_dim.27.source_ref), custom_call_target="tpu_custom_call" | custom-call | tf_op jit(solution)/shard_map/pallas_call | solution.py:60
  3.5 3.3 %collective-permute-start.3 = (bf16[32,1536]{1,0:T(8,128)(2,1)}, bf16[32,1536]{1,0:T(8,128)(2,1)S(1)}, u32[]{:S(2)}, u32[]{:S(2)}) collective-permute-start(bf16[32,1536]{1,0:T(8,128)(2,1)} %shard_map.77), channel_id=1, source_target_pairs={{0,96},{8,104},{16,112},{24,120},{32,0},{40,8},{48,16},{56,24},{64... | collective-permute-start | bytes 294920 | tf_op jit(solution)/shard_map/ppermute | solution.py:38
  7.4 0.6 collective-permute-start.1
  8.0 1.6 %collective-permute-start.8 = (bf16[64,1536]{1,0:T(8,128)(2,1)}, bf16[64,1536]{1,0:T(8,128)(2,1)S(1)}, u32[]{:S(2)}, u32[]{:S(2)}) collective-permute-start(bf16[64,1536]{1,0:T(8,128)(2,1)} %bitcast.44), channel_id=1, source_target_pairs={{0,1},{1,0},{2,3},{3,2},{4,5},{5,4},{6,7},{7,6},{8,9},{9,8},{10,11... | collective-permute-start | bytes 589832 | tf_op jit(solution)/shard_map/ppermute | solution.py:31
  9.6 1.6 %collective-permute-start = (bf16[64,1536]{1,0:T(8,128)(2,1)}, bf16[64,1536]{1,0:T(8,128)(2,1)S(1)}, u32[]{:S(2)}, u32[]{:S(2)}) collective-permute-start(bf16[64,1536]{1,0:T(8,128)(2,1)} %bitcast.45), channel_id=1, source_target_pairs={{0,0},{1,16},{2,32},{3,48},{4,64},{5,80},{6,96},{7,112},{8,8},{9,2... | collective-permute-start | bytes 589832 | tf_op jit(solution)/shard_map/ppermute | solution.py:323
  11.2 0.7 compare_and_fusion
  17.2 0.9 constant_dynamic-update-slice_fusion.4
  18.2 0.7 constant_dynamic-update-slice_fusion.3
  18.9 3.7 %collective-permute-start.4 = (bf16[56,1536]{1,0:T(8,128)(2,1)S(1)}, bf16[56,1536]{1,0:T(8,128)(2,1)S(1)}, u32[]{:S(2)}, u32[]{:S(2)}) collective-permute-start(bf16[56,1536]{1,0:T(8,128)(2,1)S(1)} %constant_dynamic-update-slice_fusion), channel_id=1, source_target_pairs={{0,16},{8,24},{16,0},{24,8},{32,48},{40,56},{48,32},{56,40},{64,80... | collective-permute-start | bytes 516104 | tf_op jit(solution)/shard_map/ppermute | solution.py:73
  22.8 2.7 %collective-permute-done.4 = bf16[56,1536]{1,0:T(8,128)(2,1)S(1)} collective-permute-done((bf16[56,1536]{1,0:T(8,128)(2,1)S(1)}, bf16[56,1536]{1,0:T(8,128)(2,1)S(1)}, u32[]{:S(2)}, u32[]{:S(2)}) %collective-permute-start.4) | collective-permute-done | bytes 172064 | tf_op jit(solution)/shard_map/ppermute | solution.py:73
  25.5 0.7 constant_dynamic-update-slice_fusion.13
  26.3 2.7 %collective-permute-start.5 = (bf16[88,1536]{1,0:T(8,128)(2,1)S(1)}, bf16[88,1536]{1,0:T(8,128)(2,1)S(1)}, u32[]{:S(2)}, u32[]{:S(2)}) collective-permute-start(bf16[88,1536]{1,0:T(8,128)(2,1)S(1)} %get-tuple-element.45), channel_id=1, source_target_pairs={{0,8},{8,0},{16,24},{24,16},{32,40},{40,32},{48,56},{56,48},{64,72... | collective-permute-start | bytes 811016 | tf_op jit(solution)/shard_map/ppermute | solution.py:73
  29.0 1.0 broadcast_select_fusion.1
  30.4 3.3 %collective-permute-start.6 = (bf16[64,512]{1,0:T(8,128)(2,1)S(1)}, bf16[64,512]{1,0:T(8,128)(2,1)S(1)}, u32[]{:S(2)}, u32[]{:S(2)}) collective-permute-start(bf16[64,512]{1,0:T(8,128)(2,1)S(1)} %pad_maximum_fusion.3), channel_id=1, source_target_pairs={{0,1},{1,0},{2,3},{3,2},{4,5},{5,4},{6,7},{7,6},{8,9},{9,8},{10,11... | collective-permute-start | bytes 196616 | tf_op jit(solution)/shard_map/ppermute | solution.py:31
  34.0 1.3 %gather_fusion.1 = bf16[512,8]{1,0:T(8,128)(2,1)S(1)} fusion(bf16[8,1536]{0,1:T(8,128)(2,1)S(1)} %bitcast.47, s32[1024]{0:T(1024)S(1)} %pad_clamp_fusion.1), kind=kCustom, calls=%fused_computation.1 | custom fusion | bytes 18432 | tf_op jit(solution)/shard_map/jit(_take)/gather | solution.py:87
  35.7 3.2 %gather_fusion = bf16[1536,8]{1,0:T(8,128)(2,1)S(1)} fusion(bf16[8,1536]{0,1:T(8,128)(2,1)S(1)} %bitcast.42, s32[2048]{0:T(1024)S(1)} %pad_clamp_fusion), kind=kCustom, calls=%fused_computation | custom fusion | bytes 55296 | tf_op jit(solution)/shard_map/jit(_take)/gather | solution.py:87
  39.6 4.8 %collective-permute-start.11 = (bf16[128,512]{1,0:T(8,128)(2,1)S(1)}, bf16[128,512]{1,0:T(8,128)(2,1)S(1)}, u32[]{:S(2)}, u32[]{:S(2)}) collective-permute-start(bf16[128,512]{1,0:T(8,128)(2,1)S(1)} %pad_maximum_fusion.2.p0), channel_id=1, source_target_pairs={{0,6},{1,7},{2,0},{3,1},{4,2},{5,3},{6,4},{7,5},{8,14},{9,15},{10,... | collective-permute-start | bytes 393224 | tf_op jit(solution)/shard_map/ppermute | solution.py:38
  44.4 0.7 collective-permute-start.9
  45.1 1.5 %collective-permute-done.7 = bf16[64,1536]{1,0:T(8,128)(2,1)S(1)} collective-permute-done((bf16[64,1536]{1,0:T(8,128)(2,1)S(1)}, bf16[64,1536]{1,0:T(8,128)(2,1)S(1)}, u32[]{:S(2)}, u32[]{:S(2)}) %collective-permute-start.7) | collective-permute-done | bytes 196640 | tf_op jit(solution)/shard_map/ppermute | solution.py:31
  46.6 2.9 %collective-permute-done.11.p3 = bf16[128,512]{1,0:T(8,128)(2,1)S(1)} collective-permute-done((bf16[128,512]{1,0:T(8,128)(2,1)S(1)}, bf16[128,512]{1,0:T(8,128)(2,1)S(1)}, u32[]{:S(2)}, u32[]{:S(2)}) %collective-permute-start.11) | collective-permute-done | bytes 131104 | tf_op jit(solution)/shard_map/ppermute | solution.py:38
  49.8 3.6 %collective-permute-done.9.p1 = bf16[128,512]{1,0:T(8,128)(2,1)S(1)} collective-permute-done((bf16[128,512]{1,0:T(8,128)(2,1)S(1)}, bf16[128,512]{1,0:T(8,128)(2,1)S(1)}, u32[]{:S(2)}, u32[]{:S(2)}) %collective-permute-start.9) | collective-permute-done | bytes 131104 | tf_op jit(solution)/shard_map/ppermute | solution.py:38
  53.4 3.4 %collective-permute-start.17 = (bf16[128,1536]{1,0:T(8,128)(2,1)S(1)}, bf16[128,1536]{1,0:T(8,128)(2,1)S(1)}, u32[]{:S(2)}, u32[]{:S(2)}) collective-permute-start(bf16[128,1536]{1,0:T(8,128)(2,1)S(1)} %get-tuple-element.20.refs_4_), channel_id=1, source_target_pairs={{0,96},{8,104},{16,112},{24,120},{32,0},{40,8},{48,16},{56,24},{64... | collective-permute-start | bytes 1179656 | tf_op jit(solution)/shard_map/ppermute | solution.py:38
  57.4 11.3 %shard_map.78 = (f32[256,512]{1,0:T(8,128)S(1)}, bf16[256,512]{1,0:T(8,128)(2,1)S(1)}, f32[256,512]{1,0:T(8,128)S(1)}) custom-call(s32[1]{0:T(128)} %bitcast.1.place_ref, bf16[128,512]{1,0:T(8,128)(2,1)S(1)} %pad_maximum_fusion.2.p0, bf16[128,512]{1,0:T(8,128)(2,1)S(1)} %collective-permute-done.9.p1, bf16[128,512]{1,0:T(8,128)(2,1)S(1)} %collective-permute-done.10.p2, ...), custom_call_target="tpu_custom_call" | custom-call | flops 10737418240 | bytes 1048576 | tf_op jit(solution)/shard_map/pallas_call | solution.py:191
  68.8 1.0 collective-permute-start.12
  69.8 4.8 %collective-permute-start.18 = (bf16[128,1536]{1,0:T(8,128)(2,1)S(1)}, bf16[128,1536]{1,0:T(8,128)(2,1)S(1)}, u32[]{:S(2)}, u32[]{:S(2)}) collective-permute-start(bf16[128,1536]{1,0:T(8,128)(2,1)S(1)} %get-tuple-element.20.refs_4_), channel_id=1, source_target_pairs={{0,8},{8,0},{16,24},{24,16},{32,40},{40,32},{48,56},{56,48},{64,72... | collective-permute-start | bytes 1179656 | tf_op jit(solution)/shard_map/ppermute | solution.py:337
  74.6 2.6 %collective-permute-done.15.refs_5_ = bf16[128,1536]{1,0:T(8,128)(2,1)S(1)} collective-permute-done((bf16[128,1536]{1,0:T(8,128)(2,1)S(1)}, bf16[128,1536]{1,0:T(8,128)(2,1)S(1)}, u32[]{:S(2)}, u32[]{:S(2)}) %collective-permute-start.15) | collective-permute-done | bytes 393248 | tf_op jit(solution)/shard_map/ppermute | solution.py:38
  77.2 0.8 collective-permute-start.19
  78.5 9.2 %shard_map.79 = (f32[256,512]{1,0:T(8,128)S(1)}, bf16[256,512]{1,0:T(8,128)(2,1)S(1)}) custom-call(f32[256,512]{1,0:T(8,128)S(1)} %get-tuple-element.19.in_ref), custom_call_target="tpu_custom_call" | custom-call | flops 10737418240 | bytes 1048576 | tf_op jit(solution)/shard_map/pallas_call | solution.py:209
  87.8 0.8 copy-done.1
  88.6 19.9 %shard_map.80 = (bf16[1536,3072]{1,0:T(8,128)(2,1)}, f32[8,1536]{1,0:T(8,128)S(1)}) custom-call(s32[4]{0:T(128)S(1)} %pad_add_fusion.place_ref, s32[12,24]{1,0:T(8,128)S(1)} %copy-done, bf16[128,1536]{1,0:T(8,128)(2,1)S(1)} %get-tuple-element.17.refs_0_, bf16[128,1536]{1,0:T(8,128)(2,1)S(1)} %collective-permute-done.12.refs_1_, ...), custom_call_target="tpu_custom_call" | custom-call | flops 8589934592 | bytes 25165824 | tf_op jit(solution)/shard_map/pallas_call | solution.py:288
  108.5 0.6 slice.103
  (63 shorter events, 3.8 us)
Async XLA Ops:
  3.5 13.7 %collective-permute-start.3 = (bf16[32,1536]{1,0:T(8,128)(2,1)}, bf16[32,1536]{1,0:T(8,128)(2,1)S(1)}, u32[]{:S(2)}, u32[]{:S(2)}) collective-permute-start(bf16[32,1536]{1,0:T(8,128)(2,1)} %shard_map.77), channel_id=1, source_target_pairs={{0,96},{8,104},{16,112},{24,120},{32,0},{40,8},{48,16},{56,24},{64... | collective-permute-start | bytes 294920 | tf_op jit(solution)/shard_map/ppermute | solution.py:38
  6.8 10.4 %collective-permute-start.2 = (bf16[32,1536]{1,0:T(8,128)(2,1)}, bf16[32,1536]{1,0:T(8,128)(2,1)S(1)}, u32[]{:S(2)}, u32[]{:S(2)}) collective-permute-start(bf16[32,1536]{1,0:T(8,128)(2,1)} %shard_map.77), channel_id=1, source_target_pairs={{0,64},{8,72},{16,80},{24,88},{32,96},{40,104},{48,112},{56,120},{... | collective-permute-start | bytes 294920 | tf_op jit(solution)/shard_map/ppermute | solution.py:38
  7.4 9.9 %collective-permute-start.1 = (bf16[32,1536]{1,0:T(8,128)(2,1)}, bf16[32,1536]{1,0:T(8,128)(2,1)S(1)}, u32[]{:S(2)}, u32[]{:S(2)}) collective-permute-start(bf16[32,1536]{1,0:T(8,128)(2,1)} %shard_map.77), channel_id=1, source_target_pairs={{0,32},{8,40},{16,48},{24,56},{32,64},{40,72},{48,80},{56,88},{64,... | collective-permute-start | bytes 294920 | tf_op jit(solution)/shard_map/ppermute | solution.py:38
  8.0 21.1 %collective-permute-start.8 = (bf16[64,1536]{1,0:T(8,128)(2,1)}, bf16[64,1536]{1,0:T(8,128)(2,1)S(1)}, u32[]{:S(2)}, u32[]{:S(2)}) collective-permute-start(bf16[64,1536]{1,0:T(8,128)(2,1)} %bitcast.44), channel_id=1, source_target_pairs={{0,1},{1,0},{2,3},{3,2},{4,5},{5,4},{6,7},{7,6},{8,9},{9,8},{10,11... | collective-permute-start | bytes 589832 | tf_op jit(solution)/shard_map/ppermute | solution.py:31
  9.6 29.6 %collective-permute-start = (bf16[64,1536]{1,0:T(8,128)(2,1)}, bf16[64,1536]{1,0:T(8,128)(2,1)S(1)}, u32[]{:S(2)}, u32[]{:S(2)}) collective-permute-start(bf16[64,1536]{1,0:T(8,128)(2,1)} %bitcast.45), channel_id=1, source_target_pairs={{0,0},{1,16},{2,32},{3,48},{4,64},{5,80},{6,96},{7,112},{8,8},{9,2... | collective-permute-start | bytes 589832 | tf_op jit(solution)/shard_map/ppermute | solution.py:323
  18.9 6.5 %collective-permute-start.4 = (bf16[56,1536]{1,0:T(8,128)(2,1)S(1)}, bf16[56,1536]{1,0:T(8,128)(2,1)S(1)}, u32[]{:S(2)}, u32[]{:S(2)}) collective-permute-start(bf16[56,1536]{1,0:T(8,128)(2,1)S(1)} %constant_dynamic-update-slice_fusion), channel_id=1, source_target_pairs={{0,16},{8,24},{16,0},{24,8},{32,48},{40,56},{48,32},{56,40},{64,80... | collective-permute-start | bytes 516104 | tf_op jit(solution)/shard_map/ppermute | solution.py:73
  26.3 3.9 %collective-permute-start.5 = (bf16[88,1536]{1,0:T(8,128)(2,1)S(1)}, bf16[88,1536]{1,0:T(8,128)(2,1)S(1)}, u32[]{:S(2)}, u32[]{:S(2)}) collective-permute-start(bf16[88,1536]{1,0:T(8,128)(2,1)S(1)} %get-tuple-element.45), channel_id=1, source_target_pairs={{0,8},{8,0},{16,24},{24,16},{32,40},{40,32},{48,56},{56,48},{64,72... | collective-permute-start | bytes 811016 | tf_op jit(solution)/shard_map/ppermute | solution.py:73
  30.4 8.7 %collective-permute-start.6 = (bf16[64,512]{1,0:T(8,128)(2,1)S(1)}, bf16[64,512]{1,0:T(8,128)(2,1)S(1)}, u32[]{:S(2)}, u32[]{:S(2)}) collective-permute-start(bf16[64,512]{1,0:T(8,128)(2,1)S(1)} %pad_maximum_fusion.3), channel_id=1, source_target_pairs={{0,1},{1,0},{2,3},{3,2},{4,5},{5,4},{6,7},{7,6},{8,9},{9,8},{10,11... | collective-permute-start | bytes 196616 | tf_op jit(solution)/shard_map/ppermute | solution.py:31
  39.2 7.4 %collective-permute-start.7 = (bf16[64,1536]{1,0:T(8,128)(2,1)S(1)}, bf16[64,1536]{1,0:T(8,128)(2,1)S(1)}, u32[]{:S(2)}, u32[]{:S(2)}) collective-permute-start(bf16[64,1536]{1,0:T(8,128)(2,1)S(1)} %collective-permute-done), channel_id=1, source_target_pairs={{0,16},{8,24},{16,0},{24,8},{32,48},{40,56},{48,32},{56,40},{64,80... | collective-permute-start | bytes 589832 | tf_op jit(solution)/shard_map/ppermute | solution.py:31
  39.6 10.0 %collective-permute-start.11 = (bf16[128,512]{1,0:T(8,128)(2,1)S(1)}, bf16[128,512]{1,0:T(8,128)(2,1)S(1)}, u32[]{:S(2)}, u32[]{:S(2)}) collective-permute-start(bf16[128,512]{1,0:T(8,128)(2,1)S(1)} %pad_maximum_fusion.2.p0), channel_id=1, source_target_pairs={{0,6},{1,7},{2,0},{3,1},{4,2},{5,3},{6,4},{7,5},{8,14},{9,15},{10,... | collective-permute-start | bytes 393224 | tf_op jit(solution)/shard_map/ppermute | solution.py:38
  44.4 5.4 %collective-permute-start.10 = (bf16[128,512]{1,0:T(8,128)(2,1)S(1)}, bf16[128,512]{1,0:T(8,128)(2,1)S(1)}, u32[]{:S(2)}, u32[]{:S(2)}) collective-permute-start(bf16[128,512]{1,0:T(8,128)(2,1)S(1)} %pad_maximum_fusion.2.p0), channel_id=1, source_target_pairs={{0,4},{1,5},{2,6},{3,7},{4,0},{5,1},{6,2},{7,3},{8,12},{9,13},{10,... | collective-permute-start | bytes 393224 | tf_op jit(solution)/shard_map/ppermute | solution.py:38
  44.4 9.0 %collective-permute-start.9 = (bf16[128,512]{1,0:T(8,128)(2,1)S(1)}, bf16[128,512]{1,0:T(8,128)(2,1)S(1)}, u32[]{:S(2)}, u32[]{:S(2)}) collective-permute-start(bf16[128,512]{1,0:T(8,128)(2,1)S(1)} %pad_maximum_fusion.2.p0), channel_id=1, source_target_pairs={{0,2},{1,3},{2,4},{3,5},{4,6},{5,7},{6,0},{7,1},{8,10},{9,11},{10,... | collective-permute-start | bytes 393224 | tf_op jit(solution)/shard_map/ppermute | solution.py:38
  53.4 24.6 %collective-permute-start.14 = (bf16[128,1536]{1,0:T(8,128)(2,1)S(1)}, bf16[128,1536]{1,0:T(8,128)(2,1)S(1)}, u32[]{:S(2)}, u32[]{:S(2)}) collective-permute-start(bf16[128,1536]{1,0:T(8,128)(2,1)S(1)} %get-tuple-element.17.refs_0_), channel_id=1, source_target_pairs={{0,6},{1,7},{2,0},{3,1},{4,2},{5,3},{6,4},{7,5},{8,14},{9,15},{10,... | collective-permute-start | bytes 1179656 | tf_op jit(solution)/shard_map/ppermute | solution.py:38
  53.4 24.6 %collective-permute-start.13 = (bf16[128,1536]{1,0:T(8,128)(2,1)S(1)}, bf16[128,1536]{1,0:T(8,128)(2,1)S(1)}, u32[]{:S(2)}, u32[]{:S(2)}) collective-permute-start(bf16[128,1536]{1,0:T(8,128)(2,1)S(1)} %get-tuple-element.17.refs_0_), channel_id=1, source_target_pairs={{0,4},{1,5},{2,6},{3,7},{4,0},{5,1},{6,2},{7,3},{8,12},{9,13},{10,... | collective-permute-start | bytes 1179656 | tf_op jit(solution)/shard_map/ppermute | solution.py:38
  53.4 15.3 %collective-permute-start.17 = (bf16[128,1536]{1,0:T(8,128)(2,1)S(1)}, bf16[128,1536]{1,0:T(8,128)(2,1)S(1)}, u32[]{:S(2)}, u32[]{:S(2)}) collective-permute-start(bf16[128,1536]{1,0:T(8,128)(2,1)S(1)} %get-tuple-element.20.refs_4_), channel_id=1, source_target_pairs={{0,96},{8,104},{16,112},{24,120},{32,0},{40,8},{48,16},{56,24},{64... | collective-permute-start | bytes 1179656 | tf_op jit(solution)/shard_map/ppermute | solution.py:38
  56.9 12.9 %collective-permute-start.16 = (bf16[128,1536]{1,0:T(8,128)(2,1)S(1)}, bf16[128,1536]{1,0:T(8,128)(2,1)S(1)}, u32[]{:S(2)}, u32[]{:S(2)}) collective-permute-start(bf16[128,1536]{1,0:T(8,128)(2,1)S(1)} %get-tuple-element.20.refs_4_), channel_id=1, source_target_pairs={{0,64},{8,72},{16,80},{24,88},{32,96},{40,104},{48,112},{56,120},{... | collective-permute-start | bytes 1179656 | tf_op jit(solution)/shard_map/ppermute | solution.py:38
  56.9 20.3 %collective-permute-start.15 = (bf16[128,1536]{1,0:T(8,128)(2,1)S(1)}, bf16[128,1536]{1,0:T(8,128)(2,1)S(1)}, u32[]{:S(2)}, u32[]{:S(2)}) collective-permute-start(bf16[128,1536]{1,0:T(8,128)(2,1)S(1)} %get-tuple-element.20.refs_4_), channel_id=1, source_target_pairs={{0,32},{8,40},{16,48},{24,56},{32,64},{40,72},{48,80},{56,88},{64,... | collective-permute-start | bytes 1179656 | tf_op jit(solution)/shard_map/ppermute | solution.py:38
  68.7 19.8 %copy-start = (s32[12,24]{1,0:T(8,128)S(1)}, s32[12,24]{1,0:T(8,128)}, u32[]{:S(2)}) copy-start(s32[12,24]{1,0:T(8,128)} %pattern_ref.1) | copy-start | bytes 3460
  68.8 19.8 %collective-permute-start.12 = (bf16[128,1536]{1,0:T(8,128)(2,1)S(1)}, bf16[128,1536]{1,0:T(8,128)(2,1)S(1)}, u32[]{:S(2)}, u32[]{:S(2)}) collective-permute-start(bf16[128,1536]{1,0:T(8,128)(2,1)S(1)} %get-tuple-element.17.refs_0_), channel_id=1, source_target_pairs={{0,2},{1,3},{2,4},{3,5},{4,6},{5,7},{6,0},{7,1},{8,10},{9,11},{10,... | collective-permute-start | bytes 1179656 | tf_op jit(solution)/shard_map/ppermute | solution.py:38
  69.8 18.8 %collective-permute-start.18 = (bf16[128,1536]{1,0:T(8,128)(2,1)S(1)}, bf16[128,1536]{1,0:T(8,128)(2,1)S(1)}, u32[]{:S(2)}, u32[]{:S(2)}) collective-permute-start(bf16[128,1536]{1,0:T(8,128)(2,1)S(1)} %get-tuple-element.20.refs_4_), channel_id=1, source_target_pairs={{0,8},{8,0},{16,24},{24,16},{32,40},{40,32},{48,56},{56,48},{64,72... | collective-permute-start | bytes 1179656 | tf_op jit(solution)/shard_map/ppermute | solution.py:337
  77.2 11.4 %collective-permute-start.19 = (bf16[128,1536]{1,0:T(8,128)(2,1)S(1)}, bf16[128,1536]{1,0:T(8,128)(2,1)S(1)}, u32[]{:S(2)}, u32[]{:S(2)}) collective-permute-start(bf16[128,1536]{1,0:T(8,128)(2,1)S(1)} %collective-permute-done.15.refs_5_), channel_id=1, source_target_pairs={{0,8},{8,0},{16,24},{24,16},{32,40},{40,32},{48,56},{56,48},{64,72... | collective-permute-start | bytes 1179656 | tf_op jit(solution)/shard_map/ppermute | solution.py:337
  78.0 10.5 %collective-permute-start.20 = (bf16[128,1536]{1,0:T(8,128)(2,1)S(1)}, bf16[128,1536]{1,0:T(8,128)(2,1)S(1)}, u32[]{:S(2)}, u32[]{:S(2)}) collective-permute-start(bf16[128,1536]{1,0:T(8,128)(2,1)S(1)} %collective-permute-done.16.refs_6_), channel_id=1, source_target_pairs={{0,8},{8,0},{16,24},{24,16},{32,40},{40,32},{48,56},{56,48},{64,72... | collective-permute-start | bytes 1179656 | tf_op jit(solution)/shard_map/ppermute | solution.py:337
  78.0 10.5 %collective-permute-start.21 = (bf16[128,1536]{1,0:T(8,128)(2,1)S(1)}, bf16[128,1536]{1,0:T(8,128)(2,1)S(1)}, u32[]{:S(2)}, u32[]{:S(2)}) collective-permute-start(bf16[128,1536]{1,0:T(8,128)(2,1)S(1)} %collective-permute-done.17.refs_7_), channel_id=1, source_target_pairs={{0,8},{8,0},{16,24},{24,16},{32,40},{40,32},{48,56},{56,48},{64,72... | collective-permute-start | bytes 1179656 | tf_op jit(solution)/shard_map/ppermute | solution.py:337
  87.8 0.8 copy-start.1

commit v3 on v2

v3 whole, which is shorter than its diff:
```python
import jax
import jax.numpy as jnp
from jax import lax
from jax.experimental import pallas as pl
from jax.experimental.pallas import tpu as pltpu
from jax.sharding import PartitionSpec as P

HI = lax.Precision.HIGHEST
F32 = jnp.float32
BF16 = jnp.bfloat16
BLOCK = 128

X_SHIFT = {k: [(i, (i // 4 + k) % 4 * 4 + i % 4) for i in range(16)] for k in (1, 2, 3)}
Y_SHIFT = {k: [(i, (i // 2 + k) % 4 * 2 + i % 2) for i in range(8)] for k in (1, 2, 3)}
Z_HI = [(i, i ^ 2) for i in range(16)]
CORE = [(i, i ^ 1) for i in range(16)]
Z_LO = [(i, i ^ 1) for i in range(8)]


def transposed_place():
    pairs = []
    for row in range(16):
        for col in range(8):
            x, z_hi, core = row // 4, row // 2 % 2, row % 2
            y, z_lo = col // 2, col % 2
            pairs.append((row * 8 + col, ((y * 2 + z_lo) * 2 + core) * 8 + x * 2 + z_hi))
    return pairs


def ring(mine, shifts, axis):
    return [mine] + [lax.ppermute(mine, axis, shifts[k]) for k in (1, 2, 3)]


def pack_kernel(panel_ref, loads_ref, source_ref, out_ref):
    size = out_ref.shape[1] // 3
    source = jnp.concatenate([source_ref[k : k + 1, :] for k in range(size // BLOCK)], 1)
    digits = jnp.concatenate([source // BLOCK, source % BLOCK, jnp.zeros((6, size), jnp.int32)], 0)
    head = jnp.concatenate([panel_ref[:, :size].astype(F32), digits.astype(F32)], 0)
    head = jnp.concatenate([head[24 * c : 24 * c + 24] for c in range(3)], 1)
    loads = loads_ref[...]
    high = loads.astype(BF16).astype(F32)
    low = loads - high
    tail = jnp.concatenate([high, low, jnp.zeros((2, loads.shape[1]), F32)], 0)
    out_ref[...] = jnp.concatenate([head, tail], 0).astype(BF16)


def pack(mine, loads, source):
    return pl.pallas_call(
        pack_kernel,
        out_shape=jax.ShapeDtypeStruct((32, mine.shape[1]), BF16),
        compiler_params=pltpu.CompilerParams(vmem_limit_bytes=4 << 20),
    )(mine, loads, source.reshape(-1, BLOCK))


def small_call(kernel, shapes, scalars, *arrays):
    vmem = pl.BlockSpec(memory_space=pltpu.VMEM)
    return pl.pallas_call(
        kernel,
        out_shape=tuple(jax.ShapeDtypeStruct(shape, BF16) for shape in shapes),
        in_specs=[pl.BlockSpec(memory_space=pltpu.SMEM)] + [vmem] * len(arrays),
        out_specs=(vmem,) * len(shapes),
        compiler_params=pltpu.CompilerParams(vmem_limit_bytes=4 << 20),
    )(scalars, *arrays)


def choose_x(at_ref, p0, p1, p2, p3, out_ref):
    back = ((at_ref[0] >> 2) + 4 - (at_ref[2] >> 2)) & 3
    pieces = [p[...].astype(F32) for p in (p0, p1, p2, p3)]
    head = pieces[0][:24]
    for k in (1, 2, 3):
        head = jnp.where(back == k, pieces[k][:24], head)
    out_ref[...] = jnp.concatenate([head] + [p[24:] for p in pieces], 0).astype(BF16)


def choose_z(at_ref, p0, p1, out_ref):
    own, other = p0[...].astype(F32), p1[...].astype(F32)
    head = jnp.where(((at_ref[0] ^ at_ref[2]) & 2) == 0, own[:24], other[:24])
    out_ref[...] = jnp.concatenate([head, own[24:], other[24:]], 0).astype(BF16)


def choose_core(at_ref, p0, p1, pivot_ref, digits_ref):
    size = pivot_ref.shape[1]
    head = jnp.where(((at_ref[0] ^ at_ref[2]) & 1) == 0, p0[...].astype(F32)[:24], p1[...].astype(F32)[:24])
    head = jnp.concatenate([head[:, c * size : (c + 1) * size] for c in range(3)], 0)
    pivot_ref[...] = head[:64].astype(BF16)
    digits_ref[...] = head[64:].astype(BF16)


def pair_z_lo(at_ref, p0, p1, out_ref):
    own, other = p0[...], p1[...]
    low = (at_ref[1] & 1) == 0
    out_ref[...] = jnp.concatenate([jnp.where(low, own, other), jnp.where(low, other, own)], 0)


def pair_z_hi(at_ref, p0, p1, out_ref):
    own, other = p0[...], p1[...]
    low = (at_ref[0] & 2) == 0
    out_ref[...] = jnp.concatenate([jnp.where(low, own, other), jnp.where(low, other, own)], 0)


def regroup(window_of, source, row_place, target, share):
    arrived = lax.dynamic_slice_in_dim(window_of, target * share, share, 2)
    arrived = arrived.transpose(1, 0, 2).reshape(arrived.shape[1], -1)
    home = lax.div(source, share * 16)
    flip = home ^ row_place
    turn = ((row_place >> 2) + 4 - (home >> 2)) & 3
    place = (flip & 1) * 8 + (flip & 2) * 2 + turn
    slot = (place - home * 16) * share + source - target * share
    parts = jnp.take(arrived, slot, axis=1)
    return jnp.concatenate([parts[:3].astype(F32) + parts[3:6].astype(F32), jnp.zeros((5, slot.shape[0]), F32)], 0)


def block_inverse(rows):
    n = rows[0].shape[1]
    lane = lax.broadcasted_iota(jnp.int32, (8, n), 1)
    sub = lax.broadcasted_iota(jnp.int32, (8, n), 0)
    rows = list(rows)
    out = []
    for g in range(len(rows)):
        p = 8 * g
        below = range(g + 1, len(rows))
        strip = rows[g]
        cols = [jnp.broadcast_to(strip[:, p + k : p + k + 1], (8, n)) for k in range(8)]
        cols_below = {
            i: [jnp.broadcast_to(rows[i][:, p + k : p + k + 1], (8, n)) for k in range(8)] for i in below
        }
        in_block = (lane >= p) & (lane < p + 8)
        for i in below:
            rows[i] = jnp.where(in_block, 0.0, rows[i])
        pivots = None
        for k in range(8):
            d = jnp.broadcast_to(cols[k][k : k + 1, :], (8, n))
            r = 1.0 / d
            pivots = d if k == 0 else jnp.where(sub == k, d, pivots)
            m = jnp.where(sub > k, cols[k] * r, 0.0)
            piv = jnp.where(lane == p + k, 1.0, jnp.broadcast_to(strip[k : k + 1, :], (8, n)))
            strip = jnp.where((lane == p + k) & (sub > k), 0.0, strip) - m * piv
            piv = jnp.where((lane > p + k) & (lane < p + 8), 0.0, piv)
            u = [None] * 8
            for q in range(k + 1, 8):
                u[q] = jnp.broadcast_to(cols[q][k : k + 1, :], (8, n))
                cols[q] = cols[q] - m * u[q]
            for i in below:
                f = cols_below[i][k] * r
                for q in range(k + 1, 8):
                    cols_below[i][q] = cols_below[i][q] - f * u[q]
                rows[i] = rows[i] - f * piv
        s = lax.rsqrt(pivots)
        out.append(jnp.where(lane == sub + p, s, strip * s))
    return out


def eliminate(g_ref, w_ref, half_ref, blocks, first_row):
    n = g_ref.shape[0]
    B = BLOCK
    lane = lax.broadcasted_iota(jnp.int32, (B, n), 1)
    row = lax.broadcasted_iota(jnp.int32, (B, n), 0)
    lane_b = lax.broadcasted_iota(jnp.int32, (B, B), 1)
    row_b = lax.broadcasted_iota(jnp.int32, (B, B), 0)

    def step(k, carry):
        at = pl.multiple_of(k * B, B)
        diag = g_ref[pl.ds(at, B), pl.ds(at, B)]
        wk = jnp.concatenate(block_inverse([diag[8 * i : 8 * i + 8] for i in range(B // 8)]), 0)
        wk = jnp.where(lane_b <= row_b, wk, 0.0)
        here = (lane >= at) & (lane < at + B)
        strip = jnp.where(here, jnp.where(lane == row + at, 1.0, 0.0), g_ref[pl.ds(at, B), :])
        y = jnp.dot(wk, strip, precision=HI, preferred_element_type=F32)
        done = jnp.where(lane <= row + at, y, 0.0)
        to = pl.multiple_of(at - first_row, B)
        w_ref[pl.ds(to, B), :] = done
        half_ref[pl.ds(to, B), :] = done.astype(BF16)
        for j in range(blocks[0] + 1, n // B):

            @pl.when(j > k)
            def _():
                old = jnp.where(here, 0.0, g_ref[j * B : (j + 1) * B, :])
                g_ref[j * B : (j + 1) * B, :] = old - lax.dot_general(
                    y[:, j * B : (j + 1) * B],
                    y,
                    (((0,), (0,)), ((), ())),
                    precision=HI,
                    preferred_element_type=F32,
                )

        return carry

    lax.fori_loop(*blocks, step, 0)


def upper_kernel(at_ref, p0, p1, p2, p3, w_ref, half_ref, g_ref):
    for k, piece in enumerate((p0, p1, p2, p3)):
        at = pl.multiple_of((((at_ref[1] >> 1) + 4 - k) & 3) * BLOCK, BLOCK)
        g_ref[pl.ds(at, BLOCK), :] = piece[...].astype(F32)
    whole = g_ref[...]
    g_ref[...] = 0.5 * (whole + whole.T)
    eliminate(g_ref, w_ref, half_ref, (0, 2), 0)


def lower_kernel(in_ref, w_ref, half_ref, g_ref):
    g_ref[in_ref.shape[0] :, :] = in_ref[...]
    eliminate(g_ref, w_ref, half_ref, (2, 4), 2 * BLOCK)


def upper_inverse(pieces, at):
    n = pieces[0].shape[1]
    vmem = pl.BlockSpec(memory_space=pltpu.VMEM)

    def kernel(at_ref, p0, p1, p2, p3, w_ref, half_ref, rest_ref, g_ref):
        upper_kernel(at_ref, p0, p1, p2, p3, w_ref, half_ref, g_ref)
        rest_ref[...] = g_ref[n // 2 :, :]

    return pl.pallas_call(
        kernel,
        out_shape=(
            jax.ShapeDtypeStruct((n // 2, n), F32),
            jax.ShapeDtypeStruct((n // 2, n), BF16),
            jax.ShapeDtypeStruct((n // 2, n), F32),
        ),
        in_specs=[pl.BlockSpec(memory_space=pltpu.SMEM)] + [vmem] * 4,
        out_specs=(vmem,) * 3,
        scratch_shapes=[pltpu.VMEM((n, n), F32)],
        compiler_params=pltpu.CompilerParams(vmem_limit_bytes=8 << 20),
        cost_estimate=pl.CostEstimate(flops=10 << 30, bytes_accessed=4 * n * n, transcendentals=0),
    )(at, *pieces)


def lower_inverse(rest):
    half, n = rest.shape
    vmem = pl.BlockSpec(memory_space=pltpu.VMEM)
    return pl.pallas_call(
        lower_kernel,
        out_shape=(jax.ShapeDtypeStruct((half, n), F32), jax.ShapeDtypeStruct((half, n), BF16)),
        in_specs=[vmem],
        out_specs=(vmem,) * 2,
        scratch_shapes=[pltpu.VMEM((n, n), F32)],
        compiler_params=pltpu.CompilerParams(vmem_limit_bytes=8 << 20),
        cost_estimate=pl.CostEstimate(flops=10 << 30, bytes_accessed=4 * n * n, transcendentals=0),
    )(rest)


def update_kernel(at_ref, pattern_ref, *refs):
    rows_in, first_in, second_in = refs[0:4], refs[4:8], refs[8:12]
    w_top, w_low, half_top, half_low, loads_ref, pivot_ref, trailing_ref, out_ref, loads_out_ref = refs[12:21]
    factor_ref, other_ref, half_ref, new_ref, list_ref, sems = refs[21:27]
    raw_refs = refs[27:30]
    n = half_ref.shape[0]
    row_dev, col_dev = trailing_ref.shape
    x, y, core = at_ref[0] >> 2, at_ref[1] >> 1, at_ref[0] & 1

    def copy(source, s):
        at = pl.ds(pl.multiple_of(s * BLOCK, BLOCK), BLOCK)
        return pltpu.make_async_copy(source.at[at, :], out_ref.at[at, :], sems.at[s])

    def sort_strip(s, count):
        filled = pattern_ref[s, 0]
        for j in range(1, col_dev // BLOCK):
            filled = filled | pattern_ref[s, j]

        @pl.when(filled != 0)
        def _():
            list_ref[count] = s

        @pl.when(filled == 0)
        def _():
            copy(trailing_ref, s).start()

        return count + (filled != 0).astype(jnp.int32)

    count = lax.fori_loop(0, row_dev // BLOCK, sort_strip, 0)
    half_ref[: n // 2, :] = half_top[...]
    half_ref[n // 2 :, :] = half_low[...]

    def assemble(raw_ref, pieces, spot):
        for k, piece in enumerate(pieces):
            at = pl.multiple_of(((spot + 4 - k) & 3) * BLOCK, BLOCK)
            raw_ref[pl.ds(at, BLOCK), :] = piece[...]

    assemble(raw_refs[0], rows_in, y)
    assemble(raw_refs[1], first_in, x)
    assemble(raw_refs[2], second_in, x)
    for c in range(0, row_dev, 512):
        part = lax.dot_general(
            raw_refs[0][:, c : c + 512], half_ref[...], (((0,), (1,)), ((), ())), preferred_element_type=F32
        )
        factor_ref[c : c + 512, :] = part.astype(BF16)
    for raw_ref, column in ((raw_refs[1], core * row_dev), (raw_refs[2], (1 - core) * row_dev)):
        for c in range(0, row_dev, 512):
            part = jnp.dot(half_ref[...], raw_ref[:, c : c + 512], preferred_element_type=F32).astype(BF16)
            other_ref[:, pl.ds(pl.multiple_of(column + c, 128), 512)] = part

    TILE = 512

    def strip_at(s):
        return pl.ds(pl.multiple_of(s * BLOCK, BLOCK), BLOCK)

    def pair_step(p, carry):
        last = 2 * p + 1 < count
        pair = (list_ref[2 * p], list_ref[jnp.where(last, 2 * p + 1, 2 * p)])
        left = jnp.concatenate([factor_ref[strip_at(s), :] for s in pair], 0)
        for t in range(0, col_dev, TILE):
            product = jnp.dot(left, other_ref[:, t : t + TILE], preferred_element_type=F32)
            for i, s in enumerate(pair):
                for j in range(0, TILE, BLOCK):
                    flag = pattern_ref[s, (t + j) // BLOCK].astype(F32)
                    old = trailing_ref[strip_at(s), t + j : t + j + BLOCK].astype(F32)
                    new = old - product[i * BLOCK : (i + 1) * BLOCK, j : j + BLOCK] * flag
                    new_ref[strip_at(s), t + j : t + j + BLOCK] = new.astype(BF16)
        copy(new_ref, pair[0]).start()

        @pl.when(last)
        def _():
            copy(new_ref, pair[1]).start()

        return carry

    lax.fori_loop(0, (count + 1) // 2, pair_step, 0)

    solve = jnp.concatenate(
        [
            lax.dot_general(
                pivot_ref[...], w[...], (((1,), (1,)), ((), ())), precision=HI, preferred_element_type=F32
            )
            for w in (w_top, w_low)
        ],
        1,
    )
    one = solve.astype(BF16)
    rest = solve - one.astype(F32)
    two = rest.astype(BF16)
    three = (rest - two.astype(F32)).astype(BF16)
    parts = jnp.concatenate([p.astype(F32) for p in (one, two, three)], 0).astype(BF16)
    change = lax.dot_general(parts, factor_ref[...], (((1,), (1,)), ((), ())), preferred_element_type=F32)
    loads_out_ref[...] = (loads_ref[...] - (change[:8] + change[8:16] + change[16:24]))[:3]

    @pl.when(at_ref[0] == at_ref[2])
    def _():
        loads_out_ref[:, :n] = solve[:3]

    lax.fori_loop(0, row_dev // BLOCK, lambda s, c: (copy(new_ref, s).wait(), c)[1], 0)


def update(at, pattern, rows, first, second, w_parts, half_parts, regrouped, pivot_loads, trailing):
    row_dev, col_dev = trailing.shape
    n = half_parts[0].shape[1]
    smem = pl.BlockSpec(memory_space=pltpu.SMEM)
    vmem = pl.BlockSpec(memory_space=pltpu.VMEM)
    return pl.pallas_call(
        update_kernel,
        out_shape=(
            jax.ShapeDtypeStruct((row_dev, col_dev), BF16),
            jax.ShapeDtypeStruct((3, row_dev), F32),
        ),
        in_specs=[smem, smem] + [vmem] * 19,
        out_specs=(pl.BlockSpec(memory_space=pl.ANY), vmem),
        scratch_shapes=[
            pltpu.VMEM((row_dev, n), BF16),
            pltpu.VMEM((n, col_dev), BF16),
            pltpu.VMEM((n, n), BF16),
            pltpu.VMEM((row_dev, col_dev), BF16),
            pltpu.SMEM((row_dev // BLOCK,), jnp.int32),
            pltpu.SemaphoreType.DMA((row_dev // BLOCK,)),
        ]
        + [pltpu.VMEM((n, row_dev), BF16)] * 3,
        compiler_params=pltpu.CompilerParams(vmem_limit_bytes=28 << 20),
        cost_estimate=pl.CostEstimate(flops=8 << 30, bytes_accessed=24 << 20, transcendentals=0),
    )(at, pattern, *rows, *first, *second, *w_parts, *half_parts, regrouped, pivot_loads, trailing)


def per_device(loads, nd_source, panel, trailing, pattern, owner):
    row_dev = panel.shape[0]
    row_count = lax.axis_size("row")
    slice_width = panel.shape[1]
    pivot_size = slice_width * lax.axis_size("col")
    share_size = row_dev // row_count
    row_place = lax.axis_index("row")
    root = owner[0]
    at = jnp.stack([row_place, lax.axis_index("col"), root])
    mine = panel.T
    both = lax.optimization_barrier

    packets = ring(pack(mine, loads, nd_source), X_SHIFT, "row")
    rows_other = lax.ppermute(mine, "col", Z_LO)
    (packet,) = small_call(choose_x, [(56, row_dev)], at, *packets)
    packet, moving = both((packet, mine))
    packet_other = lax.ppermute(packet, "row", Z_HI)
    moved = lax.ppermute(moving, ("row", "col"), transposed_place())
    (packet,) = small_call(choose_z, [(88, row_dev)], at, packet, packet_other)
    packet_other = lax.ppermute(packet, "row", CORE)
    pivot, digits = small_call(
        choose_core, [(slice_width, pivot_size), (8, pivot_size)], at, packet, packet_other
    )
    pivot, moved = both((pivot, moved))
    pivot_other = lax.ppermute(pivot, "col", Z_LO)
    moved_other = lax.ppermute(moved, "row", Z_HI)
    (pivot,) = small_call(pair_z_lo, [(2 * slice_width, pivot_size)], at, pivot, pivot_other)
    (rows,) = small_call(pair_z_lo, [(2 * slice_width, row_dev)], at, mine, rows_other)
    pivot = ring(pivot, Y_SHIFT, "col")
    (first,) = small_call(pair_z_hi, [(2 * slice_width, row_dev)], at, moved, moved_other)
    first = ring(first, X_SHIFT, "row")
    pivot, rows = both((pivot, rows))
    rows = ring(rows, Y_SHIFT, "col")

    w_top, half_top, rest = upper_inverse(pivot, at)
    rest, first, packet, packet_other = both((rest, first, packet, packet_other))
    second = [lax.ppermute(piece, "row", CORE) for piece in first]

    everyone = jnp.concatenate([packet[24:], packet_other[24:]], 0).reshape(row_count, 8, row_dev)
    regrouped = regroup(everyone, nd_source, row_place, row_place, share_size)
    pivot_source = digits[0].astype(jnp.int32) * BLOCK + digits[1].astype(jnp.int32)
    pivot_loads = regroup(everyone, pivot_source, row_place, root, share_size)

    rest, regrouped, pivot_loads = both((rest, regrouped, pivot_loads))
    w_low, half_low = lower_inverse(rest)
    trailing_out, loads_out = update(
        at, pattern, rows, first, second, (w_top, w_low), (half_top, half_low), regrouped, pivot_loads, trailing
    )
    return loads_out, trailing_out


def solution(mesh):
    return jax.shard_map(
        per_device,
        mesh=mesh,
        in_specs=(P(None, "row"), P("row"), P("row", "col"), P("row", "col"), P("row", "col"), P()),
        out_specs=(P(None, "row"), P("row", "col")),
        check_vma=False,
    )
```

time: 110 us -> 96.8 us (0.88)
  the two profiles are of different devices: /device:TPU:1 before, /device:TPU:16 now
where the time goes in v3:
time: 96.8 us; the launch traced here: 96.1 us
  Pallas kernels  33 us (34%)
  starting transfers between devices  29.1 us (30%)
  waiting for transfers between devices  16.1 us (17%)
  local copies, waits for them, and re-layouts  14.4 us (15%)
  between operations  1.85 us (2%)
  other arithmetic  1.58 us (2%)
    ppermute x12, starting transfers between devices, ring(): return [mine] + [lax.ppermute(mine, axis, shifts[k]) for k in (1, 2, 3)]  17.7 us
    pallas_call x1, Pallas kernels, upper_inverse(): pl.pallas_call(kernel, out_shape=(jax.ShapeDtypeStruct((n // 2, n), F32),...  11.9 us
    pallas_call x1, Pallas kernels, lower_inverse(): pl.pallas_call(lower_kernel, out_shape=(jax.ShapeDtypeStruct((half, n), F...  9.21 us
    pallas_call x1, Pallas kernels, update(): pl.pallas_call(update_kernel, out_shape=(jax.ShapeDtypeStruct((row_dev, c...  8.51 us
    ppermute x12, waiting for transfers between devices, ring(): return [mine] + [lax.ppermute(mine, axis, shifts[k]) for k in (1, 2, 3)]  7.78 us
    unnamed x28, local copies, waits for them, and re-layouts  7.21 us
    gather x4, local copies, waits for them, and re-layouts, regroup(): parts = jnp.take(arrived, slot, axis=1)  6.58 us
    ppermute x1, starting transfers between devices, per_device(): packet_other = lax.ppermute(packet, 'row', Z_HI)  3.96 us
  transfers between devices with their start and end apart: 22, of which 10 were waited for; matrix products, arithmetic and copies ran while one was open for 9% of the time, Pallas kernels for 25%

profile of v3, /device:TPU:16, one launch (start us, length us, event | category | flops | bytes accessed | tf_op | source)
XLA Modules:
  0.0 96.1 jit_solution(10146341395267544222)
XLA Ops:
  0.6 0.9 copy-done
  2.3 0.7 copy-done.3
  3.0 2.8 %collective-permute-start.2 = (bf16[32,1536]{1,0:T(8,128)(2,1)S(1)}, bf16[32,1536]{1,0:T(8,128)(2,1)S(1)}, u32[]{:S(2)}, u32[]{:S(2)}) collective-permute-start(bf16[32,1536]{1,0:T(8,128)(2,1)S(1)} %shard_map.77.p0), channel_id=1, source_target_pairs={{0,96},{8,104},{16,112},{24,120},{32,0},{40,8},{48,16},{56,24},{64... | collective-permute-start | bytes 294920 | tf_op jit(solution)/shard_map/ppermute | solution.py:31
  5.9 0.8 collective-permute-start.1
  6.7 0.9 collective-permute-start
  8.3 1.8 %collective-permute-done.2.p3 = bf16[32,1536]{1,0:T(8,128)(2,1)S(1)} collective-permute-done((bf16[32,1536]{1,0:T(8,128)(2,1)S(1)}, bf16[32,1536]{1,0:T(8,128)(2,1)S(1)}, u32[]{:S(2)}, u32[]{:S(2)}) %collective-permute-start.2) | collective-permute-done | bytes 98336 | tf_op jit(solution)/shard_map/ppermute | solution.py:31
  10.1 2.7 %collective-permute-done.1.p2 = bf16[32,1536]{1,0:T(8,128)(2,1)S(1)} collective-permute-done((bf16[32,1536]{1,0:T(8,128)(2,1)S(1)}, bf16[32,1536]{1,0:T(8,128)(2,1)S(1)}, u32[]{:S(2)}, u32[]{:S(2)}) %collective-permute-start.1) | collective-permute-done | bytes 98336 | tf_op jit(solution)/shard_map/ppermute | solution.py:31
  12.7 1.0 %collective-permute-done.p1 = bf16[32,1536]{1,0:T(8,128)(2,1)S(1)} collective-permute-done((bf16[32,1536]{1,0:T(8,128)(2,1)S(1)}, bf16[32,1536]{1,0:T(8,128)(2,1)S(1)}, u32[]{:S(2)}, u32[]{:S(2)}) %collective-permute-start) | collective-permute-done | bytes 98336 | tf_op jit(solution)/shard_map/ppermute | solution.py:31
  14.3 4.0 %collective-permute-start.3 = (bf16[56,1536]{1,0:T(8,128)(2,1)S(1)}, bf16[56,1536]{1,0:T(8,128)(2,1)S(1)}, u32[]{:S(2)}, u32[]{:S(2)}) collective-permute-start(bf16[56,1536]{1,0:T(8,128)(2,1)S(1)} %shard_map.78.p0), channel_id=1, source_target_pairs={{0,16},{8,24},{16,0},{24,8},{32,48},{40,56},{48,32},{56,40},{64,80... | collective-permute-start | bytes 516104 | tf_op jit(solution)/shard_map/ppermute | solution.py:386
  18.3 1.0 %collective-permute-start.10 = (bf16[64,1536]{1,0:T(8,128)(2,1)}, bf16[64,1536]{1,0:T(8,128)(2,1)S(1)}, u32[]{:S(2)}, u32[]{:S(2)}) collective-permute-start(bf16[64,1536]{1,0:T(8,128)(2,1)} %bitcast.29), channel_id=1, source_target_pairs={{0,1},{1,0},{2,3},{3,2},{4,5},{5,4},{6,7},{7,6},{8,9},{9,8},{10,11... | collective-permute-start | bytes 589832 | tf_op jit(solution)/shard_map/ppermute | solution.py:383
  19.3 2.5 %collective-permute-start.5 = (bf16[64,1536]{1,0:T(8,128)(2,1)}, bf16[64,1536]{1,0:T(8,128)(2,1)S(1)}, u32[]{:S(2)}, u32[]{:S(2)}) collective-permute-start(bf16[64,1536]{1,0:T(8,128)(2,1)} %bitcast.30), channel_id=1, source_target_pairs={{0,0},{1,16},{2,32},{3,48},{4,64},{5,80},{6,96},{7,112},{8,8},{9,2... | collective-permute-start | bytes 589832 | tf_op jit(solution)/shard_map/ppermute | solution.py:387
  21.8 1.8 %collective-permute-done.3.p1 = bf16[56,1536]{1,0:T(8,128)(2,1)S(1)} collective-permute-done((bf16[56,1536]{1,0:T(8,128)(2,1)S(1)}, bf16[56,1536]{1,0:T(8,128)(2,1)S(1)}, u32[]{:S(2)}, u32[]{:S(2)}) %collective-permute-start.3) | collective-permute-done | bytes 172064 | tf_op jit(solution)/shard_map/ppermute | solution.py:386
  25.6 1.6 %collective-permute-done.10.p1 = bf16[64,1536]{1,0:T(8,128)(2,1)S(1)} collective-permute-done((bf16[64,1536]{1,0:T(8,128)(2,1)}, bf16[64,1536]{1,0:T(8,128)(2,1)S(1)}, u32[]{:S(2)}, u32[]{:S(2)}) %collective-permute-start.10) | collective-permute-done | bytes 196640 | tf_op jit(solution)/shard_map/ppermute | solution.py:383
  27.2 0.9 copy-done.1
  29.3 2.8 %collective-permute-done.5.p0 = bf16[64,1536]{1,0:T(8,128)(2,1)S(1)} collective-permute-done((bf16[64,1536]{1,0:T(8,128)(2,1)}, bf16[64,1536]{1,0:T(8,128)(2,1)S(1)}, u32[]{:S(2)}, u32[]{:S(2)}) %collective-permute-start.5) | collective-permute-done | bytes 196640 | tf_op jit(solution)/shard_map/ppermute | solution.py:387
  32.1 1.9 %collective-permute-start.6 = (bf16[64,512]{1,0:T(8,128)(2,1)S(1)}, bf16[64,512]{1,0:T(8,128)(2,1)S(1)}, u32[]{:S(2)}, u32[]{:S(2)}) collective-permute-start(bf16[64,512]{1,0:T(8,128)(2,1)S(1)} %get-tuple-element.33.p0), channel_id=1, source_target_pairs={{0,1},{1,0},{2,3},{3,2},{4,5},{5,4},{6,7},{7,6},{8,9},{9,8},{10,11... | collective-permute-start | bytes 196616 | tf_op jit(solution)/shard_map/ppermute | solution.py:394
  34.0 0.8 collective-permute-start.14
  34.8 2.2 %collective-permute-done.6.p1 = bf16[64,512]{1,0:T(8,128)(2,1)S(1)} collective-permute-done((bf16[64,512]{1,0:T(8,128)(2,1)S(1)}, bf16[64,512]{1,0:T(8,128)(2,1)S(1)}, u32[]{:S(2)}, u32[]{:S(2)}) %collective-permute-start.6) | collective-permute-done | bytes 65568 | tf_op jit(solution)/shard_map/ppermute | solution.py:394
  37.6 5.9 %collective-permute-start.8 = (bf16[128,512]{1,0:T(8,128)(2,1)S(1)}, bf16[128,512]{1,0:T(8,128)(2,1)S(1)}, u32[]{:S(2)}, u32[]{:S(2)}) collective-permute-start(bf16[128,512]{1,0:T(8,128)(2,1)S(1)} %shard_map.81.p0), channel_id=1, source_target_pairs={{0,4},{1,5},{2,6},{3,7},{4,0},{5,1},{6,2},{7,3},{8,12},{9,13},{10,... | collective-permute-start | bytes 393224 | tf_op jit(solution)/shard_map/ppermute | solution.py:31
  44.4 1.9 %collective-permute-start.15 = (bf16[128,1536]{1,0:T(8,128)(2,1)S(1)}, bf16[128,1536]{1,0:T(8,128)(2,1)S(1)}, u32[]{:S(2)}, u32[]{:S(2)}) collective-permute-start(bf16[128,1536]{1,0:T(8,128)(2,1)S(1)} %shard_map.84.refs_4_), channel_id=1, source_target_pairs={{0,32},{8,40},{16,48},{24,56},{32,64},{40,72},{48,80},{56,88},{64,... | collective-permute-start | bytes 1179656 | tf_op jit(solution)/shard_map/ppermute | solution.py:31
  46.5 2.0 %collective-permute-done.7.p1 = bf16[128,512]{1,0:T(8,128)(2,1)S(1)} collective-permute-done((bf16[128,512]{1,0:T(8,128)(2,1)S(1)}, bf16[128,512]{1,0:T(8,128)(2,1)S(1)}, u32[]{:S(2)}, u32[]{:S(2)}) %collective-permute-start.7) | collective-permute-done | bytes 131104 | tf_op jit(solution)/shard_map/ppermute | solution.py:31
  48.5 3.5 %collective-permute-start.12 = (bf16[128,1536]{1,0:T(8,128)(2,1)S(1)}, bf16[128,1536]{1,0:T(8,128)(2,1)S(1)}, u32[]{:S(2)}, u32[]{:S(2)}) collective-permute-start(bf16[128,1536]{1,0:T(8,128)(2,1)S(1)} %shard_map.82.refs_0_), channel_id=1, source_target_pairs={{0,4},{1,5},{2,6},{3,7},{4,0},{5,1},{6,2},{7,3},{8,12},{9,13},{10,... | collective-permute-start | bytes 1179656 | tf_op jit(solution)/shard_map/ppermute | solution.py:31
  52.0 11.9 %shard_map.83 = (f32[256,512]{1,0:T(8,128)S(1)}, bf16[256,512]{1,0:T(8,128)(2,1)S(1)}, f32[256,512]{1,0:T(8,128)S(1)}) custom-call(s32[3]{0:T(128)S(1)} %pad_add_fusion.at_ref, bf16[128,512]{1,0:T(8,128)(2,1)S(1)} %shard_map.81.p0, bf16[128,512]{1,0:T(8,128)(2,1)S(1)} %collective-permute-done.7.p1, bf16[128,512]{1,0:T(8,128)(2,1)S(1)} %collective-permute-done.8.p2, ...), custom_call_target="tpu_custom_call" | custom-call | flops 10737418240 | bytes 1048576 | tf_op jit(solution)/shard_map/pallas_call | solution.py:213
  63.9 0.8 copy-done.5
  65.4 0.8 copy-done.9
  66.2 1.7 %collective-permute-start.11 = (bf16[128,1536]{1,0:T(8,128)(2,1)S(1)}, bf16[128,1536]{1,0:T(8,128)(2,1)}, u32[]{:S(2)}, u32[]{:S(2)}) collective-permute-start(bf16[128,1536]{1,0:T(8,128)(2,1)S(1)} %shard_map.82.refs_0_), channel_id=1, source_target_pairs={{0,2},{1,3},{2,4},{3,5},{4,6},{5,7},{6,0},{7,1},{8,10},{9,11},{10,... | collective-permute-start | bytes 1179656 | tf_op jit(solution)/shard_map/ppermute | solution.py:31
  68.4 1.3 %gather_fusion.1 = bf16[512,8]{1,0:T(8,128)(2,1)S(1)} fusion(bf16[8,1536]{0,1:T(8,128)(2,1)S(1)} %bitcast.37, s32[1024]{0:T(1024)S(1)} %pad_clamp_fusion.1), kind=kCustom, calls=%fused_computation.1 | custom fusion | bytes 18432 | tf_op jit(solution)/shard_map/jit(_take)/gather | solution.py:109
  70.0 4.0 %gather_fusion = bf16[1536,8]{1,0:T(8,128)(2,1)} fusion(bf16[8,1536]{0,1:T(8,128)(2,1)S(1)} %bitcast.36, s32[2048]{0:T(1024)S(1)} %pad_clamp_fusion), kind=kCustom, calls=%fused_computation | custom fusion | bytes 55296 | tf_op jit(solution)/shard_map/jit(_take)/gather | solution.py:109
  74.1 1.1 %copy.13 = bf16[1536,8]{0,1:T(8,128)(2,1)S(1)} copy(bf16[1536,8]{1,0:T(8,128)(2,1)} %gather_fusion) | data formatting | bytes 49152 | tf_op jit(solution)/shard_map/jit(_take)/gather | solution.py:109
  76.5 1.6 %copy-done.10 = f32[256,512]{1,0:T(8,128)S(1)} copy-done((f32[256,512]{1,0:T(8,128)S(1)}, f32[256,512]{1,0:T(8,128)}, u32[]{:S(2)}) %copy-start.10) | copy-done | bytes 524312
  78.0 9.2 %shard_map.85 = (f32[256,512]{1,0:T(8,128)S(1)}, bf16[256,512]{1,0:T(8,128)(2,1)S(1)}) custom-call(f32[256,512]{1,0:T(8,128)S(1)} %copy-done.10), custom_call_target="tpu_custom_call" | custom-call | flops 10737418240 | bytes 1048576 | tf_op jit(solution)/shard_map/pallas_call | solution.py:231
  87.4 8.5 %shard_map.86 = (bf16[1536,3072]{1,0:T(8,128)(2,1)}, f32[3,1536]{1,0:T(4,128)}) custom-call(s32[3]{0:T(128)S(1)} %pad_add_fusion.at_ref, s32[12,24]{1,0:T(8,128)S(1)} %copy-done.4, bf16[128,1536]{1,0:T(8,128)(2,1)S(1)} %shard_map.82.refs_0_, bf16[128,1536]{1,0:T(8,128)(2,1)} %collective-permute-done.11.refs_1_, ...), custom_call_target="tpu_custom_call" | custom-call | flops 8589934592 | bytes 25165824 | tf_op jit(solution)/shard_map/pallas_call | solution.py:348
  (73 shorter events, 8.9 us)
Async XLA Ops:
  0.6 0.9 copy-start
  3.0 7.0 %collective-permute-start.2 = (bf16[32,1536]{1,0:T(8,128)(2,1)S(1)}, bf16[32,1536]{1,0:T(8,128)(2,1)S(1)}, u32[]{:S(2)}, u32[]{:S(2)}) collective-permute-start(bf16[32,1536]{1,0:T(8,128)(2,1)S(1)} %shard_map.77.p0), channel_id=1, source_target_pairs={{0,96},{8,104},{16,112},{24,120},{32,0},{40,8},{48,16},{56,24},{64... | collective-permute-start | bytes 294920 | tf_op jit(solution)/shard_map/ppermute | solution.py:31
  5.9 6.9 %collective-permute-start.1 = (bf16[32,1536]{1,0:T(8,128)(2,1)S(1)}, bf16[32,1536]{1,0:T(8,128)(2,1)S(1)}, u32[]{:S(2)}, u32[]{:S(2)}) collective-permute-start(bf16[32,1536]{1,0:T(8,128)(2,1)S(1)} %shard_map.77.p0), channel_id=1, source_target_pairs={{0,64},{8,72},{16,80},{24,88},{32,96},{40,104},{48,112},{56,120},{... | collective-permute-start | bytes 294920 | tf_op jit(solution)/shard_map/ppermute | solution.py:31
  6.7 7.1 %collective-permute-start = (bf16[32,1536]{1,0:T(8,128)(2,1)S(1)}, bf16[32,1536]{1,0:T(8,128)(2,1)S(1)}, u32[]{:S(2)}, u32[]{:S(2)}) collective-permute-start(bf16[32,1536]{1,0:T(8,128)(2,1)S(1)} %shard_map.77.p0), channel_id=1, source_target_pairs={{0,32},{8,40},{16,48},{24,56},{32,64},{40,72},{48,80},{56,88},{64,... | collective-permute-start | bytes 294920 | tf_op jit(solution)/shard_map/ppermute | solution.py:31
  14.3 9.2 %collective-permute-start.3 = (bf16[56,1536]{1,0:T(8,128)(2,1)S(1)}, bf16[56,1536]{1,0:T(8,128)(2,1)S(1)}, u32[]{:S(2)}, u32[]{:S(2)}) collective-permute-start(bf16[56,1536]{1,0:T(8,128)(2,1)S(1)} %shard_map.78.p0), channel_id=1, source_target_pairs={{0,16},{8,24},{16,0},{24,8},{32,48},{40,56},{48,32},{56,40},{64,80... | collective-permute-start | bytes 516104 | tf_op jit(solution)/shard_map/ppermute | solution.py:386
  18.3 8.9 %collective-permute-start.10 = (bf16[64,1536]{1,0:T(8,128)(2,1)}, bf16[64,1536]{1,0:T(8,128)(2,1)S(1)}, u32[]{:S(2)}, u32[]{:S(2)}) collective-permute-start(bf16[64,1536]{1,0:T(8,128)(2,1)} %bitcast.29), channel_id=1, source_target_pairs={{0,1},{1,0},{2,3},{3,2},{4,5},{5,4},{6,7},{7,6},{8,9},{9,8},{10,11... | collective-permute-start | bytes 589832 | tf_op jit(solution)/shard_map/ppermute | solution.py:383
  19.3 12.8 %collective-permute-start.5 = (bf16[64,1536]{1,0:T(8,128)(2,1)}, bf16[64,1536]{1,0:T(8,128)(2,1)S(1)}, u32[]{:S(2)}, u32[]{:S(2)}) collective-permute-start(bf16[64,1536]{1,0:T(8,128)(2,1)} %bitcast.30), channel_id=1, source_target_pairs={{0,0},{1,16},{2,32},{3,48},{4,64},{5,80},{6,96},{7,112},{8,8},{9,2... | collective-permute-start | bytes 589832 | tf_op jit(solution)/shard_map/ppermute | solution.py:387
  24.1 4.6 %collective-permute-start.4 = (bf16[88,1536]{1,0:T(8,128)(2,1)S(1)}, bf16[88,1536]{1,0:T(8,128)(2,1)S(1)}, u32[]{:S(2)}, u32[]{:S(2)}) collective-permute-start(bf16[88,1536]{1,0:T(8,128)(2,1)S(1)} %shard_map.79.p0), channel_id=1, source_target_pairs={{0,8},{8,0},{16,24},{24,16},{32,40},{40,32},{48,56},{56,48},{64,72... | collective-permute-start | bytes 811016 | tf_op jit(solution)/shard_map/ppermute | solution.py:389
  27.2 0.9 copy-start.1
  32.1 4.9 %collective-permute-start.6 = (bf16[64,512]{1,0:T(8,128)(2,1)S(1)}, bf16[64,512]{1,0:T(8,128)(2,1)S(1)}, u32[]{:S(2)}, u32[]{:S(2)}) collective-permute-start(bf16[64,512]{1,0:T(8,128)(2,1)S(1)} %get-tuple-element.33.p0), channel_id=1, source_target_pairs={{0,1},{1,0},{2,3},{3,2},{4,5},{5,4},{6,7},{7,6},{8,9},{9,8},{10,11... | collective-permute-start | bytes 196616 | tf_op jit(solution)/shard_map/ppermute | solution.py:394
  34.0 9.6 %collective-permute-start.14 = (bf16[64,1536]{1,0:T(8,128)(2,1)S(1)}, bf16[64,1536]{1,0:T(8,128)(2,1)S(1)}, u32[]{:S(2)}, u32[]{:S(2)}) collective-permute-start(bf16[64,1536]{1,0:T(8,128)(2,1)S(1)} %collective-permute-done.5.p0), channel_id=1, source_target_pairs={{0,16},{8,24},{16,0},{24,8},{32,48},{40,56},{48,32},{56,40},{64,80... | collective-permute-start | bytes 589832 | tf_op jit(solution)/shard_map/ppermute | solution.py:395
  37.6 6.8 %collective-permute-start.9 = (bf16[128,512]{1,0:T(8,128)(2,1)S(1)}, bf16[128,512]{1,0:T(8,128)(2,1)S(1)}, u32[]{:S(2)}, u32[]{:S(2)}) collective-permute-start(bf16[128,512]{1,0:T(8,128)(2,1)S(1)} %shard_map.81.p0), channel_id=1, source_target_pairs={{0,6},{1,7},{2,0},{3,1},{4,2},{5,3},{6,4},{7,5},{8,14},{9,15},{10,... | collective-permute-start | bytes 393224 | tf_op jit(solution)/shard_map/ppermute | solution.py:31
  37.6 8.8 %collective-permute-start.8 = (bf16[128,512]{1,0:T(8,128)(2,1)S(1)}, bf16[128,512]{1,0:T(8,128)(2,1)S(1)}, u32[]{:S(2)}, u32[]{:S(2)}) collective-permute-start(bf16[128,512]{1,0:T(8,128)(2,1)S(1)} %shard_map.81.p0), channel_id=1, source_target_pairs={{0,4},{1,5},{2,6},{3,7},{4,0},{5,1},{6,2},{7,3},{8,12},{9,13},{10,... | collective-permute-start | bytes 393224 | tf_op jit(solution)/shard_map/ppermute | solution.py:31
  43.5 5.0 %collective-permute-start.7 = (bf16[128,512]{1,0:T(8,128)(2,1)S(1)}, bf16[128,512]{1,0:T(8,128)(2,1)S(1)}, u32[]{:S(2)}, u32[]{:S(2)}) collective-permute-start(bf16[128,512]{1,0:T(8,128)(2,1)S(1)} %shard_map.81.p0), channel_id=1, source_target_pairs={{0,2},{1,3},{2,4},{3,5},{4,6},{5,7},{6,0},{7,1},{8,10},{9,11},{10,... | collective-permute-start | bytes 393224 | tf_op jit(solution)/shard_map/ppermute | solution.py:31
  44.2 22.1 %collective-permute-start.17 = (bf16[128,1536]{1,0:T(8,128)(2,1)S(1)}, bf16[128,1536]{1,0:T(8,128)(2,1)S(1)}, u32[]{:S(2)}, u32[]{:S(2)}) collective-permute-start(bf16[128,1536]{1,0:T(8,128)(2,1)S(1)} %shard_map.84.refs_4_), channel_id=1, source_target_pairs={{0,96},{8,104},{16,112},{24,120},{32,0},{40,8},{48,16},{56,24},{64... | collective-permute-start | bytes 1179656 | tf_op jit(solution)/shard_map/ppermute | solution.py:31
  44.2 23.7 %collective-permute-start.16 = (bf16[128,1536]{1,0:T(8,128)(2,1)S(1)}, bf16[128,1536]{1,0:T(8,128)(2,1)S(1)}, u32[]{:S(2)}, u32[]{:S(2)}) collective-permute-start(bf16[128,1536]{1,0:T(8,128)(2,1)S(1)} %shard_map.84.refs_4_), channel_id=1, source_target_pairs={{0,64},{8,72},{16,80},{24,88},{32,96},{40,104},{48,112},{56,120},{... | collective-permute-start | bytes 1179656 | tf_op jit(solution)/shard_map/ppermute | solution.py:31
  44.4 23.5 %collective-permute-start.15 = (bf16[128,1536]{1,0:T(8,128)(2,1)S(1)}, bf16[128,1536]{1,0:T(8,128)(2,1)S(1)}, u32[]{:S(2)}, u32[]{:S(2)}) collective-permute-start(bf16[128,1536]{1,0:T(8,128)(2,1)S(1)} %shard_map.84.refs_4_), channel_id=1, source_target_pairs={{0,32},{8,40},{16,48},{24,56},{32,64},{40,72},{48,80},{56,88},{64,... | collective-permute-start | bytes 1179656 | tf_op jit(solution)/shard_map/ppermute | solution.py:31
  48.5 27.4 %collective-permute-start.13 = (bf16[128,1536]{1,0:T(8,128)(2,1)S(1)}, bf16[128,1536]{1,0:T(8,128)(2,1)S(1)}, u32[]{:S(2)}, u32[]{:S(2)}) collective-permute-start(bf16[128,1536]{1,0:T(8,128)(2,1)S(1)} %shard_map.82.refs_0_), channel_id=1, source_target_pairs={{0,6},{1,7},{2,0},{3,1},{4,2},{5,3},{6,4},{7,5},{8,14},{9,15},{10,... | collective-permute-start | bytes 1179656 | tf_op jit(solution)/shard_map/ppermute | solution.py:31
  48.5 27.5 %collective-permute-start.12 = (bf16[128,1536]{1,0:T(8,128)(2,1)S(1)}, bf16[128,1536]{1,0:T(8,128)(2,1)S(1)}, u32[]{:S(2)}, u32[]{:S(2)}) collective-permute-start(bf16[128,1536]{1,0:T(8,128)(2,1)S(1)} %shard_map.82.refs_0_), channel_id=1, source_target_pairs={{0,4},{1,5},{2,6},{3,7},{4,0},{5,1},{6,2},{7,3},{8,12},{9,13},{10,... | collective-permute-start | bytes 1179656 | tf_op jit(solution)/shard_map/ppermute | solution.py:31
  63.9 0.8 copy-start.5
  66.2 21.1 %collective-permute-start.11 = (bf16[128,1536]{1,0:T(8,128)(2,1)S(1)}, bf16[128,1536]{1,0:T(8,128)(2,1)}, u32[]{:S(2)}, u32[]{:S(2)}) collective-permute-start(bf16[128,1536]{1,0:T(8,128)(2,1)S(1)} %shard_map.82.refs_0_), channel_id=1, source_target_pairs={{0,2},{1,3},{2,4},{3,5},{4,6},{5,7},{6,0},{7,1},{8,10},{9,11},{10,... | collective-permute-start | bytes 1179656 | tf_op jit(solution)/shard_map/ppermute | solution.py:31
  75.3 12.1 %slice-start = ((s8[9437184]{0:T(1024)(128)(4,1)}), s8[4194304]{0:T(1024)(128)(4,1)S(1)}, s32[]{:S(2)}) async-start(s8[9437184]{0:T(1024)(128)(4,1)} %bitcast.34), calls=%async_computation | async-start | bytes 8388608
  75.3 12.0 %slice-start.1 = ((s8[9437184]{0:T(1024)(128)(4,1)}), s8[4194304]{0:T(1024)(128)(4,1)S(1)}, s32[]{:S(2)}) async-start(s8[9437184]{0:T(1024)(128)(4,1)} %bitcast.34), calls=%async_computation.1 | async-start | bytes 8388608
  75.3 12.0 %slice-start.2 = ((s8[9437184]{0:T(1024)(128)(4,1)}), s8[1048576]{0:T(1024)(128)(4,1)S(1)}, s32[]{:S(2)}) async-start(s8[9437184]{0:T(1024)(128)(4,1)} %bitcast.34), calls=%async_computation.2 | async-start | bytes 2097152
  75.3 12.0 %copy-start.4 = (s32[12,24]{1,0:T(8,128)S(1)}, s32[12,24]{1,0:T(8,128)}, u32[]{:S(2)}) copy-start(s32[12,24]{1,0:T(8,128)} %pattern_ref.1) | copy-start | bytes 3460
  75.3 12.0 %copy-start.6 = (f32[256,512]{1,0:T(8,128)S(1)}, f32[256,512]{1,0:T(8,128)}, u32[]{:S(2)}) copy-start(f32[256,512]{1,0:T(8,128)} %copy-done.5) | copy-start | bytes 1572868
  75.3 12.0 %copy-start.8 = (bf16[256,512]{1,0:T(8,128)(2,1)S(1)}, bf16[256,512]{1,0:T(8,128)(2,1)}, u32[]{:S(2)}) copy-start(bf16[256,512]{1,0:T(8,128)(2,1)} %copy-done.7) | copy-start | bytes 786436
  75.3 11.9 %collective-permute-start.18 = (bf16[128,1536]{1,0:T(8,128)(2,1)S(1)}, bf16[128,1536]{1,0:T(8,128)(2,1)S(1)}, u32[]{:S(2)}, u32[]{:S(2)}) collective-permute-start(bf16[128,1536]{1,0:T(8,128)(2,1)S(1)} %shard_map.84.refs_4_), channel_id=1, source_target_pairs={{0,8},{8,0},{16,24},{24,16},{32,40},{40,32},{48,56},{56,48},{64,72... | collective-permute-start | bytes 1179656 | tf_op jit(solution)/shard_map/ppermute | solution.py:406
  75.4 11.8 %collective-permute-start.19 = (bf16[128,1536]{1,0:T(8,128)(2,1)S(1)}, bf16[128,1536]{1,0:T(8,128)(2,1)S(1)}, u32[]{:S(2)}, u32[]{:S(2)}) collective-permute-start(bf16[128,1536]{1,0:T(8,128)(2,1)S(1)} %collective-permute-done.15.refs_5_), channel_id=1, source_target_pairs={{0,8},{8,0},{16,24},{24,16},{32,40},{40,32},{48,56},{56,48},{64,72... | collective-permute-start | bytes 1179656 | tf_op jit(solution)/shard_map/ppermute | solution.py:406
  75.9 11.4 %collective-permute-start.20 = (bf16[128,1536]{1,0:T(8,128)(2,1)S(1)}, bf16[128,1536]{1,0:T(8,128)(2,1)S(1)}, u32[]{:S(2)}, u32[]{:S(2)}) collective-permute-start(bf16[128,1536]{1,0:T(8,128)(2,1)S(1)} %collective-permute-done.16.refs_6_), channel_id=1, source_target_pairs={{0,8},{8,0},{16,24},{24,16},{32,40},{40,32},{48,56},{56,48},{64,72... | collective-permute-start | bytes 1179656 | tf_op jit(solution)/shard_map/ppermute | solution.py:406
  76.0 11.3 %collective-permute-start.21 = (bf16[128,1536]{1,0:T(8,128)(2,1)S(1)}, bf16[128,1536]{1,0:T(8,128)(2,1)S(1)}, u32[]{:S(2)}, u32[]{:S(2)}) collective-permute-start(bf16[128,1536]{1,0:T(8,128)(2,1)S(1)} %collective-permute-done.17.refs_7_), channel_id=1, source_target_pairs={{0,8},{8,0},{16,24},{24,16},{32,40},{40,32},{48,56},{56,48},{64,72... | collective-permute-start | bytes 1179656 | tf_op jit(solution)/shard_map/ppermute | solution.py:406
  76.5 1.6 %copy-start.10 = (f32[256,512]{1,0:T(8,128)S(1)}, f32[256,512]{1,0:T(8,128)}, u32[]{:S(2)}) copy-start(f32[256,512]{1,0:T(8,128)} %copy-done.9) | copy-start | bytes 1572868
  (4 other events, 2.9 us)

commit v4 on v3

--- a/solution.py
+++ b/solution.py
@@ -197,9 +197,12 @@
     eliminate(g_ref, w_ref, half_ref, (0, 2), 0)
 
 
-def lower_kernel(in_ref, w_ref, half_ref, g_ref):
-    g_ref[in_ref.shape[0] :, :] = in_ref[...]
-    eliminate(g_ref, w_ref, half_ref, (2, 4), 2 * BLOCK)
+def lower_kernel(in_ref, w_top, half_top, w_ref, half_ref, g_ref):
+    top = in_ref.shape[0]
+    g_ref[top:, :] = in_ref[...]
+    w_ref[:top, :] = w_top[...]
+    half_ref[:top, :] = half_top[...]
+    eliminate(g_ref, w_ref, half_ref, (2, 4), 0)
 
 
 def upper_inverse(pieces, at):
@@ -225,25 +228,25 @@
     )(at, *pieces)
 
 
-def lower_inverse(rest):
-    half, n = rest.shape
+def lower_inverse(rest, w_top, half_top):
+    n = rest.shape[1]
     vmem = pl.BlockSpec(memory_space=pltpu.VMEM)
     return pl.pallas_call(
         lower_kernel,
-        out_shape=(jax.ShapeDtypeStruct((half, n), F32), jax.ShapeDtypeStruct((half, n), BF16)),
-        in_specs=[vmem],
+        out_shape=(jax.ShapeDtypeStruct((n, n), F32), jax.ShapeDtypeStruct((n, n), BF16)),
+        in_specs=[vmem] * 3,
         out_specs=(vmem,) * 2,
         scratch_shapes=[pltpu.VMEM((n, n), F32)],
         compiler_params=pltpu.CompilerParams(vmem_limit_bytes=8 << 20),
         cost_estimate=pl.CostEstimate(flops=10 << 30, bytes_accessed=4 * n * n, transcendentals=0),
-    )(rest)
+    )(rest, w_top, half_top)
 
 
 def update_kernel(at_ref, pattern_ref, *refs):
     rows_in, first_in, second_in = refs[0:4], refs[4:8], refs[8:12]
-    w_top, w_low, half_top, half_low, loads_ref, pivot_ref, trailing_ref, out_ref, loads_out_ref = refs[12:21]
-    factor_ref, other_ref, half_ref, new_ref, list_ref, sems = refs[21:27]
-    raw_refs = refs[27:30]
+    w_ref, half_ref, loads_ref, pivot_ref, trailing_ref, out_ref, loads_out_ref = refs[12:19]
+    factor_ref, other_ref, new_ref, list_ref, sems = refs[19:24]
+    raw_refs = refs[24:27]
     n = half_ref.shape[0]
     row_dev, col_dev = trailing_ref.shape
     x, y, core = at_ref[0] >> 2, at_ref[1] >> 1, at_ref[0] & 1
@@ -268,8 +271,6 @@
         return count + (filled != 0).astype(jnp.int32)
 
     count = lax.fori_loop(0, row_dev // BLOCK, sort_strip, 0)
-    half_ref[: n // 2, :] = half_top[...]
-    half_ref[n // 2 :, :] = half_low[...]
 
     def assemble(raw_ref, pieces, spot):
         for k, piece in enumerate(pieces):
@@ -316,14 +317,8 @@
 
     lax.fori_loop(0, (count + 1) // 2, pair_step, 0)
 
-    solve = jnp.concatenate(
-        [
-            lax.dot_general(
-                pivot_ref[...], w[...], (((1,), (1,)), ((), ())), precision=HI, preferred_element_type=F32
-            )
-            for w in (w_top, w_low)
-        ],
-        1,
+    solve = lax.dot_general(
+        pivot_ref[...], w_ref[...], (((1,), (1,)), ((), ())), precision=HI, preferred_element_type=F32
     )
     one = solve.astype(BF16)
     rest = solve - one.astype(F32)
@@ -340,9 +335,9 @@
     lax.fori_loop(0, row_dev // BLOCK, lambda s, c: (copy(new_ref, s).wait(), c)[1], 0)
 
 
-def update(at, pattern, rows, first, second, w_parts, half_parts, regrouped, pivot_loads, trailing):
+def update(at, pattern, rows, first, second, w, half, regrouped, pivot_loads, trailing):
     row_dev, col_dev = trailing.shape
-    n = half_parts[0].shape[1]
+    n = half.shape[0]
     smem = pl.BlockSpec(memory_space=pltpu.SMEM)
     vmem = pl.BlockSpec(memory_space=pltpu.VMEM)
     return pl.pallas_call(
@@ -351,12 +346,11 @@
             jax.ShapeDtypeStruct((row_dev, col_dev), BF16),
             jax.ShapeDtypeStruct((3, row_dev), F32),
         ),
-        in_specs=[smem, smem] + [vmem] * 19,
+        in_specs=[smem, smem] + [vmem] * 17,
         out_specs=(pl.BlockSpec(memory_space=pl.ANY), vmem),
         scratch_shapes=[
             pltpu.VMEM((row_dev, n), BF16),
             pltpu.VMEM((n, col_dev), BF16),
-            pltpu.VMEM((n, n), BF16),
             pltpu.VMEM((row_dev, col_dev), BF16),
             pltpu.SMEM((row_dev // BLOCK,), jnp.int32),
             pltpu.SemaphoreType.DMA((row_dev // BLOCK,)),
@@ -364,7 +358,7 @@
         + [pltpu.VMEM((n, row_dev), BF16)] * 3,
         compiler_params=pltpu.CompilerParams(vmem_limit_bytes=28 << 20),
         cost_estimate=pl.CostEstimate(flops=8 << 30, bytes_accessed=24 << 20, transcendentals=0),
-    )(at, pattern, *rows, *first, *second, *w_parts, *half_parts, regrouped, pivot_loads, trailing)
+    )(at, pattern, *rows, *first, *second, w, half, regrouped, pivot_loads, trailing)
 
 
 def per_device(loads, nd_source, panel, trailing, pattern, owner):
@@ -379,12 +373,11 @@
     mine = panel.T
     both = lax.optimization_barrier
 
+    moved = lax.ppermute(mine, ("row", "col"), transposed_place())
     packets = ring(pack(mine, loads, nd_source), X_SHIFT, "row")
     rows_other = lax.ppermute(mine, "col", Z_LO)
     (packet,) = small_call(choose_x, [(56, row_dev)], at, *packets)
-    packet, moving = both((packet, mine))
     packet_other = lax.ppermute(packet, "row", Z_HI)
-    moved = lax.ppermute(moving, ("row", "col"), transposed_place())
     (packet,) = small_call(choose_z, [(88, row_dev)], at, packet, packet_other)
     packet_other = lax.ppermute(packet, "row", CORE)
     pivot, digits = small_call(
@@ -398,22 +391,20 @@
     pivot = ring(pivot, Y_SHIFT, "col")
     (first,) = small_call(pair_z_hi, [(2 * slice_width, row_dev)], at, moved, moved_other)
     first = ring(first, X_SHIFT, "row")
-    pivot, rows = both((pivot, rows))
-    rows = ring(rows, Y_SHIFT, "col")
-
-    w_top, half_top, rest = upper_inverse(pivot, at)
-    rest, first, packet, packet_other = both((rest, first, packet, packet_other))
-    second = [lax.ppermute(piece, "row", CORE) for piece in first]
 
     everyone = jnp.concatenate([packet[24:], packet_other[24:]], 0).reshape(row_count, 8, row_dev)
     regrouped = regroup(everyone, nd_source, row_place, row_place, share_size)
     pivot_source = digits[0].astype(jnp.int32) * BLOCK + digits[1].astype(jnp.int32)
     pivot_loads = regroup(everyone, pivot_source, row_place, root, share_size)
 
-    rest, regrouped, pivot_loads = both((rest, regrouped, pivot_loads))
-    w_low, half_low = lower_inverse(rest)
+    pivot, rows, regrouped, pivot_loads = both((pivot, rows, regrouped, pivot_loads))
+    rows = ring(rows, Y_SHIFT, "col")
+    w_top, half_top, rest = upper_inverse(pivot, at)
+    rest, first = both((rest, first))
+    second = [lax.ppermute(piece, "row", CORE) for piece in first]
+    w, half = lower_inverse(rest, w_top, half_top)
     trailing_out, loads_out = update(
-        at, pattern, rows, first, second, (w_top, w_low), (half_top, half_low), regrouped, pivot_loads, trailing
+        at, pattern, rows, first, second, w, half, regrouped, pivot_loads, trailing
     )
     return loads_out, trailing_out
 

time: 96.8 us -> 96.4 us (level)
  the two profiles are of different devices: /device:TPU:16 before, /device:TPU:25 now
where the time goes in v4:
time: 96.4 us
  Pallas kernels  33.6 us (35%)
  waiting for transfers between devices  26.4 us (27%)
  starting transfers between devices  24.3 us (25%)
  local copies, waits for them, and re-layouts  8.65 us (9%)
  between operations  1.82 us (2%)
  other arithmetic  1.57 us (2%)
    ppermute x12, waiting for transfers between devices, ring(): return [mine] + [lax.ppermute(mine, axis, shifts[k]) for k in (1, 2, 3)]  19.6 us
    pallas_call x1, Pallas kernels, upper_inverse(): pl.pallas_call(kernel, out_shape=(jax.ShapeDtypeStruct((n // 2, n), F32),...  11.9 us
    ppermute x12, starting transfers between devices, ring(): return [mine] + [lax.ppermute(mine, axis, shifts[k]) for k in (1, 2, 3)]  11.9 us
    pallas_call x1, Pallas kernels, lower_inverse(): pl.pallas_call(lower_kernel, out_shape=(jax.ShapeDtypeStruct((n, n), F32)...  9.26 us
    pallas_call x1, Pallas kernels, update(): pl.pallas_call(update_kernel, out_shape=(jax.ShapeDtypeStruct((row_dev, c...  9.03 us
    ppermute x1, waiting for transfers between devices, per_device(): moved = lax.ppermute(mine, ('row', 'col'), transposed_place())  5.83 us
    gather x4, local copies, waits for them, and re-layouts, regroup(): parts = jnp.take(arrived, slot, axis=1)  4.76 us
    ppermute x1, starting transfers between devices, per_device(): packet_other = lax.ppermute(packet, 'row', Z_HI)  3.68 us
  transfers between devices with their start and end apart: 22, of which 6 were waited for; matrix products, arithmetic and copies ran while one was open for 7% of the time, Pallas kernels for 25%

profile of v4, /device:TPU:25, one launch (start us, length us, event | category | flops | bytes accessed | tf_op | source)
XLA Modules:
  0.0 96.4 jit_solution(8425388897316817624)
XLA Ops:
  0.6 0.9 copy-done
  1.6 0.7 copy-done.2
  2.3 0.7 copy-done.3
  3.0 2.5 %collective-permute-start.2 = (bf16[32,1536]{1,0:T(8,128)(2,1)S(1)}, bf16[32,1536]{1,0:T(8,128)(2,1)S(1)}, u32[]{:S(2)}, u32[]{:S(2)}) collective-permute-start(bf16[32,1536]{1,0:T(8,128)(2,1)S(1)} %shard_map.77.p0), channel_id=1, source_target_pairs={{0,96},{8,104},{16,112},{24,120},{32,0},{40,8},{48,16},{56,24},{64... | collective-permute-start | bytes 294920 | tf_op jit(solution)/shard_map/ppermute | solution.py:31
  6.1 0.6 collective-permute-start
  6.7 0.7 pad_add_fusion.at_ref
  7.4 3.2 %collective-permute-done.1.p2 = bf16[32,1536]{1,0:T(8,128)(2,1)S(1)} collective-permute-done((bf16[32,1536]{1,0:T(8,128)(2,1)S(1)}, bf16[32,1536]{1,0:T(8,128)(2,1)S(1)}, u32[]{:S(2)}, u32[]{:S(2)}) %collective-permute-start.1) | collective-permute-done | bytes 98336 | tf_op jit(solution)/shard_map/ppermute | solution.py:31
  10.6 2.7 %collective-permute-done.p1 = bf16[32,1536]{1,0:T(8,128)(2,1)S(1)} collective-permute-done((bf16[32,1536]{1,0:T(8,128)(2,1)S(1)}, bf16[32,1536]{1,0:T(8,128)(2,1)S(1)}, u32[]{:S(2)}, u32[]{:S(2)}) %collective-permute-start) | collective-permute-done | bytes 98336 | tf_op jit(solution)/shard_map/ppermute | solution.py:31
  13.3 0.6 shard_map.78.p0
  13.9 3.7 %collective-permute-start.3 = (bf16[56,1536]{1,0:T(8,128)(2,1)S(1)}, bf16[56,1536]{1,0:T(8,128)(2,1)S(1)}, u32[]{:S(2)}, u32[]{:S(2)}) collective-permute-start(bf16[56,1536]{1,0:T(8,128)(2,1)S(1)} %shard_map.78.p0), channel_id=1, source_target_pairs={{0,16},{8,24},{16,0},{24,8},{32,48},{40,56},{48,32},{56,40},{64,80... | collective-permute-start | bytes 516104 | tf_op jit(solution)/shard_map/ppermute | solution.py:380
  17.6 0.7 collective-permute-start.10
  18.3 1.9 %collective-permute-start.5 = (bf16[64,1536]{1,0:T(8,128)(2,1)}, bf16[64,1536]{1,0:T(8,128)(2,1)S(1)}, u32[]{:S(2)}, u32[]{:S(2)}) collective-permute-start(bf16[64,1536]{1,0:T(8,128)(2,1)} %bitcast.30), channel_id=1, source_target_pairs={{0,0},{1,16},{2,32},{3,48},{4,64},{5,80},{6,96},{7,112},{8,8},{9,2... | collective-permute-start | bytes 589832 | tf_op jit(solution)/shard_map/ppermute | solution.py:376
  20.2 1.0 collective-permute-done.3.p1
  21.2 0.6 shard_map.79.p0
  21.8 3.1 %collective-permute-start.4 = (bf16[88,1536]{1,0:T(8,128)(2,1)S(1)}, bf16[88,1536]{1,0:T(8,128)(2,1)S(1)}, u32[]{:S(2)}, u32[]{:S(2)}) collective-permute-start(bf16[88,1536]{1,0:T(8,128)(2,1)S(1)} %shard_map.79.p0), channel_id=1, source_target_pairs={{0,8},{8,0},{16,24},{24,16},{32,40},{40,32},{48,56},{56,48},{64,72... | collective-permute-start | bytes 811016 | tf_op jit(solution)/shard_map/ppermute | solution.py:382
  24.9 0.7 compare_and_fusion
  26.3 0.9 copy-done.1
  27.2 0.6 shard_map.82.refs_0_
  27.8 0.6 shard_map.80
  28.4 5.8 %collective-permute-done.5.p0 = bf16[64,1536]{1,0:T(8,128)(2,1)S(1)} collective-permute-done((bf16[64,1536]{1,0:T(8,128)(2,1)}, bf16[64,1536]{1,0:T(8,128)(2,1)S(1)}, u32[]{:S(2)}, u32[]{:S(2)}) %collective-permute-start.5) | collective-permute-done | bytes 196640 | tf_op jit(solution)/shard_map/ppermute | solution.py:376
  34.3 1.7 %collective-permute-start.6 = (bf16[64,512]{1,0:T(8,128)(2,1)S(1)}, bf16[64,512]{1,0:T(8,128)(2,1)S(1)}, u32[]{:S(2)}, u32[]{:S(2)}) collective-permute-start(bf16[64,512]{1,0:T(8,128)(2,1)S(1)} %get-tuple-element.26.p0), channel_id=1, source_target_pairs={{0,1},{1,0},{2,3},{3,2},{4,5},{5,4},{6,7},{7,6},{8,9},{9,8},{10,11... | collective-permute-start | bytes 196616 | tf_op jit(solution)/shard_map/ppermute | solution.py:387
  36.6 1.3 %gather_fusion.1 = bf16[512,8]{1,0:T(8,128)(2,1)S(1)} fusion(bf16[8,1536]{0,1:T(8,128)(2,1)S(1)} %bitcast.37, s32[1024]{0:T(1024)S(1)} %pad_clamp_fusion.1), kind=kCustom, calls=%fused_computation.1 | custom fusion | bytes 18432 | tf_op jit(solution)/shard_map/jit(_take)/gather | solution.py:109
  38.3 3.2 %gather_fusion = bf16[1536,8]{1,0:T(8,128)(2,1)S(1)} fusion(bf16[8,1536]{0,1:T(8,128)(2,1)S(1)} %bitcast.36, s32[2048]{0:T(1024)S(1)} %pad_clamp_fusion), kind=kCustom, calls=%fused_computation | custom fusion | bytes 55296 | tf_op jit(solution)/shard_map/jit(_take)/gather | solution.py:109
  42.4 2.6 %collective-permute-start.7 = (bf16[128,512]{1,0:T(8,128)(2,1)S(1)}, bf16[128,512]{1,0:T(8,128)(2,1)S(1)}, u32[]{:S(2)}, u32[]{:S(2)}) collective-permute-start(bf16[128,512]{1,0:T(8,128)(2,1)S(1)} %shard_map.81.p0), channel_id=1, source_target_pairs={{0,2},{1,3},{2,4},{3,5},{4,6},{5,7},{6,0},{7,1},{8,10},{9,11},{10,... | collective-permute-start | bytes 393224 | tf_op jit(solution)/shard_map/ppermute | solution.py:31
  45.0 6.3 %collective-permute-done.9.p3 = bf16[128,512]{1,0:T(8,128)(2,1)S(1)} collective-permute-done((bf16[128,512]{1,0:T(8,128)(2,1)S(1)}, bf16[128,512]{1,0:T(8,128)(2,1)S(1)}, u32[]{:S(2)}, u32[]{:S(2)}) %collective-permute-start.9) | collective-permute-done | bytes 131104 | tf_op jit(solution)/shard_map/ppermute | solution.py:31
  51.3 3.7 %collective-permute-start.12 = (bf16[128,1536]{1,0:T(8,128)(2,1)S(1)}, bf16[128,1536]{1,0:T(8,128)(2,1)S(1)}, u32[]{:S(2)}, u32[]{:S(2)}) collective-permute-start(bf16[128,1536]{1,0:T(8,128)(2,1)S(1)} %shard_map.82.refs_0_), channel_id=1, source_target_pairs={{0,4},{1,5},{2,6},{3,7},{4,0},{5,1},{6,2},{7,3},{8,12},{9,13},{10,... | collective-permute-start | bytes 1179656 | tf_op jit(solution)/shard_map/ppermute | solution.py:31
  55.0 0.6 shard_map.84.refs_4_
  55.8 1.4 %collective-permute-start.15 = (bf16[128,1536]{1,0:T(8,128)(2,1)S(1)}, bf16[128,1536]{1,0:T(8,128)(2,1)S(1)}, u32[]{:S(2)}, u32[]{:S(2)}) collective-permute-start(bf16[128,1536]{1,0:T(8,128)(2,1)S(1)} %shard_map.84.refs_4_), channel_id=1, source_target_pairs={{0,32},{8,40},{16,48},{24,56},{32,64},{40,72},{48,80},{56,88},{64,... | collective-permute-start | bytes 1179656 | tf_op jit(solution)/shard_map/ppermute | solution.py:31
  57.1 11.9 %shard_map.83 = (f32[256,512]{1,0:T(8,128)S(1)}, bf16[256,512]{1,0:T(8,128)(2,1)S(1)}, f32[256,512]{1,0:T(8,128)S(1)}) custom-call(s32[3]{0:T(128)S(1)} %pad_add_fusion.at_ref, bf16[128,512]{1,0:T(8,128)(2,1)S(1)} %shard_map.81.p0, bf16[128,512]{1,0:T(8,128)(2,1)S(1)} %collective-permute-done.7.p1, bf16[128,512]{1,0:T(8,128)(2,1)S(1)} %collective-permute-done.8.p2, ...), custom_call_target="tpu_custom_call" | custom-call | flops 10737418240 | bytes 1048576 | tf_op jit(solution)/shard_map/pallas_call | solution.py:216
  69.3 7.4 %collective-permute-done.15.refs_5_ = bf16[128,1536]{1,0:T(8,128)(2,1)S(1)} collective-permute-done((bf16[128,1536]{1,0:T(8,128)(2,1)S(1)}, bf16[128,1536]{1,0:T(8,128)(2,1)S(1)}, u32[]{:S(2)}, u32[]{:S(2)}) %collective-permute-start.15) | collective-permute-done | bytes 393248 | tf_op jit(solution)/shard_map/ppermute | solution.py:31
  77.8 9.3 %shard_map.85 = (f32[512,512]{1,0:T(8,128)S(1)}, bf16[512,512]{1,0:T(8,128)(2,1)S(1)}) custom-call(f32[256,512]{1,0:T(8,128)S(1)} %get-tuple-element.39.in_ref, f32[256,512]{1,0:T(8,128)S(1)} %get-tuple-element.40.w_top, bf16[256,512]{1,0:T(8,128)(2,1)S(1)} %get-tuple-element.41.half_top), custom_call_target="tpu_custom_call" | custom-call | flops 10737418240 | bytes 1048576 | tf_op jit(solution)/shard_map/pallas_call | solution.py:234
  87.2 9.0 %shard_map.86 = (bf16[1536,3072]{1,0:T(8,128)(2,1)}, f32[3,1536]{1,0:T(4,128)}) custom-call(s32[3]{0:T(128)S(1)} %pad_add_fusion.at_ref, s32[12,24]{1,0:T(8,128)S(1)} %copy-done.4, bf16[128,1536]{1,0:T(8,128)(2,1)S(1)} %shard_map.82.refs_0_, bf16[128,1536]{1,0:T(8,128)(2,1)S(1)} %collective-permute-done.11.refs_1_, ...), custom_call_target="tpu_custom_call" | custom-call | flops 8589934592 | bytes 25165824 | tf_op jit(solution)/shard_map/pallas_call | solution.py:343
  (61 shorter events, 4.0 us)
Async XLA Ops:
  0.6 0.9 copy-start
  1.6 0.7 copy-start.2
  2.3 0.7 copy-start.3
  3.0 4.4 %collective-permute-start.2 = (bf16[32,1536]{1,0:T(8,128)(2,1)S(1)}, bf16[32,1536]{1,0:T(8,128)(2,1)S(1)}, u32[]{:S(2)}, u32[]{:S(2)}) collective-permute-start(bf16[32,1536]{1,0:T(8,128)(2,1)S(1)} %shard_map.77.p0), channel_id=1, source_target_pairs={{0,96},{8,104},{16,112},{24,120},{32,0},{40,8},{48,16},{56,24},{64... | collective-permute-start | bytes 294920 | tf_op jit(solution)/shard_map/ppermute | solution.py:31
  5.6 5.1 %collective-permute-start.1 = (bf16[32,1536]{1,0:T(8,128)(2,1)S(1)}, bf16[32,1536]{1,0:T(8,128)(2,1)S(1)}, u32[]{:S(2)}, u32[]{:S(2)}) collective-permute-start(bf16[32,1536]{1,0:T(8,128)(2,1)S(1)} %shard_map.77.p0), channel_id=1, source_target_pairs={{0,64},{8,72},{16,80},{24,88},{32,96},{40,104},{48,112},{56,120},{... | collective-permute-start | bytes 294920 | tf_op jit(solution)/shard_map/ppermute | solution.py:31
  6.1 7.2 %collective-permute-start = (bf16[32,1536]{1,0:T(8,128)(2,1)S(1)}, bf16[32,1536]{1,0:T(8,128)(2,1)S(1)}, u32[]{:S(2)}, u32[]{:S(2)}) collective-permute-start(bf16[32,1536]{1,0:T(8,128)(2,1)S(1)} %shard_map.77.p0), channel_id=1, source_target_pairs={{0,32},{8,40},{16,48},{24,56},{32,64},{40,72},{48,80},{56,88},{64,... | collective-permute-start | bytes 294920 | tf_op jit(solution)/shard_map/ppermute | solution.py:31
  13.9 7.3 %collective-permute-start.3 = (bf16[56,1536]{1,0:T(8,128)(2,1)S(1)}, bf16[56,1536]{1,0:T(8,128)(2,1)S(1)}, u32[]{:S(2)}, u32[]{:S(2)}) collective-permute-start(bf16[56,1536]{1,0:T(8,128)(2,1)S(1)} %shard_map.78.p0), channel_id=1, source_target_pairs={{0,16},{8,24},{16,0},{24,8},{32,48},{40,56},{48,32},{56,40},{64,80... | collective-permute-start | bytes 516104 | tf_op jit(solution)/shard_map/ppermute | solution.py:380
  17.6 8.7 %collective-permute-start.10 = (bf16[64,1536]{1,0:T(8,128)(2,1)}, bf16[64,1536]{1,0:T(8,128)(2,1)S(1)}, u32[]{:S(2)}, u32[]{:S(2)}) collective-permute-start(bf16[64,1536]{1,0:T(8,128)(2,1)} %bitcast.29), channel_id=1, source_target_pairs={{0,1},{1,0},{2,3},{3,2},{4,5},{5,4},{6,7},{7,6},{8,9},{9,8},{10,11... | collective-permute-start | bytes 589832 | tf_op jit(solution)/shard_map/ppermute | solution.py:378
  18.3 15.9 %collective-permute-start.5 = (bf16[64,1536]{1,0:T(8,128)(2,1)}, bf16[64,1536]{1,0:T(8,128)(2,1)S(1)}, u32[]{:S(2)}, u32[]{:S(2)}) collective-permute-start(bf16[64,1536]{1,0:T(8,128)(2,1)} %bitcast.30), channel_id=1, source_target_pairs={{0,0},{1,16},{2,32},{3,48},{4,64},{5,80},{6,96},{7,112},{8,8},{9,2... | collective-permute-start | bytes 589832 | tf_op jit(solution)/shard_map/ppermute | solution.py:376
  21.8 6.1 %collective-permute-start.4 = (bf16[88,1536]{1,0:T(8,128)(2,1)S(1)}, bf16[88,1536]{1,0:T(8,128)(2,1)S(1)}, u32[]{:S(2)}, u32[]{:S(2)}) collective-permute-start(bf16[88,1536]{1,0:T(8,128)(2,1)S(1)} %shard_map.79.p0), channel_id=1, source_target_pairs={{0,8},{8,0},{16,24},{24,16},{32,40},{40,32},{48,56},{56,48},{64,72... | collective-permute-start | bytes 811016 | tf_op jit(solution)/shard_map/ppermute | solution.py:382
  26.3 0.9 copy-start.1
  34.3 7.4 %collective-permute-start.6 = (bf16[64,512]{1,0:T(8,128)(2,1)S(1)}, bf16[64,512]{1,0:T(8,128)(2,1)S(1)}, u32[]{:S(2)}, u32[]{:S(2)}) collective-permute-start(bf16[64,512]{1,0:T(8,128)(2,1)S(1)} %get-tuple-element.26.p0), channel_id=1, source_target_pairs={{0,1},{1,0},{2,3},{3,2},{4,5},{5,4},{6,7},{7,6},{8,9},{9,8},{10,11... | collective-permute-start | bytes 196616 | tf_op jit(solution)/shard_map/ppermute | solution.py:387
  36.0 19.0 %collective-permute-start.14 = (bf16[64,1536]{1,0:T(8,128)(2,1)S(1)}, bf16[64,1536]{1,0:T(8,128)(2,1)S(1)}, u32[]{:S(2)}, u32[]{:S(2)}) collective-permute-start(bf16[64,1536]{1,0:T(8,128)(2,1)S(1)} %collective-permute-done.5.p0), channel_id=1, source_target_pairs={{0,16},{8,24},{16,0},{24,8},{32,48},{40,56},{48,32},{56,40},{64,80... | collective-permute-start | bytes 589832 | tf_op jit(solution)/shard_map/ppermute | solution.py:388
  42.3 9.1 %collective-permute-start.9 = (bf16[128,512]{1,0:T(8,128)(2,1)S(1)}, bf16[128,512]{1,0:T(8,128)(2,1)S(1)}, u32[]{:S(2)}, u32[]{:S(2)}) collective-permute-start(bf16[128,512]{1,0:T(8,128)(2,1)S(1)} %shard_map.81.p0), channel_id=1, source_target_pairs={{0,6},{1,7},{2,0},{3,1},{4,2},{5,3},{6,4},{7,5},{8,14},{9,15},{10,... | collective-permute-start | bytes 393224 | tf_op jit(solution)/shard_map/ppermute | solution.py:31
  42.4 9.0 %collective-permute-start.8 = (bf16[128,512]{1,0:T(8,128)(2,1)S(1)}, bf16[128,512]{1,0:T(8,128)(2,1)S(1)}, u32[]{:S(2)}, u32[]{:S(2)}) collective-permute-start(bf16[128,512]{1,0:T(8,128)(2,1)S(1)} %shard_map.81.p0), channel_id=1, source_target_pairs={{0,4},{1,5},{2,6},{3,7},{4,0},{5,1},{6,2},{7,3},{8,12},{9,13},{10,... | collective-permute-start | bytes 393224 | tf_op jit(solution)/shard_map/ppermute | solution.py:31
  42.4 8.9 %collective-permute-start.7 = (bf16[128,512]{1,0:T(8,128)(2,1)S(1)}, bf16[128,512]{1,0:T(8,128)(2,1)S(1)}, u32[]{:S(2)}, u32[]{:S(2)}) collective-permute-start(bf16[128,512]{1,0:T(8,128)(2,1)S(1)} %shard_map.81.p0), channel_id=1, source_target_pairs={{0,2},{1,3},{2,4},{3,5},{4,6},{5,7},{6,0},{7,1},{8,10},{9,11},{10,... | collective-permute-start | bytes 393224 | tf_op jit(solution)/shard_map/ppermute | solution.py:31
  51.3 25.9 %collective-permute-start.13 = (bf16[128,1536]{1,0:T(8,128)(2,1)S(1)}, bf16[128,1536]{1,0:T(8,128)(2,1)S(1)}, u32[]{:S(2)}, u32[]{:S(2)}) collective-permute-start(bf16[128,1536]{1,0:T(8,128)(2,1)S(1)} %shard_map.82.refs_0_), channel_id=1, source_target_pairs={{0,6},{1,7},{2,0},{3,1},{4,2},{5,3},{6,4},{7,5},{8,14},{9,15},{10,... | collective-permute-start | bytes 1179656 | tf_op jit(solution)/shard_map/ppermute | solution.py:31
  51.3 26.4 %collective-permute-start.12 = (bf16[128,1536]{1,0:T(8,128)(2,1)S(1)}, bf16[128,1536]{1,0:T(8,128)(2,1)S(1)}, u32[]{:S(2)}, u32[]{:S(2)}) collective-permute-start(bf16[128,1536]{1,0:T(8,128)(2,1)S(1)} %shard_map.82.refs_0_), channel_id=1, source_target_pairs={{0,4},{1,5},{2,6},{3,7},{4,0},{5,1},{6,2},{7,3},{8,12},{9,13},{10,... | collective-permute-start | bytes 1179656 | tf_op jit(solution)/shard_map/ppermute | solution.py:31
  55.6 13.4 %collective-permute-start.17 = (bf16[128,1536]{1,0:T(8,128)(2,1)S(1)}, bf16[128,1536]{1,0:T(8,128)(2,1)S(1)}, u32[]{:S(2)}, u32[]{:S(2)}) collective-permute-start(bf16[128,1536]{1,0:T(8,128)(2,1)S(1)} %shard_map.84.refs_4_), channel_id=1, source_target_pairs={{0,96},{8,104},{16,112},{24,120},{32,0},{40,8},{48,16},{56,24},{64... | collective-permute-start | bytes 1179656 | tf_op jit(solution)/shard_map/ppermute | solution.py:31
  55.7 13.6 %collective-permute-start.16 = (bf16[128,1536]{1,0:T(8,128)(2,1)S(1)}, bf16[128,1536]{1,0:T(8,128)(2,1)S(1)}, u32[]{:S(2)}, u32[]{:S(2)}) collective-permute-start(bf16[128,1536]{1,0:T(8,128)(2,1)S(1)} %shard_map.84.refs_4_), channel_id=1, source_target_pairs={{0,64},{8,72},{16,80},{24,88},{32,96},{40,104},{48,112},{56,120},{... | collective-permute-start | bytes 1179656 | tf_op jit(solution)/shard_map/ppermute | solution.py:31
  55.8 21.0 %collective-permute-start.15 = (bf16[128,1536]{1,0:T(8,128)(2,1)S(1)}, bf16[128,1536]{1,0:T(8,128)(2,1)S(1)}, u32[]{:S(2)}, u32[]{:S(2)}) collective-permute-start(bf16[128,1536]{1,0:T(8,128)(2,1)S(1)} %shard_map.84.refs_4_), channel_id=1, source_target_pairs={{0,32},{8,40},{16,48},{24,56},{32,64},{40,72},{48,80},{56,88},{64,... | collective-permute-start | bytes 1179656 | tf_op jit(solution)/shard_map/ppermute | solution.py:31
  57.1 30.0 %slice-start = ((s8[9437184]{0:T(1024)(128)(4,1)}), s8[4194304]{0:T(1024)(128)(4,1)S(1)}, s32[]{:S(2)}) async-start(s8[9437184]{0:T(1024)(128)(4,1)} %bitcast.34), calls=%async_computation | async-start | bytes 8388608
  57.1 30.0 %slice-start.1 = ((s8[9437184]{0:T(1024)(128)(4,1)}), s8[4194304]{0:T(1024)(128)(4,1)S(1)}, s32[]{:S(2)}) async-start(s8[9437184]{0:T(1024)(128)(4,1)} %bitcast.34), calls=%async_computation.1 | async-start | bytes 8388608
  69.0 18.1 %collective-permute-start.11 = (bf16[128,1536]{1,0:T(8,128)(2,1)S(1)}, bf16[128,1536]{1,0:T(8,128)(2,1)S(1)}, u32[]{:S(2)}, u32[]{:S(2)}) collective-permute-start(bf16[128,1536]{1,0:T(8,128)(2,1)S(1)} %shard_map.82.refs_0_), channel_id=1, source_target_pairs={{0,2},{1,3},{2,4},{3,5},{4,6},{5,7},{6,0},{7,1},{8,10},{9,11},{10,... | collective-permute-start | bytes 1179656 | tf_op jit(solution)/shard_map/ppermute | solution.py:31
  76.7 10.4 %collective-permute-start.18 = (bf16[128,1536]{1,0:T(8,128)(2,1)S(1)}, bf16[128,1536]{1,0:T(8,128)(2,1)S(1)}, u32[]{:S(2)}, u32[]{:S(2)}) collective-permute-start(bf16[128,1536]{1,0:T(8,128)(2,1)S(1)} %shard_map.84.refs_4_), channel_id=1, source_target_pairs={{0,8},{8,0},{16,24},{24,16},{32,40},{40,32},{48,56},{56,48},{64,72... | collective-permute-start | bytes 1179656 | tf_op jit(solution)/shard_map/ppermute | solution.py:404
  77.2 9.9 %collective-permute-start.19 = (bf16[128,1536]{1,0:T(8,128)(2,1)S(1)}, bf16[128,1536]{1,0:T(8,128)(2,1)S(1)}, u32[]{:S(2)}, u32[]{:S(2)}) collective-permute-start(bf16[128,1536]{1,0:T(8,128)(2,1)S(1)} %collective-permute-done.15.refs_5_), channel_id=1, source_target_pairs={{0,8},{8,0},{16,24},{24,16},{32,40},{40,32},{48,56},{56,48},{64,72... | collective-permute-start | bytes 1179656 | tf_op jit(solution)/shard_map/ppermute | solution.py:404
  77.2 9.9 %collective-permute-start.20 = (bf16[128,1536]{1,0:T(8,128)(2,1)S(1)}, bf16[128,1536]{1,0:T(8,128)(2,1)S(1)}, u32[]{:S(2)}, u32[]{:S(2)}) collective-permute-start(bf16[128,1536]{1,0:T(8,128)(2,1)S(1)} %collective-permute-done.16.refs_6_), channel_id=1, source_target_pairs={{0,8},{8,0},{16,24},{24,16},{32,40},{40,32},{48,56},{56,48},{64,72... | collective-permute-start | bytes 1179656 | tf_op jit(solution)/shard_map/ppermute | solution.py:404
  77.7 9.4 %collective-permute-start.21 = (bf16[128,1536]{1,0:T(8,128)(2,1)S(1)}, bf16[128,1536]{1,0:T(8,128)(2,1)S(1)}, u32[]{:S(2)}, u32[]{:S(2)}) collective-permute-start(bf16[128,1536]{1,0:T(8,128)(2,1)S(1)} %collective-permute-done.17.refs_7_), channel_id=1, source_target_pairs={{0,8},{8,0},{16,24},{24,16},{32,40},{40,32},{48,56},{56,48},{64,72... | collective-permute-start | bytes 1179656 | tf_op jit(solution)/shard_map/ppermute | solution.py:404
  77.8 9.3 %slice-start.2 = ((s8[9437184]{0:T(1024)(128)(4,1)}), s8[1048576]{0:T(1024)(128)(4,1)S(1)}, s32[]{:S(2)}) async-start(s8[9437184]{0:T(1024)(128)(4,1)} %bitcast.34), calls=%async_computation.2 | async-start | bytes 2097152
  77.8 9.4 %copy-start.4 = (s32[12,24]{1,0:T(8,128)S(1)}, s32[12,24]{1,0:T(8,128)}, u32[]{:S(2)}) copy-start(s32[12,24]{1,0:T(8,128)} %pattern_ref.1) | copy-start | bytes 3460

commit v5 on v4

--- a/solution.py
+++ b/solution.py
@@ -383,7 +383,6 @@
     pivot, digits = small_call(
         choose_core, [(slice_width, pivot_size), (8, pivot_size)], at, packet, packet_other
     )
-    pivot, moved = both((pivot, moved))
     pivot_other = lax.ppermute(pivot, "col", Z_LO)
     moved_other = lax.ppermute(moved, "row", Z_HI)
     (pivot,) = small_call(pair_z_lo, [(2 * slice_width, pivot_size)], at, pivot, pivot_other)

time: 96.4 us -> 91.4 us (0.948)
  the two profiles are of different devices: /device:TPU:25 before, /device:TPU:16 now
where the time goes in v5:
time: 91.4 us; the launch traced here: 91 us
  Pallas kernels  36 us (39%)
  starting transfers between devices  35.3 us (39%)
  waiting for transfers between devices  9.63 us (11%)
  local copies, waits for them, and re-layouts  6.8 us (7%)
  between operations  1.78 us (2%)
  other arithmetic  1.58 us (2%)
    ppermute x12, starting transfers between devices, ring(): return [mine] + [lax.ppermute(mine, axis, shifts[k]) for k in (1, 2, 3)]  17.3 us
    pallas_call x1, Pallas kernels, upper_inverse(): pl.pallas_call(kernel, out_shape=(jax.ShapeDtypeStruct((n // 2, n), F32),...  11.9 us
    pallas_call x1, Pallas kernels, update(): pl.pallas_call(update_kernel, out_shape=(jax.ShapeDtypeStruct((row_dev, c...  10.1 us
    pallas_call x1, Pallas kernels, lower_inverse(): pl.pallas_call(lower_kernel, out_shape=(jax.ShapeDtypeStruct((n, n), F32)...  9.26 us
    ppermute x1, starting transfers between devices, per_device(): moved_other = lax.ppermute(moved, 'row', Z_HI)  6.79 us
    ppermute x12, waiting for transfers between devices, ring(): return [mine] + [lax.ppermute(mine, axis, shifts[k]) for k in (1, 2, 3)]  6.17 us
    gather x4, local copies, waits for them, and re-layouts, regroup(): parts = jnp.take(arrived, slot, axis=1)  4.76 us
    ppermute x1, starting transfers between devices, per_device(): packet_other = lax.ppermute(packet, 'row', Z_HI)  3.96 us
  transfers between devices with their start and end apart: 22, of which 8 were waited for; matrix products, arithmetic and copies ran while one was open for 8% of the time, Pallas kernels for 27%

profile of v5, /device:TPU:16, one launch (start us, length us, event | category | flops | bytes accessed | tf_op | source)
XLA Modules:
  0.0 91.0 jit_solution(18074146305859928474)
XLA Ops:
  0.6 0.7 copy-done
  1.3 0.7 copy-done.1
  2.1 1.0 %shard_map.77.p0 = bf16[32,1536]{1,0:T(8,128)(2,1)S(1)} custom-call(bf16[64,1536]{1,0:T(8,128)(2,1)} %bitcast.2.panel_ref.p0, f32[3,1536]{1,0:T(4,128)S(1)} %copy-done.1, s32[12,128]{1,0:T(8,128)S(1)} %bitcast.29), custom_call_target="tpu_custom_call" | custom-call | tf_op jit(solution)/shard_map/pallas_call | solution.py:48
  3.0 2.8 %collective-permute-start.2 = (bf16[32,1536]{1,0:T(8,128)(2,1)S(1)}, bf16[32,1536]{1,0:T(8,128)(2,1)S(1)}, u32[]{:S(2)}, u32[]{:S(2)}) collective-permute-start(bf16[32,1536]{1,0:T(8,128)(2,1)S(1)} %shard_map.77.p0), channel_id=1, source_target_pairs={{0,96},{8,104},{16,112},{24,120},{32,0},{40,8},{48,16},{56,24},{64... | collective-permute-start | bytes 294920 | tf_op jit(solution)/shard_map/ppermute | solution.py:31
  5.9 0.8 collective-permute-start.1
  6.7 0.9 collective-permute-start
  7.5 3.5 %collective-permute-start.13 = (bf16[64,1536]{1,0:T(8,128)(2,1)}, bf16[64,1536]{1,0:T(8,128)(2,1)S(1)}, u32[]{:S(2)}, u32[]{:S(2)}) collective-permute-start(bf16[64,1536]{1,0:T(8,128)(2,1)} %bitcast.2.panel_ref.p0), channel_id=1, source_target_pairs={{0,0},{1,16},{2,32},{3,48},{4,64},{5,80},{6,96},{7,112},{8,8},{9,2... | collective-permute-start | bytes 589832 | tf_op jit(solution)/shard_map/ppermute | solution.py:376
  11.1 0.7 pad_add_fusion.at_ref
  11.8 0.9 %collective-permute-done.1.p2 = bf16[32,1536]{1,0:T(8,128)(2,1)S(1)} collective-permute-done((bf16[32,1536]{1,0:T(8,128)(2,1)S(1)}, bf16[32,1536]{1,0:T(8,128)(2,1)S(1)}, u32[]{:S(2)}, u32[]{:S(2)}) %collective-permute-start.1) | collective-permute-done | bytes 98336 | tf_op jit(solution)/shard_map/ppermute | solution.py:31
  12.7 1.0 %collective-permute-done.p1 = bf16[32,1536]{1,0:T(8,128)(2,1)S(1)} collective-permute-done((bf16[32,1536]{1,0:T(8,128)(2,1)S(1)}, bf16[32,1536]{1,0:T(8,128)(2,1)S(1)}, u32[]{:S(2)}, u32[]{:S(2)}) %collective-permute-start) | collective-permute-done | bytes 98336 | tf_op jit(solution)/shard_map/ppermute | solution.py:31
  14.3 4.0 %collective-permute-start.3 = (bf16[56,1536]{1,0:T(8,128)(2,1)S(1)}, bf16[56,1536]{1,0:T(8,128)(2,1)S(1)}, u32[]{:S(2)}, u32[]{:S(2)}) collective-permute-start(bf16[56,1536]{1,0:T(8,128)(2,1)S(1)} %shard_map.78.p0), channel_id=1, source_target_pairs={{0,16},{8,24},{16,0},{24,8},{32,48},{40,56},{48,32},{56,40},{64,80... | collective-permute-start | bytes 516104 | tf_op jit(solution)/shard_map/ppermute | solution.py:380
  18.3 1.0 %collective-permute-start.9 = (bf16[64,1536]{1,0:T(8,128)(2,1)}, bf16[64,1536]{1,0:T(8,128)(2,1)S(1)}, u32[]{:S(2)}, u32[]{:S(2)}) collective-permute-start(bf16[64,1536]{1,0:T(8,128)(2,1)} %bitcast.2.panel_ref.p0), channel_id=1, source_target_pairs={{0,1},{1,0},{2,3},{3,2},{4,5},{5,4},{6,7},{7,6},{8,9},{9,8},{10,11... | collective-permute-start | bytes 589832 | tf_op jit(solution)/shard_map/ppermute | solution.py:378
  19.3 1.1 %collective-permute-done.13.p0 = bf16[64,1536]{1,0:T(8,128)(2,1)S(1)} collective-permute-done((bf16[64,1536]{1,0:T(8,128)(2,1)}, bf16[64,1536]{1,0:T(8,128)(2,1)S(1)}, u32[]{:S(2)}, u32[]{:S(2)}) %collective-permute-start.13) | collective-permute-done | bytes 196640 | tf_op jit(solution)/shard_map/ppermute | solution.py:376
  20.4 6.8 %collective-permute-start.14 = (bf16[64,1536]{1,0:T(8,128)(2,1)S(1)}, bf16[64,1536]{1,0:T(8,128)(2,1)S(1)}, u32[]{:S(2)}, u32[]{:S(2)}) collective-permute-start(bf16[64,1536]{1,0:T(8,128)(2,1)S(1)} %collective-permute-done.13.p0), channel_id=1, source_target_pairs={{0,16},{8,24},{16,0},{24,8},{32,48},{40,56},{48,32},{56,40},{64,80... | collective-permute-start | bytes 589832 | tf_op jit(solution)/shard_map/ppermute | solution.py:387
  27.9 0.7 compare_and_fusion
  29.6 1.0 %shard_map.82.refs_0_ = bf16[128,1536]{1,0:T(8,128)(2,1)S(1)} custom-call(s32[3]{0:T(128)S(1)} %pad_add_fusion.at_ref, bf16[64,1536]{1,0:T(8,128)(2,1)} %bitcast.2.panel_ref.p0, bf16[64,1536]{1,0:T(8,128)(2,1)S(1)} %collective-permute-done.9.p1), custom_call_target="tpu_custom_call" | custom-call | tf_op jit(solution)/shard_map/pallas_call | solution.py:57
  30.6 2.0 %collective-permute-done.14.p1 = bf16[64,1536]{1,0:T(8,128)(2,1)S(1)} collective-permute-done((bf16[64,1536]{1,0:T(8,128)(2,1)S(1)}, bf16[64,1536]{1,0:T(8,128)(2,1)S(1)}, u32[]{:S(2)}, u32[]{:S(2)}) %collective-permute-start.14) | collective-permute-done | bytes 196640 | tf_op jit(solution)/shard_map/ppermute | solution.py:387
  33.3 0.7 collective-permute-start.16
  34.6 1.6 %collective-permute-start.5 = (bf16[64,512]{1,0:T(8,128)(2,1)S(1)}, bf16[64,512]{1,0:T(8,128)(2,1)S(1)}, u32[]{:S(2)}, u32[]{:S(2)}) collective-permute-start(bf16[64,512]{1,0:T(8,128)(2,1)S(1)} %get-tuple-element.23.p0), channel_id=1, source_target_pairs={{0,1},{1,0},{2,3},{3,2},{4,5},{5,4},{6,7},{7,6},{8,9},{9,8},{10,11... | collective-permute-start | bytes 196616 | tf_op jit(solution)/shard_map/ppermute | solution.py:386
  36.5 1.3 %gather_fusion.1 = bf16[512,8]{1,0:T(8,128)(2,1)S(1)} fusion(bf16[8,1536]{0,1:T(8,128)(2,1)S(1)} %bitcast.33, s32[1024]{0:T(1024)S(1)} %pad_clamp_fusion.1), kind=kCustom, calls=%fused_computation.1 | custom fusion | bytes 18432 | tf_op jit(solution)/shard_map/jit(_take)/gather | solution.py:109
  38.2 3.2 %gather_fusion = bf16[1536,8]{1,0:T(8,128)(2,1)S(1)} fusion(bf16[8,1536]{0,1:T(8,128)(2,1)S(1)} %bitcast.32, s32[2048]{0:T(1024)S(1)} %pad_clamp_fusion), kind=kCustom, calls=%fused_computation | custom fusion | bytes 55296 | tf_op jit(solution)/shard_map/jit(_take)/gather | solution.py:109
  42.1 2.9 %collective-permute-start.8 = (bf16[128,512]{1,0:T(8,128)(2,1)S(1)}, bf16[128,512]{1,0:T(8,128)(2,1)S(1)}, u32[]{:S(2)}, u32[]{:S(2)}) collective-permute-start(bf16[128,512]{1,0:T(8,128)(2,1)S(1)} %shard_map.81.p0), channel_id=1, source_target_pairs={{0,6},{1,7},{2,0},{3,1},{4,2},{5,3},{6,4},{7,5},{8,14},{9,15},{10,... | collective-permute-start | bytes 393224 | tf_op jit(solution)/shard_map/ppermute | solution.py:31
  45.1 2.7 %collective-permute-start.7 = (bf16[128,512]{1,0:T(8,128)(2,1)S(1)}, bf16[128,512]{1,0:T(8,128)(2,1)S(1)}, u32[]{:S(2)}, u32[]{:S(2)}) collective-permute-start(bf16[128,512]{1,0:T(8,128)(2,1)S(1)} %shard_map.81.p0), channel_id=1, source_target_pairs={{0,4},{1,5},{2,6},{3,7},{4,0},{5,1},{6,2},{7,3},{8,12},{9,13},{10,... | collective-permute-start | bytes 393224 | tf_op jit(solution)/shard_map/ppermute | solution.py:31
  47.8 0.9 collective-permute-done.8.p3
  48.7 0.9 %collective-permute-start.15 = (bf16[128,1536]{1,0:T(8,128)(2,1)S(1)}, bf16[128,1536]{1,0:T(8,128)(2,1)S(1)}, u32[]{:S(2)}, u32[]{:S(2)}) collective-permute-start(bf16[128,1536]{1,0:T(8,128)(2,1)S(1)} %shard_map.84.refs_4_), channel_id=1, source_target_pairs={{0,32},{8,40},{16,48},{24,56},{32,64},{40,72},{48,80},{56,88},{64,... | collective-permute-start | bytes 1179656 | tf_op jit(solution)/shard_map/ppermute | solution.py:31
  49.6 2.0 %collective-permute-done.7.p2 = bf16[128,512]{1,0:T(8,128)(2,1)S(1)} collective-permute-done((bf16[128,512]{1,0:T(8,128)(2,1)S(1)}, bf16[128,512]{1,0:T(8,128)(2,1)S(1)}, u32[]{:S(2)}, u32[]{:S(2)}) %collective-permute-start.7) | collective-permute-done | bytes 131104 | tf_op jit(solution)/shard_map/ppermute | solution.py:31
  51.6 1.4 %collective-permute-done.6.p1 = bf16[128,512]{1,0:T(8,128)(2,1)S(1)} collective-permute-done((bf16[128,512]{1,0:T(8,128)(2,1)S(1)}, bf16[128,512]{1,0:T(8,128)(2,1)S(1)}, u32[]{:S(2)}, u32[]{:S(2)}) %collective-permute-start.6) | collective-permute-done | bytes 131104 | tf_op jit(solution)/shard_map/ppermute | solution.py:31
  53.5 2.7 %collective-permute-start.11 = (bf16[128,1536]{1,0:T(8,128)(2,1)S(1)}, bf16[128,1536]{1,0:T(8,128)(2,1)S(1)}, u32[]{:S(2)}, u32[]{:S(2)}) collective-permute-start(bf16[128,1536]{1,0:T(8,128)(2,1)S(1)} %shard_map.82.refs_0_), channel_id=1, source_target_pairs={{0,4},{1,5},{2,6},{3,7},{4,0},{5,1},{6,2},{7,3},{8,12},{9,13},{10,... | collective-permute-start | bytes 1179656 | tf_op jit(solution)/shard_map/ppermute | solution.py:31
  56.2 11.9 %shard_map.83 = (f32[256,512]{1,0:T(8,128)S(1)}, bf16[256,512]{1,0:T(8,128)(2,1)S(1)}, f32[256,512]{1,0:T(8,128)S(1)}) custom-call(s32[3]{0:T(128)S(1)} %pad_add_fusion.at_ref, bf16[128,512]{1,0:T(8,128)(2,1)S(1)} %shard_map.81.p0, bf16[128,512]{1,0:T(8,128)(2,1)S(1)} %collective-permute-done.6.p1, bf16[128,512]{1,0:T(8,128)(2,1)S(1)} %collective-permute-done.7.p2, ...), custom_call_target="tpu_custom_call" | custom-call | flops 10737418240 | bytes 1048576 | tf_op jit(solution)/shard_map/pallas_call | solution.py:216
  68.1 2.3 %collective-permute-start.10 = (bf16[128,1536]{1,0:T(8,128)(2,1)S(1)}, bf16[128,1536]{1,0:T(8,128)(2,1)S(1)}, u32[]{:S(2)}, u32[]{:S(2)}) collective-permute-start(bf16[128,1536]{1,0:T(8,128)(2,1)S(1)} %shard_map.82.refs_0_), channel_id=1, source_target_pairs={{0,2},{1,3},{2,4},{3,5},{4,6},{5,7},{6,0},{7,1},{8,10},{9,11},{10,... | collective-permute-start | bytes 1179656 | tf_op jit(solution)/shard_map/ppermute | solution.py:31
  71.4 9.3 %shard_map.85 = (f32[512,512]{1,0:T(8,128)S(1)}, bf16[512,512]{1,0:T(8,128)(2,1)S(1)}) custom-call(f32[256,512]{1,0:T(8,128)S(1)} %get-tuple-element.35.in_ref, f32[256,512]{1,0:T(8,128)S(1)} %get-tuple-element.36.w_top, bf16[256,512]{1,0:T(8,128)(2,1)S(1)} %get-tuple-element.37.half_top), custom_call_target="tpu_custom_call" | custom-call | flops 10737418240 | bytes 1048576 | tf_op jit(solution)/shard_map/pallas_call | solution.py:234
  80.8 10.1 %shard_map.86 = (bf16[1536,3072]{1,0:T(8,128)(2,1)}, f32[3,1536]{1,0:T(4,128)}) custom-call(s32[3]{0:T(128)S(1)} %pad_add_fusion.at_ref, s32[12,24]{1,0:T(8,128)S(1)} %copy-done.2, bf16[128,1536]{1,0:T(8,128)(2,1)S(1)} %shard_map.82.refs_0_, bf16[128,1536]{1,0:T(8,128)(2,1)S(1)} %collective-permute-done.10.refs_1_, ...), custom_call_target="tpu_custom_call" | custom-call | flops 8589934592 | bytes 25165824 | tf_op jit(solution)/shard_map/pallas_call | solution.py:343
  (57 shorter events, 5.9 us)
Async XLA Ops:
  0.6 0.7 copy-start
  1.3 0.7 copy-start.1
  3.0 8.8 %collective-permute-start.2 = (bf16[32,1536]{1,0:T(8,128)(2,1)S(1)}, bf16[32,1536]{1,0:T(8,128)(2,1)S(1)}, u32[]{:S(2)}, u32[]{:S(2)}) collective-permute-start(bf16[32,1536]{1,0:T(8,128)(2,1)S(1)} %shard_map.77.p0), channel_id=1, source_target_pairs={{0,96},{8,104},{16,112},{24,120},{32,0},{40,8},{48,16},{56,24},{64... | collective-permute-start | bytes 294920 | tf_op jit(solution)/shard_map/ppermute | solution.py:31
  5.9 6.9 %collective-permute-start.1 = (bf16[32,1536]{1,0:T(8,128)(2,1)S(1)}, bf16[32,1536]{1,0:T(8,128)(2,1)S(1)}, u32[]{:S(2)}, u32[]{:S(2)}) collective-permute-start(bf16[32,1536]{1,0:T(8,128)(2,1)S(1)} %shard_map.77.p0), channel_id=1, source_target_pairs={{0,64},{8,72},{16,80},{24,88},{32,96},{40,104},{48,112},{56,120},{... | collective-permute-start | bytes 294920 | tf_op jit(solution)/shard_map/ppermute | solution.py:31
  6.7 7.1 %collective-permute-start = (bf16[32,1536]{1,0:T(8,128)(2,1)S(1)}, bf16[32,1536]{1,0:T(8,128)(2,1)S(1)}, u32[]{:S(2)}, u32[]{:S(2)}) collective-permute-start(bf16[32,1536]{1,0:T(8,128)(2,1)S(1)} %shard_map.77.p0), channel_id=1, source_target_pairs={{0,32},{8,40},{16,48},{24,56},{32,64},{40,72},{48,80},{56,88},{64,... | collective-permute-start | bytes 294920 | tf_op jit(solution)/shard_map/ppermute | solution.py:31
  7.5 12.9 %collective-permute-start.13 = (bf16[64,1536]{1,0:T(8,128)(2,1)}, bf16[64,1536]{1,0:T(8,128)(2,1)S(1)}, u32[]{:S(2)}, u32[]{:S(2)}) collective-permute-start(bf16[64,1536]{1,0:T(8,128)(2,1)} %bitcast.2.panel_ref.p0), channel_id=1, source_target_pairs={{0,0},{1,16},{2,32},{3,48},{4,64},{5,80},{6,96},{7,112},{8,8},{9,2... | collective-permute-start | bytes 589832 | tf_op jit(solution)/shard_map/ppermute | solution.py:376
  14.3 12.9 %collective-permute-start.3 = (bf16[56,1536]{1,0:T(8,128)(2,1)S(1)}, bf16[56,1536]{1,0:T(8,128)(2,1)S(1)}, u32[]{:S(2)}, u32[]{:S(2)}) collective-permute-start(bf16[56,1536]{1,0:T(8,128)(2,1)S(1)} %shard_map.78.p0), channel_id=1, source_target_pairs={{0,16},{8,24},{16,0},{24,8},{32,48},{40,56},{48,32},{56,40},{64,80... | collective-permute-start | bytes 516104 | tf_op jit(solution)/shard_map/ppermute | solution.py:380
  18.3 11.4 %collective-permute-start.9 = (bf16[64,1536]{1,0:T(8,128)(2,1)}, bf16[64,1536]{1,0:T(8,128)(2,1)S(1)}, u32[]{:S(2)}, u32[]{:S(2)}) collective-permute-start(bf16[64,1536]{1,0:T(8,128)(2,1)} %bitcast.2.panel_ref.p0), channel_id=1, source_target_pairs={{0,1},{1,0},{2,3},{3,2},{4,5},{5,4},{6,7},{7,6},{8,9},{9,8},{10,11... | collective-permute-start | bytes 589832 | tf_op jit(solution)/shard_map/ppermute | solution.py:378
  20.4 12.1 %collective-permute-start.14 = (bf16[64,1536]{1,0:T(8,128)(2,1)S(1)}, bf16[64,1536]{1,0:T(8,128)(2,1)S(1)}, u32[]{:S(2)}, u32[]{:S(2)}) collective-permute-start(bf16[64,1536]{1,0:T(8,128)(2,1)S(1)} %collective-permute-done.13.p0), channel_id=1, source_target_pairs={{0,16},{8,24},{16,0},{24,8},{32,48},{40,56},{48,32},{56,40},{64,80... | collective-permute-start | bytes 589832 | tf_op jit(solution)/shard_map/ppermute | solution.py:387
  27.8 6.1 %collective-permute-start.4 = (bf16[88,1536]{1,0:T(8,128)(2,1)S(1)}, bf16[88,1536]{1,0:T(8,128)(2,1)S(1)}, u32[]{:S(2)}, u32[]{:S(2)}) collective-permute-start(bf16[88,1536]{1,0:T(8,128)(2,1)S(1)} %shard_map.79.p0), channel_id=1, source_target_pairs={{0,8},{8,0},{16,24},{24,16},{32,40},{40,32},{48,56},{56,48},{64,72... | collective-permute-start | bytes 811016 | tf_op jit(solution)/shard_map/ppermute | solution.py:382
  33.2 34.9 %collective-permute-start.17 = (bf16[128,1536]{1,0:T(8,128)(2,1)S(1)}, bf16[128,1536]{1,0:T(8,128)(2,1)S(1)}, u32[]{:S(2)}, u32[]{:S(2)}) collective-permute-start(bf16[128,1536]{1,0:T(8,128)(2,1)S(1)} %shard_map.84.refs_4_), channel_id=1, source_target_pairs={{0,96},{8,104},{16,112},{24,120},{32,0},{40,8},{48,16},{56,24},{64... | collective-permute-start | bytes 1179656 | tf_op jit(solution)/shard_map/ppermute | solution.py:31
  33.3 37.2 %collective-permute-start.16 = (bf16[128,1536]{1,0:T(8,128)(2,1)S(1)}, bf16[128,1536]{1,0:T(8,128)(2,1)S(1)}, u32[]{:S(2)}, u32[]{:S(2)}) collective-permute-start(bf16[128,1536]{1,0:T(8,128)(2,1)S(1)} %shard_map.84.refs_4_), channel_id=1, source_target_pairs={{0,64},{8,72},{16,80},{24,88},{32,96},{40,104},{48,112},{56,120},{... | collective-permute-start | bytes 1179656 | tf_op jit(solution)/shard_map/ppermute | solution.py:31
  34.6 7.0 %collective-permute-start.5 = (bf16[64,512]{1,0:T(8,128)(2,1)S(1)}, bf16[64,512]{1,0:T(8,128)(2,1)S(1)}, u32[]{:S(2)}, u32[]{:S(2)}) collective-permute-start(bf16[64,512]{1,0:T(8,128)(2,1)S(1)} %get-tuple-element.23.p0), channel_id=1, source_target_pairs={{0,1},{1,0},{2,3},{3,2},{4,5},{5,4},{6,7},{7,6},{8,9},{9,8},{10,11... | collective-permute-start | bytes 196616 | tf_op jit(solution)/shard_map/ppermute | solution.py:386
  42.1 6.5 %collective-permute-start.8 = (bf16[128,512]{1,0:T(8,128)(2,1)S(1)}, bf16[128,512]{1,0:T(8,128)(2,1)S(1)}, u32[]{:S(2)}, u32[]{:S(2)}) collective-permute-start(bf16[128,512]{1,0:T(8,128)(2,1)S(1)} %shard_map.81.p0), channel_id=1, source_target_pairs={{0,6},{1,7},{2,0},{3,1},{4,2},{5,3},{6,4},{7,5},{8,14},{9,15},{10,... | collective-permute-start | bytes 393224 | tf_op jit(solution)/shard_map/ppermute | solution.py:31
  45.1 6.5 %collective-permute-start.7 = (bf16[128,512]{1,0:T(8,128)(2,1)S(1)}, bf16[128,512]{1,0:T(8,128)(2,1)S(1)}, u32[]{:S(2)}, u32[]{:S(2)}) collective-permute-start(bf16[128,512]{1,0:T(8,128)(2,1)S(1)} %shard_map.81.p0), channel_id=1, source_target_pairs={{0,4},{1,5},{2,6},{3,7},{4,0},{5,1},{6,2},{7,3},{8,12},{9,13},{10,... | collective-permute-start | bytes 393224 | tf_op jit(solution)/shard_map/ppermute | solution.py:31
  47.7 5.2 %collective-permute-start.6 = (bf16[128,512]{1,0:T(8,128)(2,1)S(1)}, bf16[128,512]{1,0:T(8,128)(2,1)S(1)}, u32[]{:S(2)}, u32[]{:S(2)}) collective-permute-start(bf16[128,512]{1,0:T(8,128)(2,1)S(1)} %shard_map.81.p0), channel_id=1, source_target_pairs={{0,2},{1,3},{2,4},{3,5},{4,6},{5,7},{6,0},{7,1},{8,10},{9,11},{10,... | collective-permute-start | bytes 393224 | tf_op jit(solution)/shard_map/ppermute | solution.py:31
  48.7 21.7 %collective-permute-start.15 = (bf16[128,1536]{1,0:T(8,128)(2,1)S(1)}, bf16[128,1536]{1,0:T(8,128)(2,1)S(1)}, u32[]{:S(2)}, u32[]{:S(2)}) collective-permute-start(bf16[128,1536]{1,0:T(8,128)(2,1)S(1)} %shard_map.84.refs_4_), channel_id=1, source_target_pairs={{0,32},{8,40},{16,48},{24,56},{32,64},{40,72},{48,80},{56,88},{64,... | collective-permute-start | bytes 1179656 | tf_op jit(solution)/shard_map/ppermute | solution.py:31
  53.0 18.0 %collective-permute-start.12 = (bf16[128,1536]{1,0:T(8,128)(2,1)S(1)}, bf16[128,1536]{1,0:T(8,128)(2,1)S(1)}, u32[]{:S(2)}, u32[]{:S(2)}) collective-permute-start(bf16[128,1536]{1,0:T(8,128)(2,1)S(1)} %shard_map.82.refs_0_), channel_id=1, source_target_pairs={{0,6},{1,7},{2,0},{3,1},{4,2},{5,3},{6,4},{7,5},{8,14},{9,15},{10,... | collective-permute-start | bytes 1179656 | tf_op jit(solution)/shard_map/ppermute | solution.py:31
  53.5 17.5 %collective-permute-start.11 = (bf16[128,1536]{1,0:T(8,128)(2,1)S(1)}, bf16[128,1536]{1,0:T(8,128)(2,1)S(1)}, u32[]{:S(2)}, u32[]{:S(2)}) collective-permute-start(bf16[128,1536]{1,0:T(8,128)(2,1)S(1)} %shard_map.82.refs_0_), channel_id=1, source_target_pairs={{0,4},{1,5},{2,6},{3,7},{4,0},{5,1},{6,2},{7,3},{8,12},{9,13},{10,... | collective-permute-start | bytes 1179656 | tf_op jit(solution)/shard_map/ppermute | solution.py:31
  56.2 24.6 %slice-start = ((s8[9437184]{0:T(1024)(128)(4,1)}), s8[4194304]{0:T(1024)(128)(4,1)S(1)}, s32[]{:S(2)}) async-start(s8[9437184]{0:T(1024)(128)(4,1)} %bitcast.30), calls=%async_computation | async-start | bytes 8388608
  56.2 24.6 %slice-start.1 = ((s8[9437184]{0:T(1024)(128)(4,1)}), s8[4194304]{0:T(1024)(128)(4,1)S(1)}, s32[]{:S(2)}) async-start(s8[9437184]{0:T(1024)(128)(4,1)} %bitcast.30), calls=%async_computation.1 | async-start | bytes 8388608
  68.1 12.6 %collective-permute-start.10 = (bf16[128,1536]{1,0:T(8,128)(2,1)S(1)}, bf16[128,1536]{1,0:T(8,128)(2,1)S(1)}, u32[]{:S(2)}, u32[]{:S(2)}) collective-permute-start(bf16[128,1536]{1,0:T(8,128)(2,1)S(1)} %shard_map.82.refs_0_), channel_id=1, source_target_pairs={{0,2},{1,3},{2,4},{3,5},{4,6},{5,7},{6,0},{7,1},{8,10},{9,11},{10,... | collective-permute-start | bytes 1179656 | tf_op jit(solution)/shard_map/ppermute | solution.py:31
  70.4 10.3 %collective-permute-start.18 = (bf16[128,1536]{1,0:T(8,128)(2,1)S(1)}, bf16[128,1536]{1,0:T(8,128)(2,1)S(1)}, u32[]{:S(2)}, u32[]{:S(2)}) collective-permute-start(bf16[128,1536]{1,0:T(8,128)(2,1)S(1)} %shard_map.84.refs_4_), channel_id=1, source_target_pairs={{0,8},{8,0},{16,24},{24,16},{32,40},{40,32},{48,56},{56,48},{64,72... | collective-permute-start | bytes 1179656 | tf_op jit(solution)/shard_map/ppermute | solution.py:403
  70.4 10.3 %collective-permute-start.19 = (bf16[128,1536]{1,0:T(8,128)(2,1)S(1)}, bf16[128,1536]{1,0:T(8,128)(2,1)S(1)}, u32[]{:S(2)}, u32[]{:S(2)}) collective-permute-start(bf16[128,1536]{1,0:T(8,128)(2,1)S(1)} %collective-permute-done.15.refs_5_), channel_id=1, source_target_pairs={{0,8},{8,0},{16,24},{24,16},{32,40},{40,32},{48,56},{56,48},{64,72... | collective-permute-start | bytes 1179656 | tf_op jit(solution)/shard_map/ppermute | solution.py:403
  70.9 9.8 %collective-permute-start.20 = (bf16[128,1536]{1,0:T(8,128)(2,1)S(1)}, bf16[128,1536]{1,0:T(8,128)(2,1)S(1)}, u32[]{:S(2)}, u32[]{:S(2)}) collective-permute-start(bf16[128,1536]{1,0:T(8,128)(2,1)S(1)} %collective-permute-done.16.refs_6_), channel_id=1, source_target_pairs={{0,8},{8,0},{16,24},{24,16},{32,40},{40,32},{48,56},{56,48},{64,72... | collective-permute-start | bytes 1179656 | tf_op jit(solution)/shard_map/ppermute | solution.py:403
  71.0 9.7 %collective-permute-start.21 = (bf16[128,1536]{1,0:T(8,128)(2,1)S(1)}, bf16[128,1536]{1,0:T(8,128)(2,1)S(1)}, u32[]{:S(2)}, u32[]{:S(2)}) collective-permute-start(bf16[128,1536]{1,0:T(8,128)(2,1)S(1)} %collective-permute-done.17.refs_7_), channel_id=1, source_target_pairs={{0,8},{8,0},{16,24},{24,16},{32,40},{40,32},{48,56},{56,48},{64,72... | collective-permute-start | bytes 1179656 | tf_op jit(solution)/shard_map/ppermute | solution.py:403
  71.4 9.3 %slice-start.2 = ((s8[9437184]{0:T(1024)(128)(4,1)}), s8[1048576]{0:T(1024)(128)(4,1)S(1)}, s32[]{:S(2)}) async-start(s8[9437184]{0:T(1024)(128)(4,1)} %bitcast.30), calls=%async_computation.2 | async-start | bytes 2097152
  71.4 9.4 %copy-start.2 = (s32[12,24]{1,0:T(8,128)S(1)}, s32[12,24]{1,0:T(8,128)}, u32[]{:S(2)}) copy-start(s32[12,24]{1,0:T(8,128)} %pattern_ref.1) | copy-start | bytes 3460
